TPU v7x, 32 devices: a whole 2x2x4 slice. The times are simulated.
32 devices in a mesh: seq: 8 (over z, x), grp: 4 (over y, core).
Axes of the slice: x: 2, y: 2, z: 4, core: 2. Of those that a mesh axis runs over, the one named last changes fastest.
Arguments:
- tokens: float32 [16384, 768], P(('seq', 'grp')), may hold values from -6 to 6
- coordinates: int32 [16384, 2], P(('seq', 'grp')), may hold values from 0 to 1023
- lengths: int32 [5], replicated, may hold values from 1 to 16128, 16384 in all
- valid: int32 [16384], P(('seq', 'grp')), may hold values 0 or 1
- first_gain: float32 [768], replicated, may hold values from 0.5 to 1.5
- first_shift: float32 [768], replicated, may hold values from -3 to 3
- query_weight: bfloat16 [768, 768], P('seq', 'grp'), may hold values from -0.21875 to 0.21875
- query_bias: float32 [768], replicated, may hold values from -3 to 3
- key_weight: bfloat16 [768, 768], P('seq', 'grp'), may hold values from -0.21875 to 0.21875
- value_weight: bfloat16 [768, 768], P('seq', 'grp'), may hold values from -0.21875 to 0.21875
- value_bias: float32 [768], replicated, may hold values from -3 to 3
- output_weight: bfloat16 [768, 768], P('seq', 'grp'), may hold values from -3.5 to 3.5
- output_bias: float32 [768], replicated, may hold values from -3 to 3
- second_gain: float32 [768], replicated, may hold values from 0.5 to 1.5
- second_shift: float32 [768], replicated, may hold values from -3 to 3
- inner_weight: bfloat16 [768, 3072], P('seq', 'grp'), may hold values from -0.21875 to 0.21875
- inner_bias: float32 [3072], replicated, may hold values from -3 to 3
- outer_weight: bfloat16 [3072, 768], P('seq', 'grp'), may hold values from -0.109375 to 0.109375
- outer_bias: float32 [768], replicated, may hold values from -3 to 3
- cotangent: float32 [16384, 768], P(('seq', 'grp')), may hold values from -6 to 6
Outputs:
- output: float32 [16384, 768], P(('seq', 'grp'))
- token_grad: float32 [16384, 768], P(('seq', 'grp'))
- first_gain_grad: float32 [768], replicated
- first_shift_grad: float32 [768], replicated
- query_weight_grad: float32 [768, 768], P('seq', 'grp')
- query_bias_grad: float32 [768], replicated
- key_weight_grad: float32 [768, 768], P('seq', 'grp')
- value_weight_grad: float32 [768, 768], P('seq', 'grp')
- value_bias_grad: float32 [768], replicated
- output_weight_grad: float32 [768, 768], P('seq', 'grp')
- output_bias_grad: float32 [768], replicated
- second_gain_grad: float32 [768], replicated
- second_shift_grad: float32 [768], replicated
- inner_weight_grad: float32 [768, 3072], P('seq', 'grp')
- inner_bias_grad: float32 [3072], replicated
- outer_weight_grad: float32 [3072, 768], P('seq', 'grp')
- outer_bias_grad: float32 [768], replicated
Inputs may be any that keep to these rules, and one draw needn't show every extreme that they name: Every slide has at least one row; the lengths add up to 16384.
All inputs are finite; a program needn't handle non-finite values. No bound on the sum of `valid` on one device may be relied on, other than what follows from the above.
Results may differ from a plain program's by a relative error of at most 0.013.
Values may be sent and summed in bfloat16 or wider, within the bound.
A program may use at most 320 MiB of HBM per device.

v0:
```python
import math

import jax
import jax.numpy as jnp
from jax import lax
from jax.sharding import PartitionSpec as P

HEADS = 16
SUBLEN = 1024


ratios = (1, 2, 4, 8, 16)
big_negative = -1e30
epsilon = 1e-05


def as_sent(x):
    return jax.tree.map(lambda a: a.astype(jnp.bfloat16) if a.dtype == jnp.float32 else a, x)


def swapped(value, axis, apart):
    mask = 2**apart
    pairs = [(source, source ^ mask) for source in range(lax.axis_size(axis))]
    return lax.ppermute(value, axis, pairs)


def position_table(coordinates, width):
    quarter = width // 4
    frequency = jnp.exp(jnp.arange(quarter, dtype=jnp.float32) * (-math.log(10000.0) / quarter))
    column = coordinates[:, 0:1].astype(jnp.float32) * frequency[None, :]
    across = coordinates[:, 1:2].astype(jnp.float32) * frequency[None, :]
    return jnp.concatenate(
        [jnp.sin(column), jnp.cos(column), jnp.sin(across), jnp.cos(across)], axis=1
    )


def slide_of(positions, lengths):
    ends = jnp.cumsum(lengths)
    return jnp.sum((positions[..., None] >= ends).astype(jnp.int32), axis=-1)


def layer_norm(values, norm_gain, norm_shift):
    average = jnp.mean(values, axis=-1, keepdims=True)
    centred = values - average
    variance = jnp.mean(centred * centred, axis=-1, keepdims=True)
    return centred * lax.rsqrt(variance + epsilon) * norm_gain + norm_shift


def gelu_slope(values):
    return (
        0.5 * (1.0 + lax.erf(values * 0.7071067811865476))
        + values * jnp.exp(-0.5 * values * values) * 0.3989422804014327
    )


def product(left, right):
    return jnp.dot(left, right, preferred_element_type=jnp.float32)


def product_left(left, right):
    return jnp.einsum("rd,rf->df", left, right, preferred_element_type=jnp.float32)


def product_right(left, right):
    return jnp.einsum("rf,df->rd", left, right, preferred_element_type=jnp.float32)


def select_rows(tensor, ratio):
    count = tensor.shape[0] // ratio
    heads = tensor.shape[1]
    feature = tensor.shape[2]
    shaped = tensor.reshape(count, ratio, heads // ratio, ratio, feature)
    picked = jnp.diagonal(shaped, axis1=1, axis2=3)
    return jnp.swapaxes(picked, 2, 3).reshape(count, heads, feature)


def spread_rows(tensor, ratio, filler):
    count = tensor.shape[0]
    heads = tensor.shape[1]
    feature = tensor.shape[2]
    shaped = tensor.reshape(count, 1, heads // ratio, ratio, feature)
    match = jnp.arange(ratio)[:, None] == jnp.arange(ratio)[None, :]
    full = jnp.where(match[None, :, None, :, None], shaped, filler)
    return full.reshape(count * ratio, heads, feature)


def split_heads(array, blocks):
    return array.reshape((blocks, array.shape[0] // blocks) + array.shape[1:])


def join_heads(array):
    return array.reshape((array.shape[0] * array.shape[1],) + array.shape[2:])


def run_blocks(function, arrays, blocks):
    outputs = lax.map(function, tuple((split_heads(array, blocks) for array in arrays)))
    return tuple((join_heads(item) for item in outputs))


def branch_prepare(query, key, value, valid, start, ratio, lengths):
    rows = query.shape[0]
    heads = query.shape[1]
    count = rows // ratio
    query_picked = jnp.swapaxes(select_rows(query, ratio), 0, 1)
    key_picked = jnp.swapaxes(select_rows(key, ratio), 0, 1)
    value_picked = jnp.swapaxes(select_rows(value, ratio), 0, 1)
    keep_picked = jnp.tile(valid.reshape(count, ratio), (1, heads // ratio)).T.astype(jnp.bfloat16)
    classes = jnp.arange(heads, dtype=jnp.int32) % ratio
    segment_rows = ratio * SUBLEN
    segment_start = start // segment_rows * segment_rows
    query_place = start + jnp.arange(count, dtype=jnp.int32)[None, :] * ratio + classes[:, None]
    key_place = (
        segment_start + jnp.arange(SUBLEN, dtype=jnp.int32)[None, :] * ratio + classes[:, None]
    )
    query_slide = slide_of(query_place, lengths)
    key_slide = slide_of(key_place, lengths)
    return (
        query_picked,
        key_picked,
        value_picked,
        keep_picked,
        query_place,
        key_place,
        query_slide,
        key_slide,
    )


def segment_gather(keys, values, keeps, linear, bits):
    for bit in range(bits):
        got_keys, got_values, got_keeps = (
            swapped(as_sent(keys), ("seq", "grp"), bit).astype(keys.dtype),
            swapped(as_sent(values), ("seq", "grp"), bit).astype(values.dtype),
            swapped(keeps, ("seq", "grp"), bit),
        )
        upper = linear // (1 << bit) % 2 == 1
        keys = jnp.where(
            upper,
            jnp.concatenate([got_keys, keys], axis=1),
            jnp.concatenate([keys, got_keys], axis=1),
        )
        values = jnp.where(
            upper,
            jnp.concatenate([got_values, values], axis=1),
            jnp.concatenate([values, got_values], axis=1),
        )
        keeps = jnp.where(
            upper,
            jnp.concatenate([got_keeps, keeps], axis=1),
            jnp.concatenate([keeps, got_keeps], axis=1),
        )
    return (keys, values, keeps)


def segment_gather_again(keys, values, keeps, linear, bits):
    for bit in range(bits):
        got_keys, got_values, got_keeps = (
            swapped(as_sent(keys), ("seq", "grp"), bit).astype(keys.dtype),
            swapped(as_sent(values), ("seq", "grp"), bit).astype(values.dtype),
            swapped(keeps, ("seq", "grp"), bit),
        )
        upper = linear // (1 << bit) % 2 == 1
        keys = jnp.where(
            upper,
            jnp.concatenate([got_keys, keys], axis=1),
            jnp.concatenate([keys, got_keys], axis=1),
        )
        values = jnp.where(
            upper,
            jnp.concatenate([got_values, values], axis=1),
            jnp.concatenate([values, got_values], axis=1),
        )
        keeps = jnp.where(
            upper,
            jnp.concatenate([got_keeps, keeps], axis=1),
            jnp.concatenate([keeps, got_keeps], axis=1),
        )
    return (keys, values, keeps)


def segment_reduce(grad_key, grad_value, linear, bits):
    for bit in reversed(range(bits)):
        half = grad_key.shape[1] // 2
        upper = linear // (1 << bit) % 2 == 1
        send_key = jnp.where(upper, grad_key[:, :half], grad_key[:, half:])
        stay_key = jnp.where(upper, grad_key[:, half:], grad_key[:, :half])
        send_value = jnp.where(upper, grad_value[:, :half], grad_value[:, half:])
        stay_value = jnp.where(upper, grad_value[:, half:], grad_value[:, :half])
        got_key, got_value = swapped((send_key, send_value), ("seq", "grp"), bit)
        grad_key = stay_key + got_key
        grad_value = stay_value + got_value
    return (grad_key, grad_value)


def block_scores(query_block, key_block, key_keep, query_place, key_place, query_slide, key_slide):
    same = query_slide[:, :, None] == key_slide[:, None, :]
    own = query_place[:, :, None] == key_place[:, None, :]
    allowed = same & ((key_keep[:, None, :] > 0.5) | own)
    scores = jnp.einsum(
        "hix,hjx->hij", query_block, key_block, preferred_element_type=jnp.float32
    ) * query_block.shape[-1] ** (-0.5)
    return jnp.where(allowed, scores, big_negative)


def block_forward(parts):
    (
        query_block,
        key_block,
        value_block,
        key_keep,
        query_place,
        key_place,
        query_slide,
        key_slide,
    ) = parts
    masked = block_scores(
        query_block, key_block, key_keep, query_place, key_place, query_slide, key_slide
    )
    top = jnp.max(masked, axis=2, keepdims=True)
    total = top[:, :, 0] + jnp.log(jnp.sum(jnp.exp(masked - top), axis=2))
    prob = jnp.exp(masked - total[:, :, None]).astype(jnp.bfloat16)
    result = jnp.einsum("hij,hjx->hix", prob, value_block, preferred_element_type=jnp.float32)
    return (result, total)


def block_backward(parts):
    (
        query_block,
        key_block,
        value_block,
        key_keep,
        query_place,
        key_place,
        query_slide,
        key_slide,
        total,
        grad_low,
        grad_total,
    ) = parts
    masked = block_scores(
        query_block, key_block, key_keep, query_place, key_place, query_slide, key_slide
    )
    prob = jnp.exp(masked - total[:, :, None])
    grad_value = jnp.einsum(
        "hij,hix->hjx", prob.astype(jnp.bfloat16), grad_low, preferred_element_type=jnp.float32
    )
    grad_prob = jnp.einsum(
        "hix,hjx->hij", grad_low, value_block, preferred_element_type=jnp.float32
    )
    row_dot = jnp.sum(prob * grad_prob, axis=2, keepdims=True)
    grad_scores = (prob * (grad_prob - row_dot + grad_total[:, :, None])).astype(jnp.bfloat16)
    factor = query_block.shape[-1] ** (-0.5)
    grad_query = (
        jnp.einsum("hij,hjx->hix", grad_scores, key_block, preferred_element_type=jnp.float32)
        * factor
    )
    grad_key = (
        jnp.einsum("hij,hix->hjx", grad_scores, query_block, preferred_element_type=jnp.float32)
        * factor
    )
    return (grad_query, grad_key, grad_value)


def body(
    tokens,
    coordinates,
    lengths,
    valid,
    first_gain,
    first_shift,
    query_weight,
    query_bias,
    key_weight,
    value_weight,
    value_bias,
    output_weight,
    output_bias,
    second_gain,
    second_shift,
    inner_weight,
    inner_bias,
    outer_weight,
    outer_bias,
    cotangent,
):
    rows, width = tokens.shape
    head_size = width // HEADS
    linear = lax.axis_index("seq") * lax.axis_size("grp") + lax.axis_index("grp")
    start = linear * rows
    part_query, part_key, part_value, part_output, part_inner, part_outer = (
        lax.all_gather(query_weight, "grp", axis=1, tiled=True),
        lax.all_gather(key_weight, "grp", axis=1, tiled=True),
        lax.all_gather(value_weight, "grp", axis=1, tiled=True),
        lax.all_gather(output_weight, "grp", axis=1, tiled=True),
        lax.all_gather(inner_weight, "grp", axis=1, tiled=True),
        lax.all_gather(outer_weight, "grp", axis=1, tiled=True),
    )
    full_query, full_key, full_value, full_output, full_inner, full_outer = (
        lax.all_gather(part_query, "seq", axis=0, tiled=True),
        lax.all_gather(part_key, "seq", axis=0, tiled=True),
        lax.all_gather(part_value, "seq", axis=0, tiled=True),
        lax.all_gather(part_output, "seq", axis=0, tiled=True),
        lax.all_gather(part_inner, "seq", axis=0, tiled=True),
        lax.all_gather(part_outer, "seq", axis=0, tiled=True),
    )
    base = tokens + position_table(coordinates, width)
    normed, first_back = jax.vjp(layer_norm, base, first_gain, first_shift)
    normed_low = normed.astype(jnp.bfloat16)
    query = (
        (product(normed_low, full_query) + query_bias)
        .astype(jnp.bfloat16)
        .reshape(rows, HEADS, head_size)
    )
    key = product(normed_low, full_key).astype(jnp.bfloat16).reshape(rows, HEADS, head_size)
    value = (
        (product(normed_low, full_value) + value_bias)
        .astype(jnp.bfloat16)
        .reshape(rows, HEADS, head_size)
    )
    kept = []
    for ratio in ratios:
        picked = branch_prepare(query, key, value, valid, start, ratio, lengths)
        bits = (ratio * SUBLEN // rows).bit_length() - 1
        gathered = segment_gather(picked[1], picked[2], picked[3], linear, bits)
        blocks = max(1, 8 // ratio)
        result, total = run_blocks(block_forward, (picked[0],) + gathered + picked[4:], blocks)
        kept.append((picked, None, result, total))
    spread_totals = jnp.stack(
        [
            spread_rows(jnp.swapaxes(item[3], 0, 1)[:, :, None], ratio, big_negative)[:, :, 0]
            for item, ratio in zip(kept, ratios)
        ]
    )
    top = jnp.max(spread_totals, axis=0)
    overall = top + jnp.log(jnp.sum(jnp.exp(spread_totals - top[None]), axis=0))
    merged = jnp.zeros((rows, HEADS, head_size), jnp.float32)
    branch_weights = []
    for item, ratio in zip(kept, ratios):
        weight = jnp.exp(
            item[3] - jnp.swapaxes(select_rows(overall[:, :, None], ratio)[:, :, 0], 0, 1)
        )
        branch_weights.append(weight)
        merged = merged + spread_rows(jnp.swapaxes(item[2] * weight[:, :, None], 0, 1), ratio, 0.0)
    merged_low = merged.reshape(rows, width).astype(jnp.bfloat16)
    middle = base + product(merged_low, full_output) + output_bias
    normed_two, second_back = jax.vjp(layer_norm, middle, second_gain, second_shift)
    normed_two_low = normed_two.astype(jnp.bfloat16)
    inner = product(normed_two_low, full_inner) + inner_bias
    activated = jax.nn.gelu(inner, approximate=False).astype(jnp.bfloat16)
    output = middle + product(activated, full_outer) + outer_bias
    grad_outer = cotangent.astype(jnp.bfloat16)
    outer_weight_grad = product_left(activated, grad_outer)
    outer_bias_grad = jnp.sum(grad_outer.astype(jnp.float32), axis=0)
    grad_inner = (product_right(grad_outer, full_outer) * gelu_slope(inner)).astype(jnp.bfloat16)
    inner_weight_grad = product_left(normed_two_low, grad_inner)
    inner_bias_grad = jnp.sum(grad_inner.astype(jnp.float32), axis=0)
    grad_middle_part, second_gain_grad, second_shift_grad = second_back(
        product_right(grad_inner, full_inner)
    )
    grad_middle = cotangent + grad_middle_part
    grad_attended = grad_middle.astype(jnp.bfloat16)
    output_weight_grad = product_left(merged_low, grad_attended)
    output_bias_grad = jnp.sum(grad_attended.astype(jnp.float32), axis=0)
    grad_merged = product_right(grad_attended, full_output).reshape(rows, HEADS, head_size)
    grad_query = jnp.zeros((rows, HEADS, head_size), jnp.float32)
    grad_key = jnp.zeros((rows, HEADS, head_size), jnp.float32)
    grad_value = jnp.zeros((rows, HEADS, head_size), jnp.float32)
    for item, weight, ratio in zip(kept, branch_weights, ratios):
        picked, gathered, result, total = item
        bits = (ratio * SUBLEN // rows).bit_length() - 1
        blocks = max(1, 8 // ratio)
        gathered = segment_gather_again(picked[1], picked[2], picked[3], linear, bits)
        grad_picked = jnp.swapaxes(select_rows(grad_merged, ratio), 0, 1)
        merged_picked = jnp.swapaxes(select_rows(merged, ratio), 0, 1)
        grad_total = weight * (
            jnp.sum(grad_picked * result, axis=2) - jnp.sum(grad_picked * merged_picked, axis=2)
        )
        grad_low = (weight[:, :, None] * grad_picked).astype(jnp.bfloat16)
        term_query, term_key, term_value = run_blocks(
            block_backward,
            (picked[0],) + gathered + picked[4:] + (total, grad_low, grad_total),
            blocks,
        )
        term_key, term_value = segment_reduce(term_key, term_value, linear, bits)
        grad_query = grad_query + spread_rows(jnp.swapaxes(term_query, 0, 1), ratio, 0.0)
        grad_key = grad_key + spread_rows(jnp.swapaxes(term_key, 0, 1), ratio, 0.0)
        grad_value = grad_value + spread_rows(jnp.swapaxes(term_value, 0, 1), ratio, 0.0)
    query_low = grad_query.reshape(rows, width).astype(jnp.bfloat16)
    key_low = grad_key.reshape(rows, width).astype(jnp.bfloat16)
    value_low = grad_value.reshape(rows, width).astype(jnp.bfloat16)
    query_weight_grad = product_left(normed_low, query_low)
    key_weight_grad = product_left(normed_low, key_low)
    value_weight_grad = product_left(normed_low, value_low)
    query_bias_grad = jnp.sum(query_low.astype(jnp.float32), axis=0)
    value_bias_grad = jnp.sum(value_low.astype(jnp.float32), axis=0)
    grad_normed = (
        product_right(query_low, full_query)
        + product_right(key_low, full_key)
        + product_right(value_low, full_value)
    )
    grad_base_part, first_gain_grad, first_shift_grad = first_back(grad_normed)
    token_grad = grad_middle + grad_base_part
    sum_query, sum_key, sum_value, sum_output, sum_inner, sum_outer = (
        lax.psum_scatter(query_weight_grad, "grp", scatter_dimension=1, tiled=True),
        lax.psum_scatter(key_weight_grad, "grp", scatter_dimension=1, tiled=True),
        lax.psum_scatter(value_weight_grad, "grp", scatter_dimension=1, tiled=True),
        lax.psum_scatter(output_weight_grad, "grp", scatter_dimension=1, tiled=True),
        lax.psum_scatter(inner_weight_grad, "grp", scatter_dimension=1, tiled=True),
        lax.psum_scatter(outer_weight_grad, "grp", scatter_dimension=1, tiled=True),
    )
    sum_query, sum_key, sum_value, sum_output, sum_inner, sum_outer = (
        lax.psum_scatter(sum_query, "seq", scatter_dimension=0, tiled=True),
        lax.psum_scatter(sum_key, "seq", scatter_dimension=0, tiled=True),
        lax.psum_scatter(sum_value, "seq", scatter_dimension=0, tiled=True),
        lax.psum_scatter(sum_output, "seq", scatter_dimension=0, tiled=True),
        lax.psum_scatter(sum_inner, "seq", scatter_dimension=0, tiled=True),
        lax.psum_scatter(sum_outer, "seq", scatter_dimension=0, tiled=True),
    )
    small = lax.psum(
        (
            first_gain_grad,
            first_shift_grad,
            query_bias_grad,
            value_bias_grad,
            output_bias_grad,
            second_gain_grad,
            second_shift_grad,
            inner_bias_grad,
            outer_bias_grad,
        ),
        ("seq", "grp"),
    )
    return (
        output,
        token_grad,
        small[0],
        small[1],
        sum_query,
        small[2],
        sum_key,
        sum_value,
        small[3],
        sum_output,
        small[4],
        small[5],
        small[6],
        sum_inner,
        small[7],
        sum_outer,
        small[8],
    )


def solution(mesh):
    placed = (
        P(("seq", "grp"), None),
        P(("seq", "grp"), None),
        P(),
        P(("seq", "grp")),
        P(),
        P(),
        P("seq", "grp"),
        P(),
        P("seq", "grp"),
        P("seq", "grp"),
        P(),
        P("seq", "grp"),
        P(),
        P(),
        P(),
        P("seq", "grp"),
        P(),
        P("seq", "grp"),
        P(),
        P(("seq", "grp"), None),
    )
    return jax.shard_map(
        body,
        mesh=mesh,
        in_specs=placed,
        out_specs=(
            P(("seq", "grp"), None),
            P(("seq", "grp"), None),
            P(),
            P(),
            P("seq", "grp"),
            P(),
            P("seq", "grp"),
            P("seq", "grp"),
            P(),
            P("seq", "grp"),
            P(),
            P(),
            P(),
            P("seq", "grp"),
            P(),
            P("seq", "grp"),
            P(),
        ),
        check_vma=False,
    )
```

profile of v0, /device:TPU:0, one launch (start us, length us, event | category | flops | bytes accessed | tf_op | source)
XLA Modules:
  0.0 2353.8 jit_solution(6573264829220335060)
XLA Ops:
  359.8 11.3 collective-permute-done.43
  378.2 54.7 %while.23 = (s32[]{:T(128)}, f32[8,2,512,48]{2,3,1,0:T(8,128)S(1)}, f32[8,2,512]{2,1,0:T(2,128)S(1)}, s32[8,2,512]{2,1,0:T(2,128)}, s32[8,2,1024]{2,1,0:T(2,128)...) while((s32[]{:T(128)}, f32[8,2,512,48]{2,3,1,0:T(8,128)S(1)}, ...), condition=%wide.region_8.9_spmd, body=%wide.region_5.8_spmd.sunk | while | flops 212861952 | bytes 13387909 | solution.py:96
  457.9 27.8 %while.24 = (s32[]{:T(128)}, f32[4,4,256,48]{2,3,1,0:T(8,128)S(1)}, f32[4,4,256]{2,1,0:T(4,128)S(1)}, s32[4,4,256]{2,1,0:T(4,128)}, s32[4,4,1024]{2,1,0:T(4,128)...) while((s32[]{:T(128)}, f32[4,4,256,48]{2,3,1,0:T(8,128)S(1)}, ...), condition=%wide.region_14.15_spmd, body=%wide.region_11.14_spmd.sunk | while | flops 212864000 | bytes 13838469 | solution.py:96
  509.1 10.5 while.25
  692.7 12.3 fusion.225
  716.3 19.6 fusion.209
  782.0 256.6 %while.26 = (s32[]{:T(128)}, f32[8,2,512,48]{2,3,1,0:T(8,128)S(1)}, f32[8,2,1024,48]{2,3,1,0:T(8,128)}, f32[8,2,1024,48]{2,3,1,0:T(8,128)}, s32[8,2,512]{2,1,0:T...) while((s32[]{:T(128)}, f32[8,2,512,48]{2,3,1,0:T(8,128)S(1)}, ...), condition=%wide.region_38.39_spmd, body=%wide.region_36.38_spmd.sunk | while | flops 522344448 | bytes 48219300 | solution.py:96
  793.6 8.9 fusion.476
  802.6 8.2 fusion.475
  825.7 8.9 fusion.476
  834.6 8.3 fusion.475
  857.7 8.9 fusion.476
  889.8 8.9 fusion.476
  898.7 8.2 fusion.475
  921.8 8.9 fusion.476
  930.8 8.2 fusion.475
  953.9 8.9 fusion.476
  962.8 8.3 fusion.475
  985.9 8.9 fusion.476
  1017.9 8.9 fusion.476
  1026.8 8.2 fusion.475
  1053.6 128.4 %while.27 = (s32[]{:T(128)}, f32[4,4,256,48]{2,3,1,0:T(8,128)}, f32[4,4,1024,48]{2,3,1,0:T(8,128)S(1)}, f32[4,4,1024,48]{2,3,1,0:T(8,128)}, s32[4,4,256]{2,1,0:T...) while((s32[]{:T(128)}, f32[4,4,256,48]{2,3,1,0:T(8,128)}, ...), condition=%wide.region_43.44_spmd, body=%wide.region_41.43_spmd.sunk | while | flops 522444800 | bytes 49652900 | solution.py:96
  1073.6 8.9 fusion.489
  1105.7 8.9 fusion.489
  1137.7 8.9 fusion.489
  1169.6 8.9 fusion.489
  1192.0 58.9 %while.28 = (s32[]{:T(128)}, f32[2,8,128,48]{2,3,1,0:T(8,128)S(1)}, f32[2,8,1024,48]{2,3,1,0:T(8,128)}, f32[2,8,1024,48]{2,3,1,0:T(8,128)}, s32[2,8,128]{2,1,0:T...) while((s32[]{:T(128)}, f32[2,8,128,48]{2,3,1,0:T(8,128)S(1)}, ...), condition=%wide.region_48.49_spmd, body=%wide.region_46.48_spmd.sunk | while | flops 522645504 | bytes 52520100 | solution.py:96
  1200.2 9.2 bitcast_dynamic-update-slice_fusion.14
  1209.4 8.3 fusion.503
  1229.6 9.2 bitcast_dynamic-update-slice_fusion.14
  1269.1 12.3 fusion.246
  1316.4 12.9 fusion.285
  1433.8 12.2 collective-permute-done.70
  1453.0 26.5 %collective-permute-done.66 = f32[16,512,48]{1,2,0:T(8,128)S(1)} collective-permute-done((f32[16,512,48]{1,2,0:T(8,128)S(1)}, f32[16,512,48]{1,2,0:T(8,128)S(1)}, u32[]{:S(2)}, u32[]{:S(2)}) %collective-permute-start.66) | collective-permute-done | bytes 1572896 | tf_op jit(solution)/shard_map/ppermute | solution.py:24
  1487.4 11.6 collective-permute-done.49
  1650.6 8.5 convert_reduce_fusion.3
  1659.1 11.5 fusion.274
  1709.5 33.3 %reduce-scatter.23.cloned.1.call-done = f32[768,192]{0,1:T(8,128)} async-done(((f32[768,768]{0,1:T(8,128)}), f32[768,192]{0,1:T(8,128)}) %reduce-scatter.23.cloned.1.call-update) | async-done | bytes 589840 | tf_op jit(solution)/shard_map/reduce_scatter | solution.py:405
  1745.1 33.3 %reduce-scatter.25.cloned.1.call-done = f32[768,192]{0,1:T(8,128)} async-done(((f32[768,768]{0,1:T(8,128)}), f32[768,192]{0,1:T(8,128)}) %reduce-scatter.25.cloned.1.call-update) | async-done | bytes 589840 | tf_op jit(solution)/shard_map/reduce_scatter | solution.py:406
  1780.7 78.8 %reduce-scatter.29.cloned.1.call-done = f32[768,768]{1,0:T(8,128)} async-done(((f32[768,3072]{1,0:T(8,128)}), f32[768,768]{1,0:T(8,128)}) %reduce-scatter.29.cloned.1.call-update) | async-done | bytes 2359312 | tf_op jit(solution)/shard_map/reduce_scatter | solution.py:408
  1859.7 80.7 %reduce-scatter.33.cloned.1.call-done = f32[3072,192]{0,1:T(8,128)} async-done(((f32[3072,768]{0,1:T(8,128)}), f32[3072,192]{0,1:T(8,128)}) %reduce-scatter.33.cloned.1.call-update) | async-done | bytes 2359312 | tf_op jit(solution)/shard_map/reduce_scatter | solution.py:409
  1957.1 40.8 %all-reduce = (f32[768]{0:T(1024)}, f32[768]{0:T(1024)}, f32[768]{0:T(1024)}, f32[768]{0:T(1024)}, f32[768]{0:T(1024)}, /*index=5*/f32[768]{0:T(1024)}, f32[768]{0:T(1024)}, f32[3072]{0:T(1024)}, f32[768]{0:T(1024)}) all-reduce(f32[768]{0:T(1024)S(1)} %get-tuple-element.720, ...), channel_id=1, replica_groups=mesh['seq'=8,'grp'=4] {'seq','grp'}, use_global_device_ids=true, to_apply=%region_58.59 | all-reduce | flops 9216 | bytes 73728 | tf_op jit(solution)/shard_map/psum | solution.py:419
  1998.0 8.9 reduce-scatter.43.cloned.1.call-done
  2006.9 65.5 %reduce-scatter.37.cloned.1.call-done = f32[96,192]{1,0:T(8,128)} async-done(((f32[768,192]{1,0:T(8,128)}), f32[96,192]{1,0:T(8,128)}) %reduce-scatter.37.cloned.1.call-update) | async-done | bytes 73744
  2072.4 65.2 %reduce-scatter.39.cloned.1.call-done = f32[96,192]{1,0:T(8,128)} async-done(((f32[768,192]{1,0:T(8,128)}), f32[96,192]{1,0:T(8,128)}) %reduce-scatter.39.cloned.1.call-update) | async-done | bytes 73744
  2137.6 65.5 %reduce-scatter.41.cloned.1.call-done = f32[96,192]{1,0:T(8,128)} async-done(((f32[768,192]{1,0:T(8,128)}), f32[96,192]{1,0:T(8,128)}) %reduce-scatter.41.cloned.1.call-update) | async-done | bytes 73744
  2203.1 71.9 %reduce-scatter.31.cloned.1.call-done = f32[96,768]{1,0:T(8,128)} async-done(((f32[768,768]{1,0:T(8,128)}), f32[96,768]{1,0:T(8,128)}) %reduce-scatter.31.cloned.1.call-update) | async-done | bytes 294928 | tf_op jit(solution)/shard_map/reduce_scatter | solution.py:416
  2275.0 71.8 %reduce-scatter.35.cloned.1.call-done = f32[384,192]{0,1:T(8,128)} async-done(((f32[3072,192]{0,1:T(8,128)}), f32[384,192]{0,1:T(8,128)}) %reduce-scatter.35.cloned.1.call-update) | async-done | bytes 294928 | tf_op jit(solution)/shard_map/reduce_scatter | solution.py:417
  (1552 shorter events, 1394.8 us)
Async XLA Ops:
  7.2 155.0 %all-gather.9.cloned.1.call-start = ((), (), s32[]{:S(2)}) async-start(), calls=%async_computation.13 | async-start | bytes 1327104 | tf_op jit(solution)/shard_map/all_gather | solution.py:300
  15.9 159.4 %all-gather.7.cloned.1.call-start = ((), (), s32[]{:S(2)}) async-start(), calls=%async_computation.12 | async-start | bytes 1327104 | tf_op jit(solution)/shard_map/all_gather | solution.py:299
  23.3 154.0 %all-gather.11.cloned.1.call-start = ((), (), s32[]{:S(2)}) async-start(), calls=%async_computation.14 | async-start | bytes 1327104 | tf_op jit(solution)/shard_map/all_gather | solution.py:301
  30.7 682.7 %all-gather.13.cloned.1.call-start = ((), (), s32[]{:S(2)}) async-start(), calls=%async_computation.15 | async-start | bytes 1327104 | tf_op jit(solution)/shard_map/all_gather | solution.py:302
  37.3 678.9 %all-gather.15.cloned.1.call-start = ((), (), s32[]{:S(2)}) async-start(), calls=%async_computation.16 | async-start | bytes 5308416 | tf_op jit(solution)/shard_map/all_gather | solution.py:303
  45.6 690.3 %all-gather.17.cloned.1.call-start = ((), (), s32[]{:S(2)}) async-start(), calls=%async_computation.17 | async-start | bytes 5308416 | tf_op jit(solution)/shard_map/all_gather | solution.py:304
  46.4 93.6 %collective-permute-start.26 = (bf16[16,32]{1,0:T(8,128)(2,1)}, bf16[16,32]{1,0:T(8,128)(2,1)}, u32[]{:S(2)}, u32[]{:S(2)}) collective-permute-start(bf16[16,32]{1,0:T(8,128)(2,1)} %bitcast.173), channel_id=1, source_target_pairs={{0,1},{1,0},{2,3},{3,2},{4,5},{5,4},{6,7},{7,6},{8,9},{9,8},{10,11... | collective-permute-start | bytes 3080 | tf_op jit(solution)/shard_map/ppermute | solution.py:24
  47.5 94.8 %collective-permute-start.18 = (bf16[16,64]{1,0:T(8,128)(2,1)}, bf16[16,64]{1,0:T(8,128)(2,1)}, u32[]{:S(2)}, u32[]{:S(2)}) collective-permute-start(bf16[16,64]{1,0:T(8,128)(2,1)} %broadcast_bitcast_fusion), channel_id=1, source_target_pairs={{0,1},{1,0},{2,3},{3,2},{4,5},{5,4},{6,7},{7,6},{8,9},{9,8},{10,11... | collective-permute-start | bytes 6152 | tf_op jit(solution)/shard_map/ppermute | solution.py:24
  48.5 97.6 %collective-permute-start.9 = (bf16[16,128]{1,0:T(8,128)(2,1)}, bf16[16,128]{1,0:T(8,128)(2,1)}, u32[]{:S(2)}, u32[]{:S(2)}) collective-permute-start(bf16[16,128]{1,0:T(8,128)(2,1)} %bitcast.122), channel_id=1, source_target_pairs={{0,1},{1,0},{2,3},{3,2},{4,5},{5,4},{6,7},{7,6},{8,9},{9,8},{10,11... | collective-permute-start | bytes 12296 | tf_op jit(solution)/shard_map/ppermute | solution.py:24
  49.5 108.8 %collective-permute-start = (bf16[16,512]{1,0:T(8,128)(2,1)}, bf16[16,512]{1,0:T(8,128)(2,1)}, u32[]{:S(2)}, u32[]{:S(2)}) collective-permute-start(bf16[16,512]{1,0:T(8,128)(2,1)} %transpose.543), channel_id=1, source_target_pairs={{0,1},{1,0},{2,3},{3,2},{4,5},{5,4},{6,7},{7,6},{8,9},{9,8},{10,11... | collective-permute-start | bytes 49160 | tf_op jit(solution)/shard_map/ppermute | solution.py:24
  50.5 100.8 %collective-permute-start.3 = (bf16[16,256]{1,0:T(8,128)(2,1)}, bf16[16,256]{1,0:T(8,128)(2,1)}, u32[]{:S(2)}, u32[]{:S(2)}) collective-permute-start(bf16[16,256]{1,0:T(8,128)(2,1)} %bitcast.93), channel_id=1, source_target_pairs={{0,1},{1,0},{2,3},{3,2},{4,5},{5,4},{6,7},{7,6},{8,9},{9,8},{10,11... | collective-permute-start | bytes 24584 | tf_op jit(solution)/shard_map/ppermute | solution.py:24
  59.0 1638.4 %reduce-scatter.27.cloned.1.call-start = ((), (), s32[]{:S(2)}) async-start(), calls=%async_computation.21 | async-start | bytes 2949120 | tf_op jit(solution)/shard_map/reduce_scatter | solution.py:407
  175.3 103.0 %collective-permute-start.31 = (bf16[16,32,48]{1,2,0:T(8,128)(2,1)}, bf16[16,32,48]{1,2,0:T(8,128)(2,1)}, u32[]{:S(2)}, u32[]{:S(2)}) collective-permute-start(bf16[16,32,48]{1,2,0:T(8,128)(2,1)} %copy.1046), channel_id=1, source_target_pairs={{0,1},{1,0},{2,3},{3,2},{4,5},{5,4},{6,7},{7,6},{8,9},{9,8},{10,11... | collective-permute-start | bytes 147464 | tf_op jit(solution)/shard_map/ppermute | solution.py:24
  234.9 45.7 %collective-permute-start.22 = (bf16[16,64,48]{1,2,0:T(8,128)(2,1)}, bf16[16,64,48]{1,2,0:T(8,128)(2,1)}, u32[]{:S(2)}, u32[]{:S(2)}) collective-permute-start(bf16[16,64,48]{1,2,0:T(8,128)(2,1)} %bitcast.169), channel_id=1, source_target_pairs={{0,1},{1,0},{2,3},{3,2},{4,5},{5,4},{6,7},{7,6},{8,9},{9,8},{10,11... | collective-permute-start | bytes 294920 | tf_op jit(solution)/shard_map/ppermute | solution.py:24
  244.8 51.3 %collective-permute-start.12 = (bf16[16,128,48]{1,2,0:T(8,128)(2,1)S(1)}, bf16[16,128,48]{1,2,0:T(8,128)(2,1)}, u32[]{:S(2)}, u32[]{:S(2)}) collective-permute-start(bf16[16,128,48]{1,2,0:T(8,128)(2,1)S(1)} %bitcast.1140), channel_id=1, source_target_pairs={{0,1},{1,0},{2,3},{3,2},{4,5},{5,4},{6,7},{7,6},{8,9},{9,8},{10,11... | collective-permute-start | bytes 589832 | tf_op jit(solution)/shard_map/ppermute | solution.py:24
  249.5 48.1 %collective-permute-start.15 = (bf16[16,128,48]{1,2,0:T(8,128)(2,1)}, bf16[16,128,48]{1,2,0:T(8,128)(2,1)}, u32[]{:S(2)}, u32[]{:S(2)}) collective-permute-start(bf16[16,128,48]{1,2,0:T(8,128)(2,1)} %bitcast.148), channel_id=1, source_target_pairs={{0,1},{1,0},{2,3},{3,2},{4,5},{5,4},{6,7},{7,6},{8,9},{9,8},{10,11... | collective-permute-start | bytes 589832 | tf_op jit(solution)/shard_map/ppermute | solution.py:24
  253.6 119.1 %collective-permute-start.1 = (bf16[16,512,48]{1,2,0:T(8,128)(2,1)}, bf16[16,512,48]{1,2,0:T(8,128)(2,1)}, u32[]{:S(2)}, u32[]{:S(2)}) collective-permute-start(bf16[16,512,48]{1,2,0:T(8,128)(2,1)} %bitcast.1126), channel_id=1, source_target_pairs={{0,1},{1,0},{2,3},{3,2},{4,5},{5,4},{6,7},{7,6},{8,9},{9,8},{10,11... | collective-permute-start | bytes 2359304 | tf_op jit(solution)/shard_map/ppermute | solution.py:24
  280.0 45.2 %collective-permute-start.7 = (bf16[16,256,48]{1,2,0:T(8,128)(2,1)S(1)}, bf16[16,256,48]{1,2,0:T(8,128)(2,1)S(1)}, u32[]{:S(2)}, u32[]{:S(2)}) collective-permute-start(bf16[16,256,48]{1,2,0:T(8,128)(2,1)S(1)} %bitcast.1117), channel_id=1, source_target_pairs={{0,1},{1,0},{2,3},{3,2},{4,5},{5,4},{6,7},{7,6},{8,9},{9,8},{10,11... | collective-permute-start | bytes 1179656 | tf_op jit(solution)/shard_map/ppermute | solution.py:24
  315.9 61.4 %collective-permute-start.2 = (bf16[16,512,48]{1,2,0:T(8,128)(2,1)S(1)}, bf16[16,512,48]{1,2,0:T(8,128)(2,1)S(1)}, u32[]{:S(2)}, u32[]{:S(2)}) collective-permute-start(bf16[16,512,48]{1,2,0:T(8,128)(2,1)S(1)} %bitcast.1124), channel_id=1, source_target_pairs={{0,1},{1,0},{2,3},{3,2},{4,5},{5,4},{6,7},{7,6},{8,9},{9,8},{10,11... | collective-permute-start | bytes 2359304 | tf_op jit(solution)/shard_map/ppermute | solution.py:24
  355.5 93.7 %collective-permute-start.8 = (bf16[16,512,48]{1,2,0:T(8,128)(2,1)}, bf16[16,512,48]{1,2,0:T(8,128)(2,1)}, u32[]{:S(2)}, u32[]{:S(2)}) collective-permute-start(bf16[16,512,48]{1,2,0:T(8,128)(2,1)} %maximum_select_fusion.12), channel_id=1, source_target_pairs={{0,2},{1,3},{2,0},{3,1},{4,6},{5,7},{6,4},{7,5},{8,10},{9,11},{10,... | collective-permute-start | bytes 2359304 | tf_op jit(solution)/shard_map/ppermute | solution.py:24
  358.1 95.0 %collective-permute-start.6 = (bf16[16,512,48]{1,2,0:T(8,128)(2,1)}, bf16[16,512,48]{1,2,0:T(8,128)(2,1)}, u32[]{:S(2)}, u32[]{:S(2)}) collective-permute-start(bf16[16,512,48]{1,2,0:T(8,128)(2,1)} %maximum_select_fusion.10), channel_id=1, source_target_pairs={{0,2},{1,3},{2,0},{3,1},{4,6},{5,7},{6,4},{7,5},{8,10},{9,11},{10,... | collective-permute-start | bytes 2359304 | tf_op jit(solution)/shard_map/ppermute | solution.py:24
  371.1 130.7 %collective-permute-start.17 = (bf16[16,512,48]{1,2,0:T(8,128)(2,1)}, bf16[16,512,48]{1,2,0:T(8,128)(2,1)}, u32[]{:S(2)}, u32[]{:S(2)}) collective-permute-start(bf16[16,512,48]{1,2,0:T(8,128)(2,1)} %maximum_select_fusion.16), channel_id=1, source_target_pairs={{0,4},{1,5},{2,6},{3,7},{4,0},{5,1},{6,2},{7,3},{8,12},{9,13},{10,... | collective-permute-start | bytes 2359304 | tf_op jit(solution)/shard_map/ppermute | solution.py:24
  372.7 133.1 %collective-permute-start.14 = (bf16[16,512,48]{1,2,0:T(8,128)(2,1)}, bf16[16,512,48]{1,2,0:T(8,128)(2,1)}, u32[]{:S(2)}, u32[]{:S(2)}) collective-permute-start(bf16[16,512,48]{1,2,0:T(8,128)(2,1)} %maximum_select_fusion.14), channel_id=1, source_target_pairs={{0,4},{1,5},{2,6},{3,7},{4,0},{5,1},{6,2},{7,3},{8,12},{9,13},{10,... | collective-permute-start | bytes 2359304 | tf_op jit(solution)/shard_map/ppermute | solution.py:24
  377.3 150.0 %collective-permute-start.25 = (bf16[16,512,48]{1,2,0:T(8,128)(2,1)}, bf16[16,512,48]{1,2,0:T(8,128)(2,1)}, u32[]{:S(2)}, u32[]{:S(2)}) collective-permute-start(bf16[16,512,48]{1,2,0:T(8,128)(2,1)} %maximum_select_fusion.18), channel_id=1, source_target_pairs={{0,8},{1,9},{2,10},{3,11},{4,12},{5,13},{6,14},{7,15},{8,0},{9,1},... | collective-permute-start | bytes 2359304 | tf_op jit(solution)/shard_map/ppermute | solution.py:24
  449.2 120.6 %collective-permute-start.39 = (bf16[16,512,48]{1,2,0:T(8,128)(2,1)}, bf16[16,512,48]{1,2,0:T(8,128)(2,1)}, u32[]{:S(2)}, u32[]{:S(2)}) collective-permute-start(bf16[16,512,48]{1,2,0:T(8,128)(2,1)} %maximum_select_fusion.20), channel_id=1, source_target_pairs={{0,8},{1,9},{2,10},{3,11},{4,12},{5,13},{6,14},{7,15},{8,0},{9,1},... | collective-permute-start | bytes 2359304 | tf_op jit(solution)/shard_map/ppermute | solution.py:24
  453.1 84.9 %collective-permute-start.35 = (bf16[16,512,48]{1,2,0:T(8,128)(2,1)}, bf16[16,512,48]{1,2,0:T(8,128)(2,1)}, u32[]{:S(2)}, u32[]{:S(2)}) collective-permute-start(bf16[16,512,48]{1,2,0:T(8,128)(2,1)} %maximum_select_fusion.19), channel_id=1, source_target_pairs={{0,16},{1,17},{2,18},{3,19},{4,20},{5,21},{6,22},{7,23},{8,24},{9,... | collective-permute-start | bytes 2359304 | tf_op jit(solution)/shard_map/ppermute | solution.py:24
  501.8 54.6 %collective-permute-start.44 = (bf16[16,512,48]{1,2,0:T(8,128)(2,1)}, bf16[16,512,48]{1,2,0:T(8,128)(2,1)}, u32[]{:S(2)}, u32[]{:S(2)}) collective-permute-start(bf16[16,512,48]{1,2,0:T(8,128)(2,1)} %maximum_select_fusion.21), channel_id=1, source_target_pairs={{0,16},{1,17},{2,18},{3,19},{4,20},{5,21},{6,22},{7,23},{8,24},{9,... | collective-permute-start | bytes 2359304 | tf_op jit(solution)/shard_map/ppermute | solution.py:24
  1184.2 236.4 %collective-permute-start.46 = (f32[16,512,48]{1,2,0:T(8,128)}, f32[16,512,48]{1,2,0:T(8,128)}, u32[]{:S(2)}, u32[]{:S(2)}) collective-permute-start(f32[16,512,48]{1,2,0:T(8,128)} %slice_select_fusion.8), channel_id=1, source_target_pairs={{0,2},{1,3},{2,0},{3,1},{4,6},{5,7},{6,4},{7,5},{8,10},{9,11},{10,... | collective-permute-start | bytes 4718600 | tf_op jit(solution)/shard_map/ppermute | solution.py:24
  1254.5 170.1 %collective-permute-start.48 = (f32[16,512,48]{1,2,0:T(8,128)}, f32[16,512,48]{1,2,0:T(8,128)}, u32[]{:S(2)}, u32[]{:S(2)}) collective-permute-start(f32[16,512,48]{1,2,0:T(8,128)} %slice_select_fusion.7), channel_id=1, source_target_pairs={{0,4},{1,5},{2,6},{3,7},{4,0},{5,1},{6,2},{7,3},{8,12},{9,13},{10,... | collective-permute-start | bytes 4718600 | tf_op jit(solution)/shard_map/ppermute | solution.py:24
  1285.0 141.9 %collective-permute-start.51 = (f32[16,512,48]{1,2,0:T(8,128)}, f32[16,512,48]{1,2,0:T(8,128)}, u32[]{:S(2)}, u32[]{:S(2)}) collective-permute-start(f32[16,512,48]{1,2,0:T(8,128)} %slice_select_fusion.6), channel_id=1, source_target_pairs={{0,8},{1,9},{2,10},{3,11},{4,12},{5,13},{6,14},{7,15},{8,0},{9,1},... | collective-permute-start | bytes 4718600 | tf_op jit(solution)/shard_map/ppermute | solution.py:24
  1313.5 115.9 %collective-permute-start.55 = (f32[16,512,48]{1,2,0:T(8,128)}, f32[16,512,48]{1,2,0:T(8,128)}, u32[]{:S(2)}, u32[]{:S(2)}) collective-permute-start(f32[16,512,48]{1,2,0:T(8,128)} %slice_select_fusion.5), channel_id=1, source_target_pairs={{0,16},{1,17},{2,18},{3,19},{4,20},{5,21},{6,22},{7,23},{8,24},{9,... | collective-permute-start | bytes 4718600 | tf_op jit(solution)/shard_map/ppermute | solution.py:24
  1364.0 82.0 %collective-permute-start.70 = (f32[16,512,48]{1,2,0:T(8,128)}, f32[16,512,48]{1,2,0:T(8,128)}, u32[]{:S(2)}, u32[]{:S(2)}) collective-permute-start(f32[16,512,48]{1,2,0:T(8,128)} %slice_select_fusion), channel_id=1, source_target_pairs={{0,16},{1,17},{2,18},{3,19},{4,20},{5,21},{6,22},{7,23},{8,24},{9,... | collective-permute-start | bytes 4718600 | tf_op jit(solution)/shard_map/ppermute | solution.py:24
  1412.0 295.2 %reduce-scatter.21.cloned.1.call-start = ((), (), s32[]{:S(2)}) async-start(), calls=%async_computation.18 | async-start | bytes 2949120 | tf_op jit(solution)/shard_map/reduce_scatter | solution.py:404
  1424.7 225.9 %collective-permute-start.60 = (f32[16,512,48]{1,2,0:T(8,128)}, f32[16,512,48]{1,2,0:T(8,128)}, u32[]{:S(2)}, u32[]{:S(2)}) collective-permute-start(f32[16,512,48]{1,2,0:T(8,128)} %slice_select_fusion.4), channel_id=1, source_target_pairs={{0,1},{1,0},{2,3},{3,2},{4,5},{5,4},{6,7},{7,6},{8,9},{9,8},{10,11... | collective-permute-start | bytes 4718600 | tf_op jit(solution)/shard_map/ppermute | solution.py:24
  1426.9 52.7 %collective-permute-start.66 = (f32[16,512,48]{1,2,0:T(8,128)S(1)}, f32[16,512,48]{1,2,0:T(8,128)S(1)}, u32[]{:S(2)}, u32[]{:S(2)}) collective-permute-start(f32[16,512,48]{1,2,0:T(8,128)S(1)} %slice_select_fusion.1), channel_id=1, source_target_pairs={{0,8},{1,9},{2,10},{3,11},{4,12},{5,13},{6,14},{7,15},{8,0},{9,1},... | collective-permute-start | bytes 4718600 | tf_op jit(solution)/shard_map/ppermute | solution.py:24
  1429.4 51.0 %collective-permute-start.63 = (f32[16,512,48]{1,2,0:T(8,128)S(1)}, f32[16,512,48]{1,2,0:T(8,128)S(1)}, u32[]{:S(2)}, u32[]{:S(2)}) collective-permute-start(f32[16,512,48]{1,2,0:T(8,128)S(1)} %slice_select_fusion.2), channel_id=1, source_target_pairs={{0,4},{1,5},{2,6},{3,7},{4,0},{5,1},{6,2},{7,3},{8,12},{9,13},{10,... | collective-permute-start | bytes 4718600 | tf_op jit(solution)/shard_map/ppermute | solution.py:24
  1499.0 58.8 %collective-permute-start.67 = (f32[16,256,48]{1,2,0:T(8,128)}, f32[16,256,48]{1,2,0:T(8,128)}, u32[]{:S(2)}, u32[]{:S(2)}) collective-permute-start(f32[16,256,48]{1,2,0:T(8,128)} %slice_select_fusion.11), channel_id=1, source_target_pairs={{0,4},{1,5},{2,6},{3,7},{4,0},{5,1},{6,2},{7,3},{8,12},{9,13},{10,... | collective-permute-start | bytes 2359304 | tf_op jit(solution)/shard_map/ppermute | solution.py:24
  1529.4 46.4 %collective-permute-start.53 = (f32[16,128,48]{1,2,0:T(8,128)S(1)}, f32[16,128,48]{1,2,0:T(8,128)}, u32[]{:S(2)}, u32[]{:S(2)}) collective-permute-start(f32[16,128,48]{1,2,0:T(8,128)S(1)} %slice_select_fusion.28), channel_id=1, source_target_pairs={{0,2},{1,3},{2,0},{3,1},{4,6},{5,7},{6,4},{7,5},{8,10},{9,11},{10,... | collective-permute-start | bytes 1179656 | tf_op jit(solution)/shard_map/ppermute | solution.py:24
  1673.9 68.9 %reduce-scatter.23.cloned.1.call-start = ((), (), s32[]{:S(2)}) async-start(), calls=%async_computation.19 | async-start | bytes 2949120 | tf_op jit(solution)/shard_map/reduce_scatter | solution.py:405
  1677.2 101.2 %reduce-scatter.25.cloned.1.call-start = ((), (), s32[]{:S(2)}) async-start(), calls=%async_computation.20 | async-start | bytes 2949120 | tf_op jit(solution)/shard_map/reduce_scatter | solution.py:406
  1679.5 180.0 %reduce-scatter.29.cloned.1.call-start = ((), (), s32[]{:S(2)}) async-start(), calls=%async_computation.22 | async-start | bytes 11796480 | tf_op jit(solution)/shard_map/reduce_scatter | solution.py:408
  1688.6 251.8 %reduce-scatter.33.cloned.1.call-start = ((), (), s32[]{:S(2)}) async-start(), calls=%async_computation.24 | async-start | bytes 11796480 | tf_op jit(solution)/shard_map/reduce_scatter | solution.py:409
  1697.4 309.5 %reduce-scatter.43.cloned.1.call-start = ((), (), s32[]{:S(2)}) async-start(), calls=%async_computation.29 | async-start | bytes 884736
  1699.7 372.7 %reduce-scatter.37.cloned.1.call-start = ((), (), s32[]{:S(2)}) async-start(), calls=%async_computation.26 | async-start | bytes 884736
  1709.4 428.1 %reduce-scatter.39.cloned.1.call-start = ((), (), s32[]{:S(2)}) async-start(), calls=%async_computation.27 | async-start | bytes 884736
  1745.0 458.1 %reduce-scatter.41.cloned.1.call-start = ((), (), s32[]{:S(2)}) async-start(), calls=%async_computation.28 | async-start | bytes 884736
  1780.6 494.3 %reduce-scatter.31.cloned.1.call-start = ((), (), s32[]{:S(2)}) async-start(), calls=%async_computation.23 | async-start | bytes 2654208 | tf_op jit(solution)/shard_map/reduce_scatter | solution.py:416
  1859.5 487.3 %reduce-scatter.35.cloned.1.call-start = ((), (), s32[]{:S(2)}) async-start(), calls=%async_computation.25 | async-start | bytes 2654208 | tf_op jit(solution)/shard_map/reduce_scatter | solution.py:417
  (327 other events, 4363.2 us)
Sparse Core Ops, SparseCore 0:
  16.0 42.4 all-gather.8
  60.7 39.7 all-gather.6
  102.7 39.7 all-gather.10
  144.5 40.3 all-gather.12
  187.0 78.6 all-gather.14
  267.6 103.4 all-gather.16
  1412.1 34.0 reduce-scatter.26
  1674.0 33.0 reduce-scatter.20
  1709.7 33.0 reduce-scatter.22
  1745.3 33.0 reduce-scatter.24
  1781.0 78.4 reduce-scatter.28
  1861.9 78.4 reduce-scatter.32
  1944.3 62.5 reduce-scatter.42
  2010.9 61.3 reduce-scatter.36
  2076.1 61.4 reduce-scatter.38
  2141.7 61.4 reduce-scatter.40
  2207.0 67.8 reduce-scatter.30
  2278.9 67.8 reduce-scatter.34
where the time goes:
time: 2370 us; the launch traced here: 2350 us
  waiting for transfers between devices  691 us (29%)
  local copies, waits for them, and re-layouts  646 us (27%)
  matrix products  611 us (26%)
  other arithmetic  245 us (10%)
  blocking collectives  80.8 us (3%)
  starting transfers between devices  58.9 us (2%)
    broadcast_in_dim x162, local copies, waits for them, and re-layouts, spread_rows(): full = jnp.where(match[None, :, None, :, None], shaped, filler)  325 us
    unnamed x22, waiting for transfers between devices  205 us
    dot_general x16, matrix products, block_backward(): jnp.einsum('hij,hix->hjx', grad_scores, query_block, preferred_element_ty...  141 us
    dot_general x16, matrix products, block_backward(): jnp.einsum('hij,hjx->hix', grad_scores, key_block, preferred_element_type...  138 us
    another operation x32, local copies, waits for them, and re-layouts, select_rows(): shaped = tensor.reshape(count, ratio, heads // ratio, ratio, feature)  118 us
    dot_general x30, matrix products, block_scores(): jnp.einsum('hix,hjx->hij', query_block, key_block, preferred_element_type...  117 us
    ppermute x75, waiting for transfers between devices, swapped(): return lax.ppermute(value, axis, pairs)  108 us
    reduce_scatter x1, waiting for transfers between devices, body(): lax.psum_scatter(outer_weight_grad, 'grp', scatter_dimension=1, tiled=True)  80.7 us
  transfers between devices with their start and end apart: 93, of which 26 were waited for; matrix products, arithmetic and copies ran while one was open for 44% of the time, Pallas kernels for 0%

commit v1 on v0

v1 whole, which is shorter than its diff:
```python
import functools
import math

import jax
import jax.numpy as jnp
from jax import lax
from jax.experimental import pallas as pl
from jax.experimental.pallas import tpu as pltpu
from jax.sharding import PartitionSpec as P

HEADS = 16

epsilon = 1e-05
NT = (((1,), (1,)), ((), ()))
NN = (((1,), (0,)), ((), ()))
f32 = jnp.float32
bf16 = jnp.bfloat16
BIG = 1e30
HD = 48
GROUP = 8
LANES = 128
BLOCK = 32
MSG = 160
FLAG = 2 * HD
MESH = pl.DeviceIdType.MESH
scale = HD ** (-0.5)
scale2 = scale * math.log2(math.e)
q_at = (0, 4096, 6144, 7168, 7680)
q_all = 7936
k_at = (0, 4096, 6144, 7168, 8192)
k_all = 9216


def reverse4(b):
    return (b & 1) * 8 + (b & 2) * 2 + (b & 4) // 2 + (b & 8) // 8


order = [reverse4(b) for b in range(16)]


def chunk_swap(head):
    return reverse4(head) >> 2


def block_swap(quad):
    return reverse4(4 * quad) & 3


def swap_blocks(rows, quad):
    return jnp.concatenate(
        [rows[BLOCK * (b ^ block_swap(quad)) :][:BLOCK] for b in range(16)], axis=0
    )


def swap_chunks(wide, head):
    return jnp.concatenate(
        [wide[:, LANES * (c ^ chunk_swap(head)) :][:, :LANES] for c in range(4)], axis=1
    )


def matmul(a, b, dims=NN):
    return lax.dot_general(a, b, dims, preferred_element_type=f32)


def spot(grp):
    linear = lax.axis_index("seq") * grp + lax.axis_index("grp")
    member = linear % GROUP
    return linear, member, linear - member


def device(linear, grp):
    return (linear // grp, linear % grp)


def greet(barrier, peers, grp):
    for peer in peers:
        pl.semaphore_signal(barrier, inc=1, device_id=device(peer, grp), device_id_type=MESH)


def plane_barrier(grp, deep):
    linear, member, base = spot(grp)
    barrier = pltpu.get_barrier_semaphore()
    for j in range(GROUP):

        @pl.when(member != j)
        def _():
            greet(barrier, [base + j], grp)

    total = GROUP - 1
    if deep:
        layer = linear // GROUP % 4
        for o in range(1, 4):
            greet(barrier, [linear + GROUP * ((layer + o) % 4 - layer)], grp)
        total += 3
    return barrier, total


def plane_copy(send, recv, send_sem, recv_sem, j, member, base, grp):
    return pltpu.make_async_remote_copy(
        src_ref=send.at[j],
        dst_ref=recv.at[member],
        send_sem=send_sem.at[j],
        recv_sem=recv_sem.at[member],
        device_id=device(base + j, grp),
        device_id_type=MESH,
    )


def plane_arrival(send, recv, send_sem, recv_sem, j, base, grp):
    return pltpu.make_async_remote_copy(
        src_ref=send.at[j],
        dst_ref=recv.at[j],
        send_sem=send_sem.at[j],
        recv_sem=recv_sem.at[j],
        device_id=device(base + j, grp),
        device_id_type=MESH,
    )


def plane_send(send, recv, send_sem, recv_sem, j, member, base, grp):
    @pl.when(member != j)
    def _():
        plane_copy(send, recv, send_sem, recv_sem, j, member, base, grp).start()

    @pl.when(member == j)
    def _():
        pltpu.make_async_copy(send.at[j], recv.at[j], recv_sem.at[j]).start()


def plane_wait(send, recv, send_sem, recv_sem, j, member, base, grp):
    @pl.when(member != j)
    def _():
        plane_arrival(send, recv, send_sem, recv_sem, j, base, grp).wait_recv()

    @pl.when(member == j)
    def _():
        pltpu.make_async_copy(send.at[j], recv.at[j], recv_sem.at[j]).wait()


def plane_drain(send, recv, send_sem, recv_sem, j, member, base, grp):
    @pl.when(member != j)
    def _():
        plane_copy(send, recv, send_sem, recv_sem, j, member, base, grp).wait_send()


def qkv_kernel(
    grp, slides, n_ref, w_ref, b_ref, f_ref, msg, q_ref, kv_ref, kv8, kv16,
    send, send_sem, recv_sem, deep_send, deep_recv,
):
    linear, member, base = spot(grp)
    barrier, total = plane_barrier(grp, True)
    plane = (send, msg, send_sem, recv_sem)
    for quad in range(4):
        part = matmul(n_ref[...], w_ref[quad]) + b_ref[quad]
        wide = swap_blocks(part.astype(bf16), quad).T
        flags = f_ref[...]
        flags = jnp.concatenate(
            [flags[:, BLOCK * (b ^ block_swap(quad)) :][:, :BLOCK] for b in range(16)], axis=1
        ).astype(bf16)
        for inner in range(4):
            head = 4 * quad + inner
            owner, at = head // 2, MSG * (head % 2)
            own = swap_chunks(wide[144 * inner : 144 * inner + 144], head)
            send[owner, at : at + 96] = own[48:]
            send[owner, at + 96 : at + 112] = swap_chunks(flags, head)
            send[owner, at + 112 : at + 160] = own[:48]
        if quad == 0:
            pl.semaphore_wait(barrier, total)
        for owner in (2 * quad, 2 * quad + 1):
            plane_send(*plane, owner, member, base, grp)
    row = lax.broadcasted_iota(jnp.int32, (16, 512), 0)
    layer = linear // GROUP % 4
    half = layer % 2
    for j in range(GROUP):
        plane_wait(*plane, j, member, base, grp)
        for i in range(2):
            block = msg[j, MSG * i : MSG * i + MSG]
            key_part = jnp.concatenate([block[:112], jnp.zeros((16, 512), bf16)], axis=0).T
            flags = block[96:112].astype(f32)
            chosen = jnp.where(
                row == 0, 1.0, jnp.where((row <= slides) & (flags == 0.0), 1.0, 0.0)
            )
            query_part = jnp.concatenate(
                [
                    block[112:160],
                    jnp.zeros((48, 512), bf16),
                    chosen.astype(bf16),
                    jnp.zeros((16, 512), bf16),
                ],
                axis=0,
            ).T
            kv_ref[i, 512 * j : 512 * j + 512] = key_part
            q_ref[i, 512 * j : 512 * j + 512] = query_part
            kv8[half, i, 64 * j : 64 * j + 64] = key_part[:64]
            kv16[layer, i, 32 * j : 32 * j + 32] = key_part[:32]
    copies = []
    for o in range(1, 4):
        other = (layer + o) % 4
        copies.append(
            pltpu.make_async_remote_copy(
                src_ref=kv16.at[layer],
                dst_ref=kv16.at[layer],
                send_sem=deep_send.at[o],
                recv_sem=deep_recv.at[4 - o],
                device_id=device(linear + GROUP * (other - layer), grp),
                device_id_type=MESH,
            )
        )
    copies.append(
        pltpu.make_async_remote_copy(
            src_ref=kv8.at[half],
            dst_ref=kv8.at[half],
            send_sem=deep_send.at[0],
            recv_sem=deep_recv.at[0],
            device_id=device(linear + GROUP - 2 * GROUP * half, grp),
            device_id_type=MESH,
        )
    )
    for copy in copies:
        copy.start()
    for j in range(GROUP):
        plane_drain(*plane, j, member, base, grp)
    for copy in copies:
        copy.wait_send()
    for o in range(1, 4):
        other = (layer + o) % 4
        pltpu.make_async_remote_copy(
            src_ref=kv16.at[layer],
            dst_ref=kv16.at[other],
            send_sem=deep_send.at[o],
            recv_sem=deep_recv.at[o],
            device_id=device(linear + GROUP * (other - layer), grp),
            device_id_type=MESH,
        ).wait_recv()
    pltpu.make_async_remote_copy(
        src_ref=kv8.at[half],
        dst_ref=kv8.at[1 - half],
        send_sem=deep_send.at[0],
        recv_sem=deep_recv.at[0],
        device_id=device(linear + GROUP - 2 * GROUP * half, grp),
        device_id_type=MESH,
    ).wait_recv()


def compact(rows, packed, at):
    for j in range(GROUP):
        for place, size in at:
            packed[place + size * j : place + size * j + size] = rows[512 * j : 512 * j + size]


def gather_keys(kv, kv8, kv16, kvc):
    compact(kv, kvc, ((0, 256), (2048, 128)))
    for i in range(2):
        kvc[3072 + 512 * i : 3584 + 512 * i] = kv8[i]
    for i in range(4):
        kvc[4096 + 256 * i : 4352 + 256 * i] = kv16[i]


def unit_forward(query, key, out):
    lane = lax.broadcasted_iota(jnp.int32, (256, LANES), 1)
    count = len(query)
    scores = [matmul(query[i](), key, NT) for i in range(count)]
    for i in range(count):
        top = jnp.max(scores[i], axis=1, keepdims=True) * scale2
        prob = jnp.exp2(scores[i] * scale2 - top).astype(bf16)
        out[i](jnp.where(lane == FLAG + 8, top, matmul(prob, key)))


def forward_kernel(slides, q_ref, kv_ref, kv8, kv16, om, stat, acc, qc, kvc):
    ones_lane = FLAG + 1 + slides
    q = q_ref.at[0]
    kv = kv_ref.at[0]
    compact(q, qc, ((0, 256), (2048, 128), (3072, 64), (3584, 32)))
    gather_keys(kv, kv8.at[:, 0], kv16.at[:, 0], kvc)

    def unit(source, q_from, keys, k_from, out_from, count):
        def reader(i):
            return lambda: source[pl.ds(q_from + 256 * i, 256)]

        def writer(i):
            def put(value):
                acc[pl.ds(out_from + 256 * i, 256)] = value

            return put

        unit_forward(
            [reader(i) for i in range(count)],
            keys[pl.ds(k_from, 1024)],
            [writer(i) for i in range(count)],
        )

    def first(u, _):
        at = pl.multiple_of(u * 1024, 1024)
        unit(q, at, kv, at, at, 4)
        return 0

    lax.fori_loop(0, 4, first, 0)

    def second(u, _):
        at = pl.multiple_of(u * 1024, 1024)
        unit(qc, at, kvc, at, at + 4096, 4)
        return 0

    lax.fori_loop(0, 3, second, 0)
    unit(qc, 3072, kvc, 3072, 7168, 2)
    unit(qc, 3584, kvc, 4096, 7680, 1)

    def merge(j, _):
        spans = ((256, 512, 1), (128, 256, 2), (64, 128, 3), (32, 64, 4), (0, 32, 5))
        parts = []
        for low, high, uses in reversed(spans):
            size = high - low
            lane = lax.broadcasted_iota(jnp.int32, (size, LANES), 1)
            pieces = [
                acc[pl.ds(q_at[r] + (512 >> r) * j + low, size)] for r in range(uses)
            ]
            tops = [piece[:, FLAG + 8 : FLAG + 9] for piece in pieces]
            query = q[pl.ds(512 * j + low, size)].astype(f32)
            key = kv[pl.ds(512 * j + low, size)].astype(f32)
            dots = jnp.sum(jnp.where(lane < HD, query * key, 0.0), axis=1, keepdims=True)
            own = jnp.where(
                key[:, FLAG : FLAG + 1] == 0.0, -BIG, dots * scale2 + math.log2(uses)
            )
            top = own
            for item in tops:
                top = jnp.maximum(top, item)
            weight = jnp.exp2(own - top)
            total = weight
            mix = weight * key
            for piece, item in zip(pieces, tops):
                weight = jnp.exp2(item - top)
                total = total + weight * piece[:, ones_lane : ones_lane + 1]
                mix = mix + weight * piece
            mix = mix / total
            parts.append(jnp.where(lane == FLAG, top + jnp.log2(total), mix))
        wide = jnp.concatenate(parts, axis=0).T
        om[j] = wide[HD : 2 * HD].astype(bf16)
        stat[0, j] = wide[HD : HD + 56]
        return 0

    lax.fori_loop(0, GROUP, merge, 0)


def join_quads(read):
    pairs = []
    for half in range(2):
        quads = []
        for quad in (2 * half, 2 * half + 1):
            wide = jnp.concatenate(
                [swap_chunks(read(4 * quad + i), 4 * quad + i) for i in range(4)], axis=0
            )
            quads.append(swap_blocks(wide.T, quad))
        pairs.append(jnp.concatenate(quads, axis=1))
    return jnp.concatenate(pairs, axis=1)


def merged_kernel(grp, om, out, recv, send_sem, recv_sem):
    linear, member, base = spot(grp)
    barrier, total = plane_barrier(grp, False)
    pl.semaphore_wait(barrier, total)
    plane = (om, recv, send_sem, recv_sem)
    for j in range(GROUP):
        plane_send(*plane, j, member, base, grp)
    for j in range(GROUP):
        plane_wait(*plane, j, member, base, grp)
    out[...] = join_quads(lambda h: recv[h // 2, HD * (h % 2) : HD * (h % 2) + HD])
    for j in range(GROUP):
        plane_drain(*plane, j, member, base, grp)


def spread_kernel(grp, rows_ref, recv, send, send_sem, recv_sem):
    linear, member, base = spot(grp)
    barrier, total = plane_barrier(grp, False)
    plane = (send, recv, send_sem, recv_sem)
    for quad in range(4):
        wide = swap_blocks(rows_ref[:, 192 * quad : 192 * quad + 192], quad).T
        for inner in range(4):
            head = 4 * quad + inner
            at = HD * (head % 2)
            send[head // 2, at : at + HD] = swap_chunks(wide[HD * inner : HD * inner + HD], head)
        if quad == 0:
            pl.semaphore_wait(barrier, total)
        for owner in (2 * quad, 2 * quad + 1):
            plane_send(*plane, owner, member, base, grp)
    for j in range(GROUP):
        plane_wait(*plane, j, member, base, grp)
    for j in range(GROUP):
        plane_drain(*plane, j, member, base, grp)


def backward_kernel(
    q_ref, kv_ref, kv8, kv16, msg, gm, stat, pre, dkv8, dkv16,
    qc, kvc, dor, kt, ld, dkv, dqt,
):
    q = q_ref.at[0]
    kv = kv_ref.at[0]
    compact(q, qc, ((0, 256), (2048, 128), (3072, 64), (3584, 32)))
    gather_keys(kv, kv8.at[:, 0], kv16.at[:, 0], kvc)
    rows = []
    for j in range(GROUP):
        grad = gm[j]
        delta = jnp.sum(grad.astype(f32) * stat[0, j, :HD], axis=0, keepdims=True)
        both = jnp.concatenate(
            [stat[0, j, HD : HD + 1], delta, jnp.zeros((6, 512), f32)], axis=0
        )
        rows.append(both)
        ld[:, 512 * j : 512 * j + 512] = both
        ld[:, 4096 + 256 * j : 4352 + 256 * j] = both[:, :256]
        ld[:, 6144 + 128 * j : 6272 + 128 * j] = both[:, :128]
        tall = jnp.concatenate(
            [jnp.zeros((HD, 512), bf16), grad, jnp.zeros((32, 512), bf16)], axis=0
        ).T
        for r, at in enumerate(q_at):
            size = 512 >> r
            dor[at + size * j : at + size * j + size] = tall[:size]
        key = msg[j, :HD]
        kt[j // 2, :, 512 * (j % 2) : 512 * (j % 2) + 512] = key
        kt[4 + j // 4, :, 256 * (j % 4) : 256 * (j % 4) + 256] = key[:, :256]
        kt[6, :, 128 * j : 128 * j + 128] = key[:, :128]
    ld[:, 7168:7680] = jnp.concatenate([both[:, :64] for both in rows], axis=1)
    ld[:, 7680:7936] = jnp.concatenate([both[:, :32] for both in rows], axis=1)
    for i in range(2):
        kt[7 + i] = kvc[3072 + 1024 * i : 4096 + 1024 * i].T[:HD]

    def unit(source, q_from, keys, k_from, place, seg, count):
        width = 256 * count
        query = source[pl.ds(q_from, width)]
        grad = dor[pl.ds(place, width)]
        total = ld[0:1, pl.ds(place, width)]
        delta = ld[1:2, pl.ds(place, width)]
        sides = jnp.concatenate([grad, query], axis=0)
        size = 256
        dq = jnp.zeros((HD, width), f32)
        for c in range(1024 // size):
            key = keys[pl.ds(k_from + size * c, size)]
            prob = jnp.exp2(matmul(key, query, NT) * scale2 - total)
            slope = (prob * (matmul(key, grad, NT) - delta)).astype(bf16)
            both = jnp.concatenate([prob.astype(bf16), slope], axis=1)
            dkv[pl.ds(seg * 1024 + size * c, size)] = matmul(both, sides)
            dq = dq + matmul(kt[seg, :, size * c : size * c + size], slope)
        dqt[:, pl.ds(place, width)] = dq

    def first(u, _):
        at = pl.multiple_of(u * 1024, 1024)
        unit(q, at, kv, at, at, u, 4)
        return 0

    lax.fori_loop(0, 4, first, 0)

    def second(u, _):
        at = pl.multiple_of(u * 1024, 1024)
        unit(qc, at, kvc, at, at + 4096, u + 4, 4)
        return 0

    lax.fori_loop(0, 3, second, 0)
    unit(qc, 3072, kvc, 3072, 7168, 7, 2)
    unit(qc, 3584, kvc, 4096, 7680, 8, 1)
    for i in range(2):
        dkv8[i, 0] = dkv[7168 + 512 * i : 7680 + 512 * i].astype(bf16)
    for i in range(4):
        dkv16[i, 0] = dkv[8192 + 256 * i : 8448 + 256 * i].astype(bf16)
    lane = lax.broadcasted_iota(jnp.int32, (1, 512), 1)
    uses = jnp.where(
        lane < 32, 5.0, jnp.where(lane < 64, 4.0, jnp.where(lane < 128, 3.0, jnp.where(lane < 256, 2.0, 1.0)))
    )
    for j in range(GROUP):
        tall = dkv[512 * j : 512 * j + 512]
        tall = jnp.concatenate(
            [
                tall[:128] + dkv[4096 + 256 * j : 4224 + 256 * j] + dkv[6144 + 128 * j : 6272 + 128 * j],
                tall[128:256] + dkv[4224 + 256 * j : 4352 + 256 * j],
                tall[256:],
            ],
            axis=0,
        )
        wide = tall.T
        key = msg[j, :HD].astype(f32)
        value = msg[j, HD : 2 * HD].astype(f32)
        query = msg[j, 112:160].astype(f32)
        grad = gm[j].astype(f32)
        total = ld[0:1, 512 * j : 512 * j + 512]
        delta = ld[1:2, 512 * j : 512 * j + 512]
        dots = jnp.sum(query * key, axis=0, keepdims=True)
        dropped = msg[j, FLAG : FLAG + 1].astype(f32) != 0.0
        prob = jnp.where(
            dropped, uses * jnp.exp2(jnp.where(dropped, dots * scale2 - total, 0.0)), 0.0
        )
        slope = prob * (jnp.sum(grad * value, axis=0, keepdims=True) - delta)
        dq = dqt[:, 512 * j : 512 * j + 512] + slope * key
        second_part = dqt[:, 4096 + 256 * j : 4352 + 256 * j]
        third_part = dqt[:, 6144 + 128 * j : 6272 + 128 * j]
        fourth_part = dqt[:, 7168 + 64 * j : 7232 + 64 * j]
        fifth_part = dqt[:, 7680 + 32 * j : 7712 + 32 * j]
        fifth_part = jnp.concatenate([fifth_part, jnp.zeros((HD, 32), f32)], axis=1)
        fourth_part = jnp.concatenate([fourth_part + fifth_part, jnp.zeros((HD, 64), f32)], axis=1)
        third_part = jnp.concatenate([third_part + fourth_part, jnp.zeros((HD, 128), f32)], axis=1)
        second_part = jnp.concatenate([second_part + third_part, jnp.zeros((HD, 256), f32)], axis=1)
        pre[0, j, :HD] = (wide[:HD] + slope * query) * scale
        pre[0, j, HD : 2 * HD] = wide[HD : 2 * HD] + prob * grad
        pre[0, j, 2 * HD :] = (dq + second_part) * scale


def return_kernel(
    grp, pre, dkv8, dkv16, dq_ref, dk_ref, dv_ref,
    send, recv, got8, got16, send_sem, recv_sem, deep_send, deep_recv,
):
    linear, member, base = spot(grp)
    barrier, total = plane_barrier(grp, True)
    pl.semaphore_wait(barrier, total)
    plane = (send, recv, send_sem, recv_sem)
    layer = linear // GROUP % 4
    half = layer % 2
    copies = []
    for o in range(1, 4):
        other = (layer + o) % 4
        copies.append(
            pltpu.make_async_remote_copy(
                src_ref=dkv16.at[other],
                dst_ref=got16.at[4 - o],
                send_sem=deep_send.at[o],
                recv_sem=deep_recv.at[4 - o],
                device_id=device(linear + GROUP * (other - layer), grp),
                device_id_type=MESH,
            )
        )
    copies.append(
        pltpu.make_async_remote_copy(
            src_ref=dkv8.at[1 - half],
            dst_ref=got8.at[0],
            send_sem=deep_send.at[0],
            recv_sem=deep_recv.at[0],
            device_id=device(linear + GROUP - 2 * GROUP * half, grp),
            device_id_type=MESH,
        )
    )
    for copy in copies:
        copy.start()
    for copy in copies:
        copy.wait()
    row = lax.broadcasted_iota(jnp.int32, (96, 1), 0)
    factor = jnp.where(row < HD, scale, 1.0)
    for j in range(GROUP):
        for i in range(2):
            eight = dkv8[half, i, 64 * j : 64 * j + 64].astype(f32) + got8[
                0, i, 64 * j : 64 * j + 64
            ].astype(f32)
            sixteen = dkv16[layer, i, 32 * j : 32 * j + 32].astype(f32)
            for o in range(1, 4):
                sixteen = sixteen + got16[o, i, 32 * j : 32 * j + 32].astype(f32)
            more = jnp.concatenate(
                [eight[:32] + sixteen, eight[32:], jnp.zeros((64, LANES), f32)], axis=0
            ).T
            at = 144 * i
            first_part = pre[i, j, :96]
            send[j, at : at + 96] = jnp.concatenate(
                [first_part[:, :LANES] + more[:96] * factor, first_part[:, LANES:]], axis=1
            ).astype(bf16)
            send[j, at + 96 : at + 144] = pre[i, j, 96:].astype(bf16)
        plane_send(*plane, j, member, base, grp)
    for j in range(GROUP):
        plane_wait(*plane, j, member, base, grp)
    for n, out in enumerate((dk_ref, dv_ref, dq_ref)):

        def read(h, n=n):
            at = 144 * (h % 2) + HD * n
            return recv[h // 2, at : at + HD]

        out[...] = join_quads(read)
    for j in range(GROUP):
        plane_drain(*plane, j, member, base, grp)


def vmem():
    return pl.BlockSpec(memory_space=pltpu.VMEM)


def sems(n):
    return pltpu.SemaphoreType.DMA((n,))


def params(identity=None):
    if identity is None:
        return pltpu.CompilerParams(vmem_limit_bytes=58 << 20)
    return pltpu.CompilerParams(
        vmem_limit_bytes=58 << 20, collective_id=identity, has_side_effects=True
    )


def shape(dims, dtype):
    return jax.ShapeDtypeStruct(dims, dtype)


def attention_in(grp, slides, normed, weight, bias, flags):
    return pl.pallas_call(
        functools.partial(qkv_kernel, grp, slides),
        name="project_and_share",
        in_specs=[vmem()] * 4,
        out_specs=[vmem()] * 5,
        out_shape=[
            shape((GROUP, 2 * MSG, 512), bf16),
            shape((2, 4096, LANES), bf16),
            shape((2, 4096, LANES), bf16),
            shape((2, 2, 512, LANES), bf16),
            shape((4, 2, 256, LANES), bf16),
        ],
        scratch_shapes=[
            pltpu.VMEM((GROUP, 2 * MSG, 512), bf16),
            sems(GROUP),
            sems(GROUP),
            sems(4),
            sems(4),
        ],
        compiler_params=params(1),
    )(normed, weight, bias, flags)


def attention_forward(slides, q, kv, kv8, kv16):
    return pl.pallas_call(
        functools.partial(forward_kernel, slides),
        name="attention_forward",
        grid=(2,),
        in_specs=[
            pl.BlockSpec((1, 4096, LANES), lambda h: (h, 0, 0)),
            pl.BlockSpec((1, 4096, LANES), lambda h: (h, 0, 0)),
            pl.BlockSpec((2, 1, 512, LANES), lambda h: (0, h, 0, 0)),
            pl.BlockSpec((4, 1, 256, LANES), lambda h: (0, h, 0, 0)),
        ],
        out_specs=[
            pl.BlockSpec((GROUP, HD, 512), lambda h: (0, h, 0)),
            pl.BlockSpec((1, GROUP, 56, 512), lambda h: (h, 0, 0, 0)),
        ],
        out_shape=[shape((GROUP, 2 * HD, 512), bf16), shape((2, GROUP, 56, 512), f32)],
        scratch_shapes=[
            pltpu.VMEM((q_all, LANES), f32),
            pltpu.VMEM((q_all - 4096, LANES), bf16),
            pltpu.VMEM((k_all - 4096, LANES), bf16),
        ],
        compiler_params=params(),
    )(q, kv, kv8, kv16)


def attention_out(grp, om):
    return pl.pallas_call(
        functools.partial(merged_kernel, grp),
        name="share_merged",
        in_specs=[vmem()],
        out_specs=vmem(),
        out_shape=shape((512, 768), bf16),
        scratch_shapes=[pltpu.VMEM((GROUP, 2 * HD, 512), bf16), sems(GROUP), sems(GROUP)],
        compiler_params=params(2),
    )(om)


def gradient_in(grp, grad):
    return pl.pallas_call(
        functools.partial(spread_kernel, grp),
        name="share_gradient",
        in_specs=[vmem()],
        out_specs=vmem(),
        out_shape=shape((GROUP, 2 * HD, 512), bf16),
        scratch_shapes=[pltpu.VMEM((GROUP, 2 * HD, 512), bf16), sems(GROUP), sems(GROUP)],
        compiler_params=params(3),
    )(grad)


def attention_backward(q, kv, kv8, kv16, msg, gm, stat):
    return pl.pallas_call(
        backward_kernel,
        name="attention_backward",
        grid=(2,),
        in_specs=[
            pl.BlockSpec((1, 4096, LANES), lambda h: (h, 0, 0)),
            pl.BlockSpec((1, 4096, LANES), lambda h: (h, 0, 0)),
            pl.BlockSpec((2, 1, 512, LANES), lambda h: (0, h, 0, 0)),
            pl.BlockSpec((4, 1, 256, LANES), lambda h: (0, h, 0, 0)),
            pl.BlockSpec((GROUP, MSG, 512), lambda h: (0, h, 0)),
            pl.BlockSpec((GROUP, HD, 512), lambda h: (0, h, 0)),
            pl.BlockSpec((1, GROUP, 56, 512), lambda h: (h, 0, 0, 0)),
        ],
        out_specs=[
            pl.BlockSpec((1, GROUP, 144, 512), lambda h: (h, 0, 0, 0)),
            pl.BlockSpec((2, 1, 512, LANES), lambda h: (0, h, 0, 0)),
            pl.BlockSpec((4, 1, 256, LANES), lambda h: (0, h, 0, 0)),
        ],
        out_shape=[
            shape((2, GROUP, 144, 512), f32),
            shape((2, 2, 512, LANES), bf16),
            shape((4, 2, 256, LANES), bf16),
        ],
        scratch_shapes=[
            pltpu.VMEM((q_all - 4096, LANES), bf16),
            pltpu.VMEM((k_all - 4096, LANES), bf16),
            pltpu.VMEM((q_all, LANES), bf16),
            pltpu.VMEM((9, HD, 1024), bf16),
            pltpu.VMEM((8, q_all), f32),
            pltpu.VMEM((k_all, LANES), f32),
            pltpu.VMEM((HD, q_all), f32),
        ],
        compiler_params=params(),
    )(q, kv, kv8, kv16, msg, gm, stat)


def gradient_out(grp, pre, dkv8, dkv16):
    return pl.pallas_call(
        functools.partial(return_kernel, grp),
        name="return_gradients",
        in_specs=[vmem()] * 3,
        out_specs=[vmem()] * 3,
        out_shape=[shape((512, 768), bf16)] * 3,
        scratch_shapes=[
            pltpu.VMEM((GROUP, 288, 512), bf16),
            pltpu.VMEM((GROUP, 288, 512), bf16),
            pltpu.VMEM((1, 2, 512, LANES), bf16),
            pltpu.VMEM((4, 2, 256, LANES), bf16),
            sems(GROUP),
            sems(GROUP),
            sems(4),
            sems(4),
        ],
        compiler_params=params(4),
    )(pre, dkv8, dkv16)


def position_table(coordinates, width):
    quarter = width // 4
    frequency = jnp.exp(jnp.arange(quarter, dtype=jnp.float32) * (-math.log(10000.0) / quarter))
    column = coordinates[:, 0:1].astype(jnp.float32) * frequency[None, :]
    across = coordinates[:, 1:2].astype(jnp.float32) * frequency[None, :]
    return jnp.concatenate(
        [jnp.sin(column), jnp.cos(column), jnp.sin(across), jnp.cos(across)], axis=1
    )


def layer_norm(values, norm_gain, norm_shift):
    average = jnp.mean(values, axis=-1, keepdims=True)
    centred = values - average
    variance = jnp.mean(centred * centred, axis=-1, keepdims=True)
    return centred * lax.rsqrt(variance + epsilon) * norm_gain + norm_shift


def gelu_slope(values):
    return (
        0.5 * (1.0 + lax.erf(values * 0.7071067811865476))
        + values * jnp.exp(-0.5 * values * values) * 0.3989422804014327
    )


def product(left, right):
    return jnp.dot(left, right, preferred_element_type=jnp.float32)


def product_left(left, right):
    return jnp.einsum("rd,rf->df", left, right, preferred_element_type=jnp.float32)


def product_right(left, right):
    return jnp.einsum("rf,df->rd", left, right, preferred_element_type=jnp.float32)


def in_order(rows):
    split = rows.reshape((BLOCK, 16) + rows.shape[1:])
    return jnp.stack([split[:, b] for b in order]).reshape(rows.shape)


def back_order(rows):
    split = rows.reshape((16, BLOCK) + rows.shape[1:])
    return jnp.stack([split[b] for b in order], axis=1).reshape(rows.shape)


def body(
    tokens,
    coordinates,
    lengths,
    valid,
    first_gain,
    first_shift,
    query_weight,
    query_bias,
    key_weight,
    value_weight,
    value_bias,
    output_weight,
    output_bias,
    second_gain,
    second_shift,
    inner_weight,
    inner_bias,
    outer_weight,
    outer_bias,
    cotangent,
):
    rows, width = tokens.shape
    grp = lax.axis_size("grp")
    slides = lengths.shape[0]
    linear = lax.axis_index("seq") * grp + lax.axis_index("grp")
    start = linear * rows
    part = [
        lax.all_gather(w, "grp", axis=1, tiled=True)
        for w in (query_weight, key_weight, value_weight, output_weight, inner_weight, outer_weight)
    ]
    full_query, full_key, full_value, full_output, full_inner, full_outer = [
        lax.all_gather(w, "seq", axis=0, tiled=True) for w in part
    ]
    quads = [
        w.reshape(width, 4, 4, HD).transpose(1, 0, 2, 3) for w in (full_query, full_key, full_value)
    ]
    joint_weight = jnp.stack(quads, axis=3).reshape(4, width, 576)
    joint_bias = jnp.stack(
        [b.reshape(4, 4, HD) for b in (query_bias, jnp.zeros_like(query_bias), value_bias)], axis=2
    ).reshape(4, 1, 576)
    base = in_order(tokens + position_table(coordinates, width))
    cotangent = in_order(cotangent)
    places = in_order(start + jnp.arange(rows, dtype=jnp.int32))
    keep = in_order(valid)
    slide = jnp.sum((places[:, None] >= jnp.cumsum(lengths)).astype(jnp.int32), axis=-1)
    apart = slide[None, :] != jnp.arange(slides, dtype=jnp.int32)[:, None]
    flags = jnp.concatenate(
        [
            jnp.where(keep == 1, 0.0, -BIG)[None, :],
            jnp.where(apart, -BIG, 0.0),
            jnp.ones((1, rows), f32),
            jnp.zeros((14 - slides, rows), f32),
        ],
        axis=0,
    )
    normed, first_back = jax.vjp(layer_norm, base, first_gain, first_shift)
    normed_low = normed.astype(bf16)
    msg, q_rows, kv_rows, kv8, kv16 = attention_in(
        grp, slides, normed_low, joint_weight, joint_bias, flags
    )
    own, stat = attention_forward(slides, q_rows, kv_rows, kv8, kv16)
    merged_low = attention_out(grp, own)
    middle = base + product(merged_low, full_output) + output_bias
    normed_two, second_back = jax.vjp(layer_norm, middle, second_gain, second_shift)
    normed_two_low = normed_two.astype(jnp.bfloat16)
    inner = product(normed_two_low, full_inner) + inner_bias
    activated = jax.nn.gelu(inner, approximate=False).astype(jnp.bfloat16)
    output = middle + product(activated, full_outer) + outer_bias
    grad_outer = cotangent.astype(jnp.bfloat16)
    outer_weight_grad = product_left(activated, grad_outer)
    outer_bias_grad = jnp.sum(grad_outer.astype(jnp.float32), axis=0)
    grad_inner = (product_right(grad_outer, full_outer) * gelu_slope(inner)).astype(jnp.bfloat16)
    inner_weight_grad = product_left(normed_two_low, grad_inner)
    inner_bias_grad = jnp.sum(grad_inner.astype(jnp.float32), axis=0)
    grad_middle_part, second_gain_grad, second_shift_grad = second_back(
        product_right(grad_inner, full_inner)
    )
    grad_middle = cotangent + grad_middle_part
    grad_attended = grad_middle.astype(jnp.bfloat16)
    output_weight_grad = product_left(merged_low, grad_attended)
    output_bias_grad = jnp.sum(grad_attended.astype(jnp.float32), axis=0)
    grad_merged = product_right(grad_attended, full_output).astype(bf16)
    shared = gradient_in(grp, grad_merged)
    pre, dkv8, dkv16 = attention_backward(q_rows, kv_rows, kv8, kv16, msg, shared, stat)
    query_low, key_low, value_low = gradient_out(grp, pre, dkv8, dkv16)
    query_weight_grad = product_left(normed_low, query_low)
    key_weight_grad = product_left(normed_low, key_low)
    value_weight_grad = product_left(normed_low, value_low)
    query_bias_grad = jnp.sum(query_low.astype(jnp.float32), axis=0)
    value_bias_grad = jnp.sum(value_low.astype(jnp.float32), axis=0)
    grad_normed = (
        product_right(query_low, full_query)
        + product_right(key_low, full_key)
        + product_right(value_low, full_value)
    )
    grad_base_part, first_gain_grad, first_shift_grad = first_back(grad_normed)
    token_grad = grad_middle + grad_base_part
    sum_query, sum_key, sum_value, sum_output, sum_inner, sum_outer = (
        lax.psum_scatter(query_weight_grad, "grp", scatter_dimension=1, tiled=True),
        lax.psum_scatter(key_weight_grad, "grp", scatter_dimension=1, tiled=True),
        lax.psum_scatter(value_weight_grad, "grp", scatter_dimension=1, tiled=True),
        lax.psum_scatter(output_weight_grad, "grp", scatter_dimension=1, tiled=True),
        lax.psum_scatter(inner_weight_grad, "grp", scatter_dimension=1, tiled=True),
        lax.psum_scatter(outer_weight_grad, "grp", scatter_dimension=1, tiled=True),
    )
    sum_query, sum_key, sum_value, sum_output, sum_inner, sum_outer = (
        lax.psum_scatter(sum_query, "seq", scatter_dimension=0, tiled=True),
        lax.psum_scatter(sum_key, "seq", scatter_dimension=0, tiled=True),
        lax.psum_scatter(sum_value, "seq", scatter_dimension=0, tiled=True),
        lax.psum_scatter(sum_output, "seq", scatter_dimension=0, tiled=True),
        lax.psum_scatter(sum_inner, "seq", scatter_dimension=0, tiled=True),
        lax.psum_scatter(sum_outer, "seq", scatter_dimension=0, tiled=True),
    )
    small = lax.psum(
        (
            first_gain_grad,
            first_shift_grad,
            query_bias_grad,
            value_bias_grad,
            output_bias_grad,
            second_gain_grad,
            second_shift_grad,
            inner_bias_grad,
            outer_bias_grad,
        ),
        ("seq", "grp"),
    )
    return (
        back_order(output),
        back_order(token_grad),
        small[0],
        small[1],
        sum_query,
        small[2],
        sum_key,
        sum_value,
        small[3],
        sum_output,
        small[4],
        small[5],
        small[6],
        sum_inner,
        small[7],
        sum_outer,
        small[8],
    )


def solution(mesh):
    placed = (
        P(("seq", "grp"), None),
        P(("seq", "grp"), None),
        P(),
        P(("seq", "grp")),
        P(),
        P(),
        P("seq", "grp"),
        P(),
        P("seq", "grp"),
        P("seq", "grp"),
        P(),
        P("seq", "grp"),
        P(),
        P(),
        P(),
        P("seq", "grp"),
        P(),
        P("seq", "grp"),
        P(),
        P(("seq", "grp"), None),
    )
    return jax.shard_map(
        body,
        mesh=mesh,
        in_specs=placed,
        out_specs=(
            P(("seq", "grp"), None),
            P(("seq", "grp"), None),
            P(),
            P(),
            P("seq", "grp"),
            P(),
            P("seq", "grp"),
            P("seq", "grp"),
            P(),
            P("seq", "grp"),
            P(),
            P(),
            P(),
            P("seq", "grp"),
            P(),
            P("seq", "grp"),
            P(),
        ),
        check_vma=False,
    )
```

time: 2370 us -> 1220 us (0.51)
  local copies, waits for them, and re-layouts: 646 us -> 69.2 us
  matrix products: 611 us -> 75.4 us
  Pallas kernels: 0 us -> 257 us
  other arithmetic: 245 us -> 17.1 us
  starting transfers between devices: 58.9 us -> 1.38 us
    dot_general x110 -> x0, matrix products: 532 us -> none  [the longest x16 141 us: block_backward(): jnp.einsum('hij,hix->hjx', grad_scores, query_block, preferred_element_ty...]
    broadcast_in_dim x162 -> x1, local copies, waits for them, and re-layouts: 325 us -> 0.01 us  [body(): jnp.zeros((14 - slides, rows), f32)]
    pallas_call x0 -> x6, Pallas kernels: none -> 257 us  [the longest x1 55.8 us: attention_forward(): pl.pallas_call(functools.partial(forward_kernel, slides), name='attention...]
    another operation x42 -> x12, local copies, waits for them, and re-layouts: 120 us -> 6.67 us  [the longest x4 6.29 us: back_order(): return jnp.stack([split[b] for b in order], axis=1).reshape(rows.shape)]
    ppermute x75 -> x0, waiting for transfers between devices: 108 us -> none  [swapped(): return lax.ppermute(value, axis, pairs)]
    all_gather x6, waiting for transfers between devices: 0.06 us -> 98.6 us  [body(): lax.all_gather(w, 'seq', axis=0, tiled=True)]
    select_n x87 -> x2, other arithmetic: 86.2 us -> 0.01 us  [the longest x1 0.01 us: body(): jnp.where(keep == 1, 0.0, -BIG)[None, :]]
    ppermute x75 -> x0, starting transfers between devices: 57.8 us -> none  [swapped(): return lax.ppermute(value, axis, pairs)]
  transfers between devices with their start and end apart: 93 -> 18, of which waited for: 26 -> 15; matrix products, arithmetic and copies ran while one was open for 44% -> 11% of each run, Pallas kernels for 0% -> 12%
where the time goes in v1:
time: 1220 us; the launch traced here: 1210 us
  waiting for transfers between devices  698 us (57%)
  Pallas kernels  257 us (21%)
  blocking collectives  81.1 us (7%)
  matrix products  75.4 us (6%)
  local copies, waits for them, and re-layouts  69.2 us (6%)
  other arithmetic  17.1 us (1%)
  between operations  15.6 us (1%)
    unnamed x22, waiting for transfers between devices  209 us
    all_gather x6, waiting for transfers between devices, body(): lax.all_gather(w, 'seq', axis=0, tiled=True)  98.6 us
    reduce_scatter x1, waiting for transfers between devices, body(): lax.psum_scatter(inner_weight_grad, 'grp', scatter_dimension=1, tiled=True)  73.1 us
    reduce_scatter x1, waiting for transfers between devices, body(): lax.psum_scatter(sum_outer, 'seq', scatter_dimension=0, tiled=True)  72.1 us
    reduce_scatter x1, waiting for transfers between devices, body(): lax.psum_scatter(sum_inner, 'seq', scatter_dimension=0, tiled=True)  72 us
    reduce_scatter x1, waiting for transfers between devices, body(): lax.psum_scatter(outer_weight_grad, 'grp', scatter_dimension=1, tiled=True)  64.9 us
    pallas_call x1, Pallas kernels, attention_forward(): pl.pallas_call(functools.partial(forward_kernel, slides), name='attention...  55.8 us
    pallas_call x1, Pallas kernels, attention_in(): pl.pallas_call(functools.partial(qkv_kernel, grp, slides), name='project_...  50.8 us
  transfers between devices with their start and end apart: 18, of which 15 were waited for; matrix products, arithmetic and copies ran while one was open for 11% of the time, Pallas kernels for 12%

profile of v1, /device:TPU:0, one launch (start us, length us, event | category | flops | bytes accessed | tf_op | source)
XLA Modules:
  0.0 1214.6 jit_solution(18092008987974226377)
XLA Ops:
  8.2 7.0 all_gather.36
  17.0 5.6 all_gather.38
  23.6 5.6 all_gather.40
  30.2 5.6 all_gather.42
  36.6 8.2 all_gather.44
  44.9 8.2 all_gather.46
  53.5 3.7 multiply_sine_fusion.1
  80.2 2.4 copy.275
  82.6 18.7 %all-gather.9.cloned.1.call-done = bf16[768,768]{1,0:T(8,128)(2,1)} async-done(((bf16[96,768]{1,0:T(8,128)(2,1)}), bf16[768,768]{1,0:T(8,128)(2,1)}) %all-gather.9.cloned.1.call-update) | async-done | bytes 1179664 | tf_op jit(solution)/shard_map/all_gather | solution.py:802
  101.3 2.4 copy.278
  103.6 40.2 %all-gather.11.cloned.1.call-done = bf16[768,768]{1,0:T(8,128)(2,1)} async-done(((bf16[96,768]{1,0:T(8,128)(2,1)}), bf16[768,768]{1,0:T(8,128)(2,1)}) %all-gather.11.cloned.1.call-update) | async-done | bytes 1179664 | tf_op jit(solution)/shard_map/all_gather | solution.py:802
  143.9 2.4 copy.281
  146.2 3.5 pad_maximum_fusion
  149.7 5.9 copy.282.w_ref
  155.7 50.8 %project_and_share.1 = (bf16[8,320,512]{2,1,0:T(8,128)(2,1)}, bf16[2,4096,128]{2,1,0:T(8,128)(2,1)}, bf16[2,4096,128]{2,1,0:T(8,128)(2,1)}, bf16[2,2,512,128]{3,2,1,0:T(8,128)(2,1)}, bf16[4,2,256,128]{3,2,1,0:T(8,128)(2,1)}) custom-call(bf16[512,768]{1,0:T(8,128)(2,1)} %add_convert_fusion.1.n_ref, bf16[4,768,576]{2,1,0:T(8,128)(2,1)} %copy.282.w_ref, ...), custom_call_target="tpu_custom_call" | custom-call | tf_op jit(solution)/shard_map/project_and_share/pallas_call | solution.py:594
  206.5 55.8 %attention_forward.1 = (bf16[8,96,512]{2,1,0:T(8,128)(2,1)}, f32[2,8,56,512]{3,2,1,0:T(8,128)}) custom-call(bf16[2,4096,128]{2,1,0:T(8,128)(2,1)} %get-tuple-element.30.q_ref, bf16[2,4096,128]{2,1,0:T(8,128)(2,1)} %get-tuple-element.31.kv_ref, bf16[2,2,512,128]{3,2,1,0:T(8,128)(2,1)} %get-tuple-element.32.kv8, bf16[4,2,256,128]{3,2,1,0:T(8,128)(2,1)} %get-tuple-element.33.kv16), custom_call_target="tpu_custom_call" | custom-call | tf_op jit(solution)/shard_map/attention_forward/pallas_call | solution.py:618
  262.3 38.9 %share_merged.1 = bf16[512,768]{1,0:T(8,128)(2,1)} custom-call(bf16[8,96,512]{2,1,0:T(8,128)(2,1)} %get-tuple-element.34.om), custom_call_target="tpu_custom_call" | custom-call | tf_op jit(solution)/shard_map/share_merged/pallas_call | solution.py:643
  301.3 2.4 fusion.27
  305.2 20.2 %fusion.2 = (bf16[512,3072]{1,0:T(8,128)(2,1)}, f32[512,3072]{1,0:T(8,128)}) fusion(f32[3072]{0:T(1024)S(1)} %copy-done.56, bf16[768,3072]{1,0:T(8,128)(2,1)} %all-gather.15.cloned.1.call-done, f32[512,768]{1,0:T(8,128)} %copy-done.6, f32[768]{0:T(1024)S(1)} %copy-done.58, f32[768]{0:T(1024)S(1)} %copy-done.50, f32[512]{0:T(512)S(1)} %fusion.19, ...), kind=kOutput, calls=%fused_computation.4 | convolution fusion | flops 2521694208 | bytes 15751168 | tf_op jit(solution)/shard_map/dot_general | solution.py:749
  325.4 39.6 %all-gather.17.cloned.1.call-done = bf16[3072,768]{0,1:T(8,128)(2,1)} async-done(((bf16[384,768]{0,1:T(8,128)(2,1)}), bf16[3072,768]{0,1:T(8,128)(2,1)}) %all-gather.17.cloned.1.call-update) | async-done | bytes 4718608 | tf_op jit(solution)/shard_map/all_gather | solution.py:802
  365.1 8.2 convert_reduce_fusion
  373.2 3.5 multiply_reduce_fusion
  381.2 13.9 %share_gradient.1.gm = bf16[8,96,512]{2,1,0:T(8,128)(2,1)} custom-call(bf16[512,768]{1,0:T(8,128)(2,1)} %convolution_convert_fusion.rows_ref), custom_call_target="tpu_custom_call" | custom-call | tf_op jit(solution)/shard_map/share_gradient/pallas_call | solution.py:655
  395.1 49.9 %attention_backward.1 = (f32[2,8,144,512]{3,2,1,0:T(8,128)}, bf16[2,2,512,128]{3,2,1,0:T(8,128)(2,1)}, bf16[4,2,256,128]{3,2,1,0:T(8,128)(2,1)}) custom-call(bf16[2,4096,128]{2,1,0:T(8,128)(2,1)} %get-tuple-element.30.q_ref, bf16[2,4096,128]{2,1,0:T(8,128)(2,1)} %get-tuple-element.31.kv_ref, bf16[2,2,512,128]{3,2,1,0:T(8,128)(2,1)} %get-tuple-element.32.kv8, ...), custom_call_target="tpu_custom_call" | custom-call | tf_op jit(solution)/shard_map/attention_backward/pallas_call | solution.py:667
  445.0 47.6 %return_gradients.1 = (bf16[512,768]{1,0:T(8,128)(2,1)}, bf16[512,768]{1,0:T(8,128)(2,1)}, bf16[512,768]{1,0:T(8,128)(2,1)}) custom-call(f32[2,8,144,512]{3,2,1,0:T(8,128)} %get-tuple-element.37.pre, bf16[2,2,512,128]{3,2,1,0:T(8,128)(2,1)} %get-tuple-element.38.dkv8, bf16[4,2,256,128]{3,2,1,0:T(8,128)(2,1)} %get-tuple-element.39.dkv16), custom_call_target="tpu_custom_call" | custom-call | tf_op jit(solution)/shard_map/return_gradients/pallas_call | solution.py:704
  492.7 3.3 fusion.32
  504.4 2.3 fusion.33
  508.1 7.2 fusion.20
  516.5 7.0 fusion.34
  523.6 7.8 reduce-scatter.25.cloned.1.call-done
  531.3 2.2 copy.312
  533.7 33.5 %reduce-scatter.21.cloned.1.call-done = f32[768,192]{0,1:T(8,128)} async-done(((f32[768,768]{0,1:T(8,128)}), f32[768,192]{0,1:T(8,128)}) %reduce-scatter.21.cloned.1.call-update) | async-done | bytes 589840 | tf_op jit(solution)/shard_map/reduce_scatter | solution.py:869
  569.4 33.3 %reduce-scatter.23.cloned.1.call-done = f32[768,192]{0,1:T(8,128)} async-done(((f32[768,768]{0,1:T(8,128)}), f32[768,192]{0,1:T(8,128)}) %reduce-scatter.23.cloned.1.call-update) | async-done | bytes 589840 | tf_op jit(solution)/shard_map/reduce_scatter | solution.py:870
  602.8 2.2 copy.310
  605.1 33.3 %reduce-scatter.27.cloned.1.call-done = f32[768,192]{0,1:T(8,128)} async-done(((f32[768,768]{0,1:T(8,128)}), f32[768,192]{0,1:T(8,128)}) %reduce-scatter.27.cloned.1.call-update) | async-done | bytes 589840 | tf_op jit(solution)/shard_map/reduce_scatter | solution.py:872
  640.7 3.6 fusion.29
  646.3 73.1 %reduce-scatter.29.cloned.1.call-done = f32[768,768]{1,0:T(8,128)} async-done(((f32[768,3072]{1,0:T(8,128)}), f32[768,768]{1,0:T(8,128)}) %reduce-scatter.29.cloned.1.call-update) | async-done | bytes 2359312 | tf_op jit(solution)/shard_map/reduce_scatter | solution.py:873
  719.8 3.8 multiply_reduce_fusion.1
  735.5 64.9 %reduce-scatter.33.cloned.1.call-done = f32[3072,192]{0,1:T(8,128)} async-done(((f32[3072,768]{0,1:T(8,128)}), f32[3072,192]{0,1:T(8,128)}) %reduce-scatter.33.cloned.1.call-update) | async-done | bytes 2359312 | tf_op jit(solution)/shard_map/reduce_scatter | solution.py:874
  801.0 3.6 copy.303
  804.6 5.9 add_add_fusion.4
  813.7 40.8 %all-reduce = (f32[768]{0:T(1024)}, f32[768]{0:T(1024)}, f32[768]{0:T(1024)}, f32[768]{0:T(1024)}, f32[768]{0:T(1024)}, /*index=5*/f32[768]{0:T(1024)}, f32[768]{0:T(1024)}, f32[3072]{0:T(1024)}, f32[768]{0:T(1024)}) all-reduce(f32[768]{0:T(1024)S(1)} %copy-done.39, ...), channel_id=1, replica_groups=mesh['seq'=8,'grp'=4] {'seq','grp'}, use_global_device_ids=true, to_apply=%region_11.12 | all-reduce | flops 9216 | bytes 73728 | tf_op jit(solution)/shard_map/psum | solution.py:884
  854.5 12.3 %reduce-scatter.41.cloned.1.call-done = f32[96,192]{1,0:T(8,128)} async-done(((f32[768,192]{1,0:T(8,128)}), f32[96,192]{1,0:T(8,128)}) %reduce-scatter.41.cloned.1.call-update) | async-done | bytes 73744
  866.8 65.6 %reduce-scatter.37.cloned.1.call-done = f32[96,192]{1,0:T(8,128)} async-done(((f32[768,192]{1,0:T(8,128)}), f32[96,192]{1,0:T(8,128)}) %reduce-scatter.37.cloned.1.call-update) | async-done | bytes 73744
  932.5 65.3 %reduce-scatter.39.cloned.1.call-done = f32[96,192]{1,0:T(8,128)} async-done(((f32[768,192]{1,0:T(8,128)}), f32[96,192]{1,0:T(8,128)}) %reduce-scatter.39.cloned.1.call-update) | async-done | bytes 73744
  997.8 65.6 %reduce-scatter.43.cloned.1.call-done = f32[96,192]{1,0:T(8,128)} async-done(((f32[768,192]{1,0:T(8,128)}), f32[96,192]{1,0:T(8,128)}) %reduce-scatter.43.cloned.1.call-update) | async-done | bytes 73744
  1063.3 72.0 %reduce-scatter.31.cloned.1.call-done = f32[96,768]{1,0:T(8,128)} async-done(((f32[768,768]{1,0:T(8,128)}), f32[96,768]{1,0:T(8,128)}) %reduce-scatter.31.cloned.1.call-update) | async-done | bytes 294928 | tf_op jit(solution)/shard_map/reduce_scatter | solution.py:881
  1135.3 72.1 %reduce-scatter.35.cloned.1.call-done = f32[384,192]{0,1:T(8,128)} async-done(((f32[3072,192]{0,1:T(8,128)}), f32[384,192]{0,1:T(8,128)}) %reduce-scatter.35.cloned.1.call-update) | async-done | bytes 294928 | tf_op jit(solution)/shard_map/reduce_scatter | solution.py:882
  (287 shorter events, 67.8 us)
Async XLA Ops:
  7.2 16.3 %copy-start.27 = (bf16[96,192]{1,0:T(8,128)(2,1)S(1)}, bf16[96,192]{1,0:T(8,128)(2,1)}, u32[]{:S(2)}) copy-start(bf16[96,192]{1,0:T(8,128)(2,1)} %param.29) | copy-start | bytes 110596
  7.2 22.8 %copy-start.28 = (bf16[96,192]{1,0:T(8,128)(2,1)S(1)}, bf16[96,192]{1,0:T(8,128)(2,1)}, u32[]{:S(2)}) copy-start(bf16[96,192]{1,0:T(8,128)(2,1)} %param.31) | copy-start | bytes 110596
  7.2 73.0 %all-gather.7.cloned.1.call-start = ((), (), s32[]{:S(2)}) async-start(), calls=%async_computation.12 | async-start | bytes 1327104 | tf_op jit(solution)/shard_map/all_gather | solution.py:802
  8.2 28.5 %copy-start.25 = (bf16[96,768]{1,0:T(8,128)(2,1)S(1)}, bf16[96,768]{1,0:T(8,128)(2,1)}, u32[]{:S(2)}) copy-start(bf16[96,768]{1,0:T(8,128)(2,1)} %param.35) | copy-start | bytes 442372
  16.0 85.3 %all-gather.9.cloned.1.call-start = ((), (), s32[]{:S(2)}) async-start(), calls=%async_computation.13 | async-start | bytes 1327104 | tf_op jit(solution)/shard_map/all_gather | solution.py:802
  23.4 21.6 %copy-start.26 = (bf16[384,192]{0,1:T(8,128)(2,1)S(1)}, bf16[384,192]{0,1:T(8,128)(2,1)}, u32[]{:S(2)}) copy-start(bf16[384,192]{0,1:T(8,128)(2,1)} %param.37) | copy-start | bytes 442372
  23.4 120.5 %all-gather.11.cloned.1.call-start = ((), (), s32[]{:S(2)}) async-start(), calls=%async_computation.14 | async-start | bytes 1327104 | tf_op jit(solution)/shard_map/all_gather | solution.py:802
  30.0 271.3 %all-gather.13.cloned.1.call-start = ((), (), s32[]{:S(2)}) async-start(), calls=%async_computation.15 | async-start | bytes 1327104 | tf_op jit(solution)/shard_map/all_gather | solution.py:802
  35.8 17.7 %copy-start.47 = (s32[512,2]{0,1:T(2,128)S(1)}, s32[512,2]{0,1:T(2,128)}, u32[]{:S(2)}) copy-start(s32[512,2]{0,1:T(2,128)} %param.21) | copy-start | bytes 12292
  36.6 268.6 %all-gather.15.cloned.1.call-start = ((), (), s32[]{:S(2)}) async-start(), calls=%async_computation.16 | async-start | bytes 5308416 | tf_op jit(solution)/shard_map/all_gather | solution.py:802
  44.9 12.3 %copy-start.18 = (f32[512,768]{1,0:T(8,128)S(1)}, f32[512,768]{1,0:T(8,128)}, u32[]{:S(2)}) copy-start(f32[512,768]{1,0:T(8,128)} %param.20) | copy-start | bytes 4718596
  44.9 320.2 %all-gather.17.cloned.1.call-start = ((), (), s32[]{:S(2)}) async-start(), calls=%async_computation.17 | async-start | bytes 5308416 | tf_op jit(solution)/shard_map/all_gather | solution.py:802
  53.2 478.1 %reduce-scatter.25.cloned.1.call-start = ((), (), s32[]{:S(2)}) async-start(), calls=%async_computation.20 | async-start | bytes 2949120 | tf_op jit(solution)/shard_map/reduce_scatter | solution.py:871
  59.3 3.7 copy-start.45
  59.3 3.8 copy-start.46
  59.3 4.7 copy-start.51
  59.4 6.0 copy-start.17
  67.4 10.9 copy-start.36
  67.4 11.6 copy-start.33
  68.2 8.0 copy-start.24
  68.2 8.0 copy-start.23
  68.2 8.1 copy-start.22
  76.4 300.9 %copy-start.1 = (f32[16,32,768]{2,1,0:T(8,128)}, f32[16,32,768]{2,1,0:T(8,128)S(1)}, u32[]{:S(2)}) copy-start(f32[16,32,768]{2,1,0:T(8,128)S(1)} %constant_dynamic-update-slice_fusion.32) | copy-start | bytes 4718596
  262.3 39.0 %copy-start.57 = (f32[768]{0:T(1024)S(1)}, f32[768]{0:T(1024)}, u32[]{:S(2)}) copy-start(f32[768]{0:T(1024)} %param.32) | copy-start | bytes 9220
  365.1 8.2 copy-start.7
  365.1 8.2 copy-start.54
  445.0 47.7 %copy-start = (bf16[512,768]{1,0:T(8,128)(2,1)S(1)}, bf16[512,768]{1,0:T(8,128)(2,1)}, u32[]{:S(2)}) copy-start(bf16[512,768]{1,0:T(8,128)(2,1)} %add_convert_fusion.1.n_ref) | copy-start | bytes 2359300
  496.0 71.1 %reduce-scatter.21.cloned.1.call-start = ((), (), s32[]{:S(2)}) async-start(), calls=%async_computation.18 | async-start | bytes 2949120 | tf_op jit(solution)/shard_map/reduce_scatter | solution.py:869
  499.4 103.4 %reduce-scatter.23.cloned.1.call-start = ((), (), s32[]{:S(2)}) async-start(), calls=%async_computation.19 | async-start | bytes 2949120 | tf_op jit(solution)/shard_map/reduce_scatter | solution.py:870
  502.7 135.7 %reduce-scatter.27.cloned.1.call-start = ((), (), s32[]{:S(2)}) async-start(), calls=%async_computation.21 | async-start | bytes 2949120 | tf_op jit(solution)/shard_map/reduce_scatter | solution.py:872
  506.7 212.8 %reduce-scatter.29.cloned.1.call-start = ((), (), s32[]{:S(2)}) async-start(), calls=%async_computation.22 | async-start | bytes 11796480 | tf_op jit(solution)/shard_map/reduce_scatter | solution.py:873
  515.3 285.0 %reduce-scatter.33.cloned.1.call-start = ((), (), s32[]{:S(2)}) async-start(), calls=%async_computation.24 | async-start | bytes 11796480 | tf_op jit(solution)/shard_map/reduce_scatter | solution.py:874
  523.5 343.3 %reduce-scatter.41.cloned.1.call-start = ((), (), s32[]{:S(2)}) async-start(), calls=%async_computation.28 | async-start | bytes 884736
  533.6 398.8 %reduce-scatter.37.cloned.1.call-start = ((), (), s32[]{:S(2)}) async-start(), calls=%async_computation.26 | async-start | bytes 884736
  569.4 428.4 %reduce-scatter.39.cloned.1.call-start = ((), (), s32[]{:S(2)}) async-start(), calls=%async_computation.27 | async-start | bytes 884736
  605.0 458.3 %reduce-scatter.43.cloned.1.call-start = ((), (), s32[]{:S(2)}) async-start(), calls=%async_computation.29 | async-start | bytes 884736
  640.7 3.7 copy-start.13
  640.7 3.7 copy-start.19
  640.7 494.6 %reduce-scatter.31.cloned.1.call-start = ((), (), s32[]{:S(2)}) async-start(), calls=%async_computation.23 | async-start | bytes 2654208 | tf_op jit(solution)/shard_map/reduce_scatter | solution.py:881
  646.3 73.4 %copy-start.5 = (bf16[512,768]{1,0:T(8,128)(2,1)S(1)}, bf16[512,768]{1,0:T(8,128)(2,1)}, u32[]{:S(2)}) copy-start(bf16[512,768]{1,0:T(8,128)(2,1)} %get-tuple-element.42) | copy-start | bytes 2359300
  646.3 73.5 %copy-start.11 = (bf16[768,768]{1,0:T(8,128)(2,1)S(1)}, bf16[768,768]{1,0:T(8,128)(2,1)}, u32[]{:S(2)}) copy-start(bf16[768,768]{1,0:T(8,128)(2,1)} %all-gather.11.cloned.1.call-done) | copy-start | bytes 3538948
  646.3 73.5 %copy-start.30 = (f32[768]{0:T(1024)S(1)}, f32[768]{0:T(1024)}, u32[]{:S(2)}) copy-start(f32[768]{0:T(1024)} %param.24) | copy-start | bytes 9220
  646.3 73.5 %copy-start.32 = (f32[512]{0:T(512)S(1)}, f32[512]{0:T(512)}, u32[]{:S(2)}) copy-start(f32[512]{0:T(512)} %div.39) | copy-start | bytes 6148
  646.3 73.5 %copy-start.34 = (f32[512]{0:T(512)S(1)}, f32[512]{0:T(512)}, u32[]{:S(2)}) copy-start(f32[512]{0:T(512)} %copy-done.33) | copy-start | bytes 6148
  719.5 488.0 %reduce-scatter.35.cloned.1.call-start = ((), (), s32[]{:S(2)}) async-start(), calls=%async_computation.25 | async-start | bytes 2654208 | tf_op jit(solution)/shard_map/reduce_scatter | solution.py:882
  719.8 3.8 copy-start.37
  801.0 3.6 copy-start.9
  801.0 3.6 copy-start.59
  (31 other events, 47.2 us)
Sparse Core Ops, SparseCore 0:
  16.1 42.4 all-gather.6
  61.4 39.8 all-gather.8
  104.0 39.8 all-gather.10
  145.9 51.6 all-gather.12
  199.6 78.2 all-gather.14
  279.8 85.2 all-gather.16
  496.2 35.1 reduce-scatter.24
  534.0 33.0 reduce-scatter.20
  569.7 33.0 reduce-scatter.22
  605.3 33.0 reduce-scatter.26
  641.0 78.3 reduce-scatter.28
  721.9 78.4 reduce-scatter.32
  804.2 62.5 reduce-scatter.40
  870.9 61.5 reduce-scatter.36
  936.2 61.5 reduce-scatter.38
  1001.8 61.4 reduce-scatter.42
  1067.2 68.0 reduce-scatter.30
  1139.2 68.1 reduce-scatter.34

commit v2 on v1

--- a/solution.py
+++ b/solution.py
@@ -151,7 +151,7 @@
     barrier, total = plane_barrier(grp, True)
     plane = (send, msg, send_sem, recv_sem)
     for quad in range(4):
-        part = matmul(n_ref[...], w_ref[quad]) + b_ref[quad]
+        part = matmul(n_ref[...], pick(w_ref, quad)) + b_ref[quad]
         wide = swap_blocks(part.astype(bf16), quad).T
         flags = f_ref[...]
         flags = jnp.concatenate(
@@ -501,9 +501,10 @@
 
 
 def return_kernel(
-    grp, pre, dkv8, dkv16, dq_ref, dk_ref, dv_ref,
-    send, recv, got8, got16, send_sem, recv_sem, deep_send, deep_recv,
+    grp, pre, dkv8, dkv16, *refs,
 ):
+    outs, sums_ref = refs[:4], refs[4]
+    send, recv, got8, got16, send_sem, recv_sem, deep_send, deep_recv = refs[5:]
     linear, member, base = spot(grp)
     barrier, total = plane_barrier(grp, True)
     pl.semaphore_wait(barrier, total)
@@ -559,15 +560,30 @@
         plane_send(*plane, j, member, base, grp)
     for j in range(GROUP):
         plane_wait(*plane, j, member, base, grp)
-    for n, out in enumerate((dk_ref, dv_ref, dq_ref)):
-
-        def read(h, n=n):
-            at = 144 * (h % 2) + HD * n
-            return recv[h // 2, at : at + HD]
-
-        out[...] = join_quads(read)
+    for quad, out in enumerate(outs):
+        parts = []
+        for inner in range(4):
+            head = 4 * quad + inner
+            block = recv[head // 2, 144 * (head % 2) : 144 * (head % 2) + 144]
+            block = jnp.concatenate([block[96:], block[:96]], axis=0)
+            parts.append(swap_chunks(block, head))
+        rows = swap_blocks(jnp.concatenate(parts, axis=0).T, quad)
+        out[...] = rows
+        sums = column_sum(rows.astype(f32))
+        sums_ref[quad] = sums
     for j in range(GROUP):
         plane_drain(*plane, j, member, base, grp)
+
+
+def pick(ref, g):
+    both = jnp.stack([ref[:, g], ref[:, g + 4]], axis=1)
+    return both.reshape(768, ref.shape[3])
+
+
+def put(ref, g, value):
+    value = value.reshape(4, 2, 96, ref.shape[3])
+    ref[:, g] = value[:, 0]
+    ref[:, g + 4] = value[:, 1]
 
 
 def vmem():
@@ -705,8 +721,8 @@
         functools.partial(return_kernel, grp),
         name="return_gradients",
         in_specs=[vmem()] * 3,
-        out_specs=[vmem()] * 3,
-        out_shape=[shape((512, 768), bf16)] * 3,
+        out_specs=[vmem()] * 5,
+        out_shape=[shape((512, 576), bf16)] * 4 + [shape((4, 1, 576), f32)],
         scratch_shapes=[
             pltpu.VMEM((GROUP, 288, 512), bf16),
             pltpu.VMEM((GROUP, 288, 512), bf16),
@@ -721,6 +737,447 @@
     )(pre, dkv8, dkv16)
 
 
+def norm_parts(values):
+    average = jnp.mean(values, axis=-1, keepdims=True)
+    centred = values - average
+    variance = jnp.mean(centred * centred, axis=-1, keepdims=True)
+    inverse = lax.rsqrt(variance + epsilon)
+    return centred * inverse, inverse
+
+
+def norm_backward(hat, inverse, gain, grad):
+    scaled = grad * gain
+    first = jnp.mean(scaled, axis=-1, keepdims=True)
+    second = jnp.mean(scaled * hat, axis=-1, keepdims=True)
+    return (scaled - first - hat * second) * inverse
+
+
+def column_sum(values):
+    return jnp.sum(values, axis=0, keepdims=True)
+
+
+def dense_kernel(
+    merged, base, cot, wo, wi, wt, out_bias, gain, shift, in_bias, last_bias,
+    out, grad_middle, grad_merged, wo_grad, wi_grad, wt_grad, small, small_in,
+    full, middle, hat, low, low_t, cot_low, cot_t, grad_low,
+):
+    for g in range(0, 4, 2):
+        pair = [pick(wo, g + i) for i in range(2)]
+        full[:, 192 * g : 192 * g + 384] = jnp.concatenate(pair, axis=1)
+    middle[...] = base[...] + matmul(merged[...], full[...]) + out_bias[...]
+    normal, inverse = norm_parts(middle[...])
+    hat[...] = normal
+    low[...] = (normal * gain[...] + shift[...]).astype(bf16)
+    low_t[...] = low[...].T
+    cot_low[...] = cot[...].astype(bf16)
+    cot_t[...] = cot_low[...].T
+    out[...] = middle[...] + last_bias[...]
+    small[0:1] = column_sum(cot_low[...].astype(f32))
+    grad_middle[...] = jnp.zeros((512, 768), f32)
+
+    def chunk(g, _):
+        weight = pick(wi, g)
+        inner = matmul(low[...], weight) + in_bias[g]
+        phi = 0.5 * (1.0 + lax.erf(inner * 0.7071067811865476))
+        active = (inner * phi).astype(bf16)
+        slope = phi + inner * jnp.exp(-0.5 * inner * inner) * 0.3989422804014327
+        for x in range(2):
+            part = wt[g, 4 * x : 4 * x + 4].reshape(768, 384)
+            now = active[:, 384 * x : 384 * x + 384]
+            out[...] += matmul(now, part, NT)
+            wt_grad[g, 4 * x : 4 * x + 4] = (
+                matmul(cot_t[...], now).astype(bf16).reshape(4, 192, 384)
+            )
+            back = matmul(cot_low[...], part)
+            grad_low[:, 384 * x : 384 * x + 384] = (
+                back * slope[:, 384 * x : 384 * x + 384]
+            ).astype(bf16)
+        small_in[g] = column_sum(grad_low[...].astype(f32))
+        put(wi_grad, g, matmul(low_t[...], grad_low[...]).astype(bf16))
+        grad_middle[...] += matmul(grad_low[...], weight, NT)
+        return 0
+
+    lax.fori_loop(0, 4, chunk, 0)
+    grad = grad_middle[...]
+    small[1:2] = column_sum(grad * hat[...])
+    small[2:3] = column_sum(grad)
+    grad = cot[...] + norm_backward(hat[...], inverse, gain[...], grad)
+    grad_middle[...] = grad
+    attended = grad.astype(bf16)
+    small[3:4] = column_sum(attended.astype(f32))
+    small[4:8] = jnp.zeros((4, 768), f32)
+    grads = matmul(merged[...].T, attended).astype(bf16)
+    for g in range(4):
+        put(wo_grad, g, grads[:, 192 * g : 192 * g + 192])
+    grad_merged[...] = matmul(attended, full[...], NT).astype(bf16)
+
+
+def dense(merged, base, cot, wo, wi, wt, out_bias, gain, shift, in_bias, last_bias):
+    rows = (512, 768)
+    return pl.pallas_call(
+        dense_kernel,
+        name="dense",
+        in_specs=[vmem()] * 11,
+        out_specs=[vmem()] * 8,
+        out_shape=[
+            shape(rows, f32), shape(rows, f32), shape(rows, bf16),
+            shape((4, GROUP, 96, 192), bf16), shape((4, GROUP, 96, 768), bf16),
+            shape((4, GROUP, 192, 384), bf16), shape((8, 768), f32), shape((4, 1, 768), f32),
+        ],
+        scratch_shapes=[
+            pltpu.VMEM((768, 768), bf16), pltpu.VMEM(rows, f32), pltpu.VMEM(rows, f32),
+            pltpu.VMEM(rows, bf16), pltpu.VMEM((768, 512), bf16), pltpu.VMEM(rows, bf16),
+            pltpu.VMEM((768, 512), bf16), pltpu.VMEM(rows, bf16),
+        ],
+        compiler_params=params(),
+    )(merged, base, cot, wo, wi, wt, out_bias, gain, shift, in_bias, last_bias)
+
+
+def final_kernel(
+    base, grad_middle, d0, d1, d2, d3, weight, gain, shift, token_grad, grads_out, small,
+):
+    hat, inverse = norm_parts(base[...])
+    low_t = (hat * gain[...] + shift[...]).astype(bf16).T
+    grad = jnp.zeros((512, 768), f32)
+    small[...] = jnp.zeros((8, 768), f32)
+    for quad, part in enumerate((d0, d1, d2, d3)):
+        now = part[...]
+        put(grads_out, quad, matmul(low_t, now).astype(bf16))
+        grad = grad + matmul(now, pick(weight, quad), NT)
+    small[0:1] = column_sum(grad * hat)
+    small[1:2] = column_sum(grad)
+    token_grad[...] = grad_middle[...] + norm_backward(hat, inverse, gain[...], grad)
+
+
+def final(base, grad_middle, quads, weight, gain, shift):
+    rows = (512, 768)
+    return pl.pallas_call(
+        final_kernel,
+        name="input_gradients",
+        in_specs=[vmem()] * 9,
+        out_specs=[vmem()] * 3,
+        out_shape=[shape(rows, f32), shape((4, GROUP, 96, 576), bf16), shape((8, 768), f32)],
+        compiler_params=params(),
+    )(base, grad_middle, *quads, weight, gain, shift)
+
+
+def member_of(x, y, c):
+    return x * 4 + y * 2 + c
+
+
+def place():
+    seq, col = lax.axis_index("seq"), lax.axis_index("grp")
+    return seq // 2, seq % 2, col // 2, col % 2
+
+
+def at_place(z, x, y, c):
+    return (z * 2 + x, y * 2 + c)
+
+
+def remote(src, dst, send_sem, recv_sem, target):
+    return pltpu.make_async_remote_copy(
+        src_ref=src, dst_ref=dst, send_sem=send_sem, recv_sem=recv_sem,
+        device_id=target, device_id_type=MESH,
+    )
+
+
+def block_barrier(z, x, y, c):
+    barrier = pltpu.get_barrier_semaphore()
+    near = [at_place((z + o) % 4, x, y, c) for o in (1, 2, 3)]
+    near += [at_place(z, 1 - x, y, c), at_place(z, x, 1 - y, c), at_place(z, 1 - x, 1 - y, c)]
+    near += [at_place(z, x, y, 1 - c)]
+    for target in near:
+        pl.semaphore_signal(barrier, inc=1, device_id=target, device_id_type=MESH)
+    pl.semaphore_wait(barrier, len(near))
+
+
+def gather_kernel(count, *refs):
+    ins, outs = refs[:count], refs[count : 2 * count]
+    loc, zs, zr, ps, pr, qs, qr, cs, cr = refs[2 * count :]
+    z, x, y, c = place()
+    me = member_of(x, y, c)
+    block_barrier(z, x, y, c)
+    arrays = range(count)
+    local = [pltpu.make_async_copy(ins[k], outs[k].at[z, me], loc.at[k]) for k in arrays]
+    for copy in local:
+        copy.start()
+    started = []
+    beside = [(1 - x, y), (x, 1 - y)]
+
+    def go(copy):
+        copy.start()
+        started.append(copy)
+
+    for o in (1, 2, 3):
+        for k in arrays:
+            go(remote(ins[k], outs[k].at[z, me], zs.at[o, k], zr.at[4 - o, k],
+                      at_place((z + o) % 4, x, y, c)))
+
+    def push(layer, slot, sources):
+        for p, (px, py) in enumerate(beside):
+            for k in arrays:
+                go(remote(sources[k], outs[k].at[layer, me], ps.at[p, slot, k], pr.at[p, slot, k],
+                          at_place(z, px, py, c)))
+
+    def relay(layer, slot):
+        for p, (px, py) in enumerate(beside):
+            m = member_of(px, py, c)
+            for k in arrays:
+                part = outs[k].at[layer, m]
+                remote(part, part, ps.at[p, slot, k], pr.at[p, slot, k],
+                       at_place(z, px, py, c)).wait_recv()
+        for k in arrays:
+            rows = ins[k].shape[0] // 2
+            for p, (px, py) in enumerate(beside):
+                part = outs[k].at[layer, member_of(px, py, c), p * rows : (p + 1) * rows]
+                tx, ty = beside[1 - p]
+                go(remote(part, part, qs.at[p, slot, k], qr.at[p, slot, k],
+                          at_place(z, tx, ty, c)))
+
+    push(z, 0, ins)
+    for copy in local:
+        copy.wait()
+    for o in (1, 2, 3):
+        layer = (z + o) % 4
+        for k in arrays:
+            part = outs[k].at[layer, me]
+            remote(part, part, zs.at[o, k], zr.at[o, k], at_place(layer, x, y, c)).wait_recv()
+        push(layer, o, [outs[k].at[layer, me] for k in arrays])
+        relay((z + o - 1) % 4, o - 1)
+    relay((z + 3) % 4, 3)
+
+    def across(slot, px, py):
+        m = member_of(px, py, c)
+        for k in arrays:
+            part = outs[k].at[:, m]
+            go(remote(part, part, cs.at[slot, k], cr.at[slot, k], at_place(z, x, y, 1 - c)))
+
+    across(0, x, y)
+    across(1, 1 - x, y)
+    across(2, x, 1 - y)
+    far = member_of(1 - x, 1 - y, c)
+    for slot in range(4):
+        layer = (z + slot) % 4
+        for k in arrays:
+            rows = ins[k].shape[0] // 2
+            for p in range(2):
+                part = outs[k].at[layer, far, p * rows : (p + 1) * rows]
+                remote(part, part, qs.at[p, slot, k], qr.at[p, slot, k],
+                       at_place(z, *beside[1 - p], c)).wait_recv()
+    across(3, 1 - x, 1 - y)
+    for slot, (px, py) in enumerate([(x, y), (1 - x, y), (x, 1 - y), (1 - x, 1 - y)]):
+        m = member_of(px, py, 1 - c)
+        for k in arrays:
+            part = outs[k].at[:, m]
+            remote(part, part, cs.at[slot, k], cr.at[slot, k], at_place(z, x, y, 1 - c)).wait_recv()
+    for copy in started:
+        copy.wait_send()
+
+
+def gather_weights(parts, identity):
+    count = len(parts)
+    return pl.pallas_call(
+        functools.partial(gather_kernel, count),
+        name="gather_weights",
+        in_specs=[pl.BlockSpec(memory_space=pl.ANY)] * count,
+        out_specs=[pl.BlockSpec(memory_space=pl.ANY)] * count,
+        out_shape=[shape((4, GROUP) + part.shape, part.dtype) for part in parts],
+        scratch_shapes=[
+            sems(count), dsems(4, count), dsems(4, count), dsems(2, 4, count), dsems(2, 4, count),
+            dsems(2, 4, count), dsems(2, 4, count), dsems(4, count), dsems(4, count),
+        ],
+        compiler_params=params(identity),
+    )(*parts)
+
+
+def dsems(*dims):
+    return pltpu.SemaphoreType.DMA(dims)
+
+
+def reduce_kernel(count, *refs):
+    ins, small = refs[:count], refs[count]
+    outs, total = refs[count + 1 : 2 * count + 1], refs[2 * count + 1]
+    rest = refs[2 * count + 2 :]
+    own, across, one, two, deep = [rest[i * count : (i + 1) * count] for i in range(5)]
+    (sm_c, sm_p, sm_z, loc, cs, cr, xs, xr, ys, yr, zs, zr, sms, smr) = rest[5 * count :]
+    z, x, y, c = place()
+    block_barrier(z, x, y, c)
+    arrays = range(count)
+    started = []
+
+    def go(copy):
+        copy.start()
+        started.append(copy)
+
+    mine, px_, py_, far = (x, y), (1 - x, y), (x, 1 - y), (1 - x, 1 - y)
+    other = at_place(z, x, y, 1 - c)
+    slot_of = lambda p: p[0] * 2 + p[1]
+    sm_c[c] = small[...]
+    go(remote(sm_c.at[c], sm_c.at[c], sms.at[0], smr.at[0], other))
+    for n, p in enumerate((far, px_, py_, mine)):
+        for k in arrays:
+            go(remote(ins[k].at[:, member_of(*p, 1 - c)], across[k].at[slot_of(p)],
+                      cs.at[n, k], cr.at[n, k], other))
+            pltpu.make_async_copy(
+                ins[k].at[:, member_of(*p, c)], own[k].at[slot_of(p)], loc.at[n, k]
+            ).start()
+    remote(sm_c.at[c], sm_c.at[1 - c], sms.at[0], smr.at[0], other).wait_recv()
+    flat = x * 2 + y
+    sm_p[flat] = sm_c[0] + sm_c[1]
+    plane = (px_, py_, far)
+    for n, p in enumerate(plane):
+        go(remote(sm_p.at[flat], sm_p.at[flat], sms.at[1 + n], smr.at[1 + n], at_place(z, *p, c)))
+
+    def add(target, source):
+        rows = target.shape[-2]
+
+        def step(i, _):
+            target[i] = (target[i].astype(f32) + source[i].astype(f32)).astype(bf16)
+            return 0
+
+        lax.fori_loop(0, 4, step, 0)
+
+    def landed(n, p):
+        for k in arrays:
+            pltpu.make_async_copy(
+                ins[k].at[:, member_of(*p, c)], own[k].at[slot_of(p)], loc.at[n, k]
+            ).wait()
+            remote(ins[k].at[:, member_of(*p, 1 - c)], across[k].at[slot_of(p)],
+                   cs.at[n, k], cr.at[n, k], other).wait_recv()
+            add(own[k].at[slot_of(p)], across[k].at[slot_of(p)])
+
+    halves = [ins[k].shape[2] // 2 for k in arrays]
+    hx = lambda k: slice(0, halves[k])
+    hy = lambda k: slice(halves[k], 2 * halves[k])
+    to_x, to_y = at_place(z, *px_, c), at_place(z, *py_, c)
+
+    def x_first(k, p, i, target):
+        src = own[k].at[slot_of(p), :, hx(k)]
+        return remote(src, target, xs.at[i, k], xr.at[i, k], to_x)
+
+    def y_first(k, p, i, target):
+        src = own[k].at[slot_of(p), :, hy(k)]
+        return remote(src, target, ys.at[i, k], yr.at[i, k], to_y)
+
+    landed(0, far)
+    for k in arrays:
+        go(x_first(k, far, 0, one[k].at[0]))
+        go(y_first(k, far, 0, one[k].at[1]))
+    landed(1, px_)
+    for k in arrays:
+        go(x_first(k, px_, 1, one[k].at[2]))
+    landed(2, py_)
+    for k in arrays:
+        go(y_first(k, py_, 1, one[k].at[3]))
+    landed(3, mine)
+    for n, p in enumerate(plane):
+        index = slot_of(p)
+        remote(sm_p.at[index], sm_p.at[index], sms.at[1 + n], smr.at[1 + n],
+               at_place(z, *p, c)).wait_recv()
+    sm_z[z] = (sm_p[0] + sm_p[1]) + (sm_p[2] + sm_p[3])
+    for o in (1, 2, 3):
+        go(remote(sm_z.at[z], sm_z.at[z], sms.at[3 + o], smr.at[7 - o],
+                  at_place((z + o) % 4, x, y, c)))
+    for k in arrays:
+        x_first(k, far, 0, one[k].at[0]).wait_recv()
+        add(own[k].at[slot_of(py_), :, hx(k)], one[k].at[0])
+        go(remote(own[k].at[slot_of(py_), :, hx(k)], two[k].at[0], ys.at[2, k], yr.at[2, k], to_y))
+        y_first(k, far, 0, one[k].at[1]).wait_recv()
+        add(own[k].at[slot_of(px_), :, hy(k)], one[k].at[1])
+        go(remote(own[k].at[slot_of(px_), :, hy(k)], two[k].at[1], xs.at[2, k], xr.at[2, k], to_x))
+    for k in arrays:
+        x_first(k, px_, 1, one[k].at[2]).wait_recv()
+        add(own[k].at[slot_of(mine), :, hx(k)], one[k].at[2])
+        y_first(k, py_, 1, one[k].at[3]).wait_recv()
+        add(own[k].at[slot_of(mine), :, hy(k)], one[k].at[3])
+    for k in arrays:
+        remote(own[k].at[slot_of(py_), :, hx(k)], two[k].at[0], ys.at[2, k], yr.at[2, k], to_y).wait_recv()
+        add(own[k].at[slot_of(mine), :, hx(k)], two[k].at[0])
+        remote(own[k].at[slot_of(px_), :, hy(k)], two[k].at[1], xs.at[2, k], xr.at[2, k], to_x).wait_recv()
+        add(own[k].at[slot_of(mine), :, hy(k)], two[k].at[1])
+        for o in (1, 2, 3):
+            layer = (z + o) % 4
+            go(remote(own[k].at[slot_of(mine), layer], deep[k].at[4 - o], zs.at[o, k],
+                      zr.at[4 - o, k], at_place(layer, x, y, c)))
+    for o in (1, 2, 3):
+        layer = (z + o) % 4
+        remote(sm_z.at[layer], sm_z.at[layer], sms.at[3 + o], smr.at[3 + o],
+               at_place(layer, x, y, c)).wait_recv()
+    total[...] = (sm_z[0] + sm_z[1]) + (sm_z[2] + sm_z[3])
+    for k in arrays:
+        value = own[k][slot_of(mine), z].astype(f32)
+        for o in (1, 2, 3):
+            remote(own[k].at[slot_of(mine), z], deep[k].at[o], zs.at[o, k], zr.at[o, k],
+                   at_place((z + o) % 4, x, y, c)).wait_recv()
+            value = value + deep[k][o].astype(f32)
+        outs[k][...] = value
+    for copy in started:
+        copy.wait_send()
+
+
+def reduce_gradients(parts, small, identity):
+    count = len(parts)
+    dims = [part.shape[2:] for part in parts]
+    half = [(rows // 2, lanes) for rows, lanes in dims]
+    return pl.pallas_call(
+        functools.partial(reduce_kernel, count),
+        name="reduce_gradients",
+        in_specs=[pl.BlockSpec(memory_space=pl.ANY)] * count + [vmem()],
+        out_specs=[vmem()] * (count + 1),
+        out_shape=[shape(d, f32) for d in dims] + [shape(small.shape, f32)],
+        scratch_shapes=[pltpu.VMEM((4, 4) + d, bf16) for d in dims]
+        + [pltpu.VMEM((4, 4) + d, bf16) for d in dims]
+        + [pltpu.VMEM((4, 4) + d, bf16) for d in half]
+        + [pltpu.VMEM((2, 4) + d, bf16) for d in half]
+        + [pltpu.VMEM((4,) + d, bf16) for d in dims]
+        + [
+            pltpu.VMEM((2,) + small.shape, f32),
+            pltpu.VMEM((4,) + small.shape, f32),
+            pltpu.VMEM((4,) + small.shape, f32),
+            dsems(4, count), dsems(4, count), dsems(4, count),
+            dsems(3, count), dsems(3, count), dsems(3, count), dsems(3, count),
+            dsems(4, count), dsems(4, count), sems(7), sems(7),
+        ],
+        compiler_params=params(identity),
+    )(*parts, small)
+
+
+def all_weights(parts, seq, grp):
+    if (seq, grp) == (8, 4):
+        return gather_weights(parts, 5)
+    gathered = []
+    for n, part in enumerate(parts):
+        whole = lax.all_gather(lax.all_gather(part, "grp"), "seq")
+        lead = whole.shape[0] // 8
+        whole = whole.reshape((8, lead) + whole.shape[1:])
+        if n == 3:
+            whole = whole.transpose(0, 2, 3, 1, 4)
+            whole = whole.reshape(4, GROUP, part.shape[0], lead * part.shape[1])
+        else:
+            whole = whole.transpose(0, 2, 1, 3, 4)
+            whole = whole.reshape(4, GROUP, lead * part.shape[0], part.shape[1])
+        gathered.append(whole)
+    return gathered
+
+
+def sum_gradients(parts, small, seq, grp):
+    if (seq, grp) == (8, 4):
+        return reduce_gradients(parts, small, 6)
+    lead = seq // 8
+    sums = []
+    for n, part in enumerate(parts):
+        height, lanes = part.shape[2:]
+        whole = part.reshape(8, grp, height, lanes)
+        if n == 3:
+            whole = whole.reshape(8, grp, height, lead, lanes // lead).transpose(0, 3, 1, 2, 4)
+        else:
+            whole = whole.reshape(8, grp, lead, height // lead, lanes).transpose(0, 2, 1, 3, 4)
+        whole = whole.reshape((seq, grp) + whole.shape[3:]).astype(f32)
+        whole = lax.psum_scatter(whole, "seq", scatter_dimension=0)
+        sums.append(lax.psum_scatter(whole, "grp", scatter_dimension=0))
+    return sums + [lax.psum(small, ("seq", "grp"))]
+
+
 def position_table(coordinates, width):
     quarter = width // 4
     frequency = jnp.exp(jnp.arange(quarter, dtype=jnp.float32) * (-math.log(10000.0) / quarter))
@@ -736,25 +1193,6 @@
     centred = values - average
     variance = jnp.mean(centred * centred, axis=-1, keepdims=True)
     return centred * lax.rsqrt(variance + epsilon) * norm_gain + norm_shift
-
-
-def gelu_slope(values):
-    return (
-        0.5 * (1.0 + lax.erf(values * 0.7071067811865476))
-        + values * jnp.exp(-0.5 * values * values) * 0.3989422804014327
-    )
-
-
-def product(left, right):
-    return jnp.dot(left, right, preferred_element_type=jnp.float32)
-
-
-def product_left(left, right):
-    return jnp.einsum("rd,rf->df", left, right, preferred_element_type=jnp.float32)
-
-
-def product_right(left, right):
-    return jnp.einsum("rf,df->rd", left, right, preferred_element_type=jnp.float32)
 
 
 def in_order(rows):
@@ -791,20 +1229,19 @@
 ):
     rows, width = tokens.shape
     grp = lax.axis_size("grp")
+    seq = lax.axis_size("seq")
     slides = lengths.shape[0]
     linear = lax.axis_index("seq") * grp + lax.axis_index("grp")
     start = linear * rows
-    part = [
-        lax.all_gather(w, "grp", axis=1, tiled=True)
-        for w in (query_weight, key_weight, value_weight, output_weight, inner_weight, outer_weight)
+    shard = query_weight.shape[0]
+    heads = [w.reshape(shard, 4, 1, HD) for w in (query_weight, key_weight, value_weight)]
+    parts = [
+        jnp.concatenate(heads, axis=2).reshape(shard, 576),
+        output_weight,
+        inner_weight,
+        outer_weight.T,
     ]
-    full_query, full_key, full_value, full_output, full_inner, full_outer = [
-        lax.all_gather(w, "seq", axis=0, tiled=True) for w in part
-    ]
-    quads = [
-        w.reshape(width, 4, 4, HD).transpose(1, 0, 2, 3) for w in (full_query, full_key, full_value)
-    ]
-    joint_weight = jnp.stack(quads, axis=3).reshape(4, width, 576)
+    joint_weight, wo, wi, wt = all_weights(parts, seq, grp)
     joint_bias = jnp.stack(
         [b.reshape(4, 4, HD) for b in (query_bias, jnp.zeros_like(query_bias), value_bias)], axis=2
     ).reshape(4, 1, 576)
@@ -823,78 +1260,41 @@
         ],
         axis=0,
     )
-    normed, first_back = jax.vjp(layer_norm, base, first_gain, first_shift)
-    normed_low = normed.astype(bf16)
+    row = lambda v: v.reshape(1, -1)
+    normed_low = layer_norm(base, first_gain, first_shift).astype(bf16)
     msg, q_rows, kv_rows, kv8, kv16 = attention_in(
         grp, slides, normed_low, joint_weight, joint_bias, flags
     )
     own, stat = attention_forward(slides, q_rows, kv_rows, kv8, kv16)
     merged_low = attention_out(grp, own)
-    middle = base + product(merged_low, full_output) + output_bias
-    normed_two, second_back = jax.vjp(layer_norm, middle, second_gain, second_shift)
-    normed_two_low = normed_two.astype(jnp.bfloat16)
-    inner = product(normed_two_low, full_inner) + inner_bias
-    activated = jax.nn.gelu(inner, approximate=False).astype(jnp.bfloat16)
-    output = middle + product(activated, full_outer) + outer_bias
-    grad_outer = cotangent.astype(jnp.bfloat16)
-    outer_weight_grad = product_left(activated, grad_outer)
-    outer_bias_grad = jnp.sum(grad_outer.astype(jnp.float32), axis=0)
-    grad_inner = (product_right(grad_outer, full_outer) * gelu_slope(inner)).astype(jnp.bfloat16)
-    inner_weight_grad = product_left(normed_two_low, grad_inner)
-    inner_bias_grad = jnp.sum(grad_inner.astype(jnp.float32), axis=0)
-    grad_middle_part, second_gain_grad, second_shift_grad = second_back(
-        product_right(grad_inner, full_inner)
-    )
-    grad_middle = cotangent + grad_middle_part
-    grad_attended = grad_middle.astype(jnp.bfloat16)
-    output_weight_grad = product_left(merged_low, grad_attended)
-    output_bias_grad = jnp.sum(grad_attended.astype(jnp.float32), axis=0)
-    grad_merged = product_right(grad_attended, full_output).astype(bf16)
+    output, grad_middle, grad_merged, wo_grad, wi_grad, wt_grad, small, small_in = dense(
+        merged_low, base, cotangent, wo, wi, wt, row(output_bias), row(second_gain),
+        row(second_shift), inner_bias.reshape(4, 1, 768), row(outer_bias),
+    )
     shared = gradient_in(grp, grad_merged)
     pre, dkv8, dkv16 = attention_backward(q_rows, kv_rows, kv8, kv16, msg, shared, stat)
-    query_low, key_low, value_low = gradient_out(grp, pre, dkv8, dkv16)
-    query_weight_grad = product_left(normed_low, query_low)
-    key_weight_grad = product_left(normed_low, key_low)
-    value_weight_grad = product_left(normed_low, value_low)
-    query_bias_grad = jnp.sum(query_low.astype(jnp.float32), axis=0)
-    value_bias_grad = jnp.sum(value_low.astype(jnp.float32), axis=0)
-    grad_normed = (
-        product_right(query_low, full_query)
-        + product_right(key_low, full_key)
-        + product_right(value_low, full_value)
-    )
-    grad_base_part, first_gain_grad, first_shift_grad = first_back(grad_normed)
-    token_grad = grad_middle + grad_base_part
-    sum_query, sum_key, sum_value, sum_output, sum_inner, sum_outer = (
-        lax.psum_scatter(query_weight_grad, "grp", scatter_dimension=1, tiled=True),
-        lax.psum_scatter(key_weight_grad, "grp", scatter_dimension=1, tiled=True),
-        lax.psum_scatter(value_weight_grad, "grp", scatter_dimension=1, tiled=True),
-        lax.psum_scatter(output_weight_grad, "grp", scatter_dimension=1, tiled=True),
-        lax.psum_scatter(inner_weight_grad, "grp", scatter_dimension=1, tiled=True),
-        lax.psum_scatter(outer_weight_grad, "grp", scatter_dimension=1, tiled=True),
-    )
-    sum_query, sum_key, sum_value, sum_output, sum_inner, sum_outer = (
-        lax.psum_scatter(sum_query, "seq", scatter_dimension=0, tiled=True),
-        lax.psum_scatter(sum_key, "seq", scatter_dimension=0, tiled=True),
-        lax.psum_scatter(sum_value, "seq", scatter_dimension=0, tiled=True),
-        lax.psum_scatter(sum_output, "seq", scatter_dimension=0, tiled=True),
-        lax.psum_scatter(sum_inner, "seq", scatter_dimension=0, tiled=True),
-        lax.psum_scatter(sum_outer, "seq", scatter_dimension=0, tiled=True),
-    )
-    small = lax.psum(
-        (
-            first_gain_grad,
-            first_shift_grad,
-            query_bias_grad,
-            value_bias_grad,
-            output_bias_grad,
-            second_gain_grad,
-            second_shift_grad,
-            inner_bias_grad,
-            outer_bias_grad,
-        ),
-        ("seq", "grp"),
-    )
+    *quads, sums = gradient_out(grp, pre, dkv8, dkv16)
+    token_grad, joint_grad, first_small = final(
+        base, grad_middle, quads, joint_weight, row(first_gain), row(first_shift)
+    )
+    sums = sums.reshape(4, 4, 3, HD)
+    vectors = [
+        first_small[0], first_small[1], sums[:, :, 0].reshape(-1), sums[:, :, 2].reshape(-1),
+        small[3], small[1], small[2], small_in.reshape(-1), small[0],
+    ]
+    sizes = [v.shape[0] for v in vectors]
+    pack = jnp.concatenate(vectors).reshape(-1, LANES)
+    joint_sum, sum_output, sum_inner, sum_outer, pack = sum_gradients(
+        [joint_grad, wo_grad, wi_grad, wt_grad], pack, seq, grp
+    )
+    joint_sum = joint_sum.reshape(shard, 4, 3, HD)
+    sum_query, sum_key, sum_value = [joint_sum[:, :, i].reshape(shard, 192) for i in range(3)]
+    sum_outer = sum_outer.T
+    small = []
+    pack = pack.reshape(-1)
+    for size in sizes:
+        small.append(pack[:size])
+        pack = pack[size:]
     return (
         back_order(output),
         back_order(token_grad),

time: 1220 us -> 518 us (0.42)
  waiting for transfers between devices: 698 us -> 0 us
  Pallas kernels: 257 us -> 476 us
  blocking collectives: 81.1 us -> 0 us
  matrix products: 75.4 us -> 0 us
  local copies, waits for them, and re-layouts: 69.2 us -> 23.8 us
  between operations: 15.6 us -> 2.11 us
    reduce_scatter x8 -> x0, waiting for transfers between devices: 390 us -> none  [the longest x1 73.1 us: body(): lax.psum_scatter(inner_weight_grad, 'grp', scatter_dimension=1, tiled=True)]
    pallas_call x0 -> x4, Pallas kernels: none -> 226 us  [the longest x1 96.1 us: reduce_gradients(): pl.pallas_call(functools.partial(reduce_kernel, count), name='reduce_grad...]
    unnamed x22 -> x0, waiting for transfers between devices: 209 us -> none
    all_gather x6 -> x0, waiting for transfers between devices: 98.6 us -> none  [body(): lax.all_gather(w, 'seq', axis=0, tiled=True)]
    dot_general x15 -> x0, matrix products: 75.4 us -> none  [the longest x3 28.6 us: product(): return jnp.dot(left, right, preferred_element_type=jnp.float32)]
    psum x1 -> x0, blocking collectives: 40.8 us -> none  [body(): lax.psum((first_gain_grad, first_shift_grad, query_bias_grad, value_bias_...]
    all_gather x6 -> x0, blocking collectives: 40.3 us -> none  [body(): lax.all_gather(w, 'grp', axis=1, tiled=True)]
    unnamed x190 -> x131, local copies, waits for them, and re-layouts: 38.5 us -> 6.72 us
  transfers between devices with their start and end apart: 18 -> 0, of which waited for: 15 -> 0; matrix products, arithmetic and copies ran while one was open for 11% -> 0% of each run, Pallas kernels for 12% -> 0%
where the time goes in v2:
time: 518 us; the launch traced here: 510 us
  Pallas kernels  476 us (92%)
  local copies, waits for them, and re-layouts  23.8 us (5%)
  other arithmetic  7.75 us (1%)
    pallas_call x1, Pallas kernels, reduce_gradients(): pl.pallas_call(functools.partial(reduce_kernel, count), name='reduce_grad...  96.1 us
    pallas_call x1, Pallas kernels, gather_weights(): pl.pallas_call(functools.partial(gather_kernel, count), name='gather_weig...  86.6 us
    pallas_call x1, Pallas kernels, attention_in(): pl.pallas_call(functools.partial(qkv_kernel, grp, slides), name='project_...  61.6 us
    pallas_call x1, Pallas kernels, attention_forward(): pl.pallas_call(functools.partial(forward_kernel, slides), name='attention...  55.8 us
    pallas_call x1, Pallas kernels, attention_backward(): pl.pallas_call(backward_kernel, name='attention_backward', grid=(2,), in_...  49.9 us
    pallas_call x1, Pallas kernels, gradient_out(): pl.pallas_call(functools.partial(return_kernel, grp), name='return_gradie...  48.7 us
    pallas_call x1, Pallas kernels, dense(): pl.pallas_call(dense_kernel, name='dense', in_specs=[vmem()] * 11, out_sp...  31.6 us
    pallas_call x1, Pallas kernels, attention_out(): pl.pallas_call(functools.partial(merged_kernel, grp), name='share_merged'...  19.3 us

profile of v2, /device:TPU:0, one launch (start us, length us, event | category | flops | bytes accessed | tf_op | source)
XLA Modules:
  0.0 509.6 jit_solution(16984412451590224918)
XLA Ops:
  0.7 0.8 slice_convert_fusion.1
  1.5 3.7 multiply_sine_fusion.1
  5.2 0.4 maximum_add_fusion
  5.6 1.4 fusion.2
  7.4 0.1 reduce_sum.27
  7.5 0.3 multiply_reduce_fusion
  8.0 0.4 copy-done
  8.5 1.2 add_convert_fusion.n_ref
  9.8 0.2 reduce-window.8
  10.2 0.5 slice_reduce_fusion
  11.0 0.7 maximum_maximum_fusion.f_ref
  11.7 0.1 copy.176
  11.8 0.1 copy.177
  11.9 0.1 copy.178
  12.1 0.8 copy.180.refs_0_
  12.9 86.6 %gather_weights.1 = (bf16[4,8,96,576]{3,2,1,0:T(8,128)(2,1)}, bf16[4,8,96,192]{3,2,1,0:T(8,128)(2,1)}, bf16[4,8,96,768]{3,2,1,0:T(8,128)(2,1)}, bf16[4,8,192,384]{3,2,1,0:T(8,128)(2,1)}) custom-call(bf16[96,576]{1,0:T(8,128)(2,1)} %copy.180.refs_0_, bf16[96,192]{1,0:T(8,128)(2,1)} %refs_1_.1, bf16[96,768]{1,0:T(8,128)(2,1)} %refs_2_.1, ...), custom_call_target="tpu_custom_call" | custom-call | tf_op jit(solution)/shard_map/gather_weights/pallas_call | solution.py:979
  99.8 0.7 reshape.291.b_ref
  100.5 61.6 %project_and_share.1 = (bf16[8,320,512]{2,1,0:T(8,128)(2,1)}, bf16[2,4096,128]{2,1,0:T(8,128)(2,1)}, bf16[2,4096,128]{2,1,0:T(8,128)(2,1)}, bf16[2,2,512,128]{3,2,1,0:T(8,128)(2,1)}, bf16[4,2,256,128]{3,2,1,0:T(8,128)(2,1)}) custom-call(bf16[512,768]{1,0:T(8,128)(2,1)} %add_convert_fusion.n_ref, bf16[4,8,96,576]{3,2,1,0:T(8,128)(2,1)} %get-tuple-element.52.w_ref.weight, ...), custom_call_target="tpu_custom_call" | custom-call | tf_op jit(solution)/shard_map/project_and_share/pallas_call | solution.py:610
  162.2 55.8 %attention_forward.1 = (bf16[8,96,512]{2,1,0:T(8,128)(2,1)}, f32[2,8,56,512]{3,2,1,0:T(8,128)}) custom-call(bf16[2,4096,128]{2,1,0:T(8,128)(2,1)} %get-tuple-element.53.q_ref, bf16[2,4096,128]{2,1,0:T(8,128)(2,1)} %get-tuple-element.54.kv_ref, bf16[2,2,512,128]{3,2,1,0:T(8,128)(2,1)} %get-tuple-element.55.kv8, bf16[4,2,256,128]{3,2,1,0:T(8,128)(2,1)} %get-tuple-element.56.kv16), custom_call_target="tpu_custom_call" | custom-call | tf_op jit(solution)/shard_map/attention_forward/pallas_call | solution.py:634
  218.0 19.3 %share_merged.1.merged = bf16[512,768]{1,0:T(8,128)(2,1)} custom-call(bf16[8,96,512]{2,1,0:T(8,128)(2,1)} %get-tuple-element.57.om), custom_call_target="tpu_custom_call" | custom-call | tf_op jit(solution)/shard_map/share_merged/pallas_call | solution.py:659
  237.3 1.4 fusion.1
  239.1 0.4 copy-done.21
  239.4 0.7 reshape.280.out_bias
  240.2 0.6 reshape.281.gain
  240.7 0.6 reshape.282.shift
  241.3 0.6 reshape.284.last_bias
  241.9 31.6 %dense.1 = (f32[512,768]{1,0:T(8,128)}, f32[512,768]{1,0:T(8,128)}, bf16[512,768]{1,0:T(8,128)(2,1)}, bf16[4,8,96,192]{3,2,1,0:T(8,128)(2,1)}, bf16[4,8,96,768]{...) custom-call(bf16[512,768]{1,0:T(8,128)(2,1)} %share_merged.1.merged, ...), custom_call_target="tpu_custom_call" | custom-call | tf_op jit(solution)/shard_map/dense/pallas_call | solution.py:817
  273.5 14.8 %share_gradient.1.gm = bf16[8,96,512]{2,1,0:T(8,128)(2,1)} custom-call(bf16[512,768]{1,0:T(8,128)(2,1)} %get-tuple-element.64.rows_ref), custom_call_target="tpu_custom_call" | custom-call | tf_op jit(solution)/shard_map/share_gradient/pallas_call | solution.py:671
  288.4 49.9 %attention_backward.1 = (f32[2,8,144,512]{3,2,1,0:T(8,128)}, bf16[2,2,512,128]{3,2,1,0:T(8,128)(2,1)}, bf16[4,2,256,128]{3,2,1,0:T(8,128)(2,1)}) custom-call(bf16[2,4096,128]{2,1,0:T(8,128)(2,1)} %get-tuple-element.53.q_ref, bf16[2,4096,128]{2,1,0:T(8,128)(2,1)} %get-tuple-element.54.kv_ref, bf16[2,2,512,128]{3,2,1,0:T(8,128)(2,1)} %get-tuple-element.55.kv8, ...), custom_call_target="tpu_custom_call" | custom-call | tf_op jit(solution)/shard_map/attention_backward/pallas_call | solution.py:683
  338.3 48.7 %return_gradients.1 = (bf16[512,576]{1,0:T(8,128)(2,1)}, bf16[512,576]{1,0:T(8,128)(2,1)}, bf16[512,576]{1,0:T(8,128)(2,1)}, bf16[512,576]{1,0:T(8,128)(2,1)}, f32[4,1,576]{2,1,0:T(1,128)}) custom-call(f32[2,8,144,512]{3,2,1,0:T(8,128)} %get-tuple-element.66.pre, bf16[2,2,512,128]{3,2,1,0:T(8,128)(2,1)} %get-tuple-element.67.dkv8, ...), custom_call_target="tpu_custom_call" | custom-call | tf_op jit(solution)/shard_map/return_gradients/pallas_call | solution.py:720
  386.9 0.6 broadcast_in_dim.42.gain
  387.5 0.6 broadcast_in_dim.43.shift
  388.1 11.5 %input_gradients.1 = (f32[512,768]{1,0:T(8,128)}, bf16[4,8,96,576]{3,2,1,0:T(8,128)(2,1)}, f32[8,768]{1,0:T(8,128)}) custom-call(f32[512,768]{1,0:T(8,128)} %bitcast.285, f32[512,768]{1,0:T(8,128)} %get-tuple-element.62.grad_middle, bf16[512,576]{1,0:T(8,128)(2,1)} %get-tuple-element.69.d0, bf16[512,576]{1,0:T(8,128)(2,1)} %get-tuple-element.70.d1, ...), custom_call_target="tpu_custom_call" | custom-call | tf_op jit(solution)/shard_map/input_gradients/pallas_call | solution.py:854
  399.6 0.8 slice_reduce_fusion.22
  400.5 0.1 reshape.287
  401.0 0.6 copy-done.13
  401.6 96.1 %reduce_gradients.1 = (f32[96,576]{1,0:T(8,128)}, f32[96,192]{1,0:T(8,128)}, f32[96,768]{1,0:T(8,128)}, f32[192,384]{1,0:T(8,128)}, f32[72,128]{1,0:T(8,128)}) custom-call(bf16[4,8,96,576]{3,2,1,0:T(8,128)(2,1)} %get-tuple-element.74.refs_0_, bf16[4,8,96,192]{3,2,1,0:T(8,128)(2,1)} %get-tuple-element.75.refs_1_, ...), custom_call_target="tpu_custom_call" | custom-call | tf_op jit(solution)/shard_map/reduce_gradients/pallas_call | solution.py:1122
  497.7 1.2 copy.200
  499.0 0.7 copy.201
  499.7 0.7 copy.202
  500.5 0.7 copy.203
  501.2 0.6 slice_bitcast_fusion.1
  501.8 0.6 slice_bitcast_fusion
  502.7 2.1 copy.199
  505.1 2.1 copy.198
  507.1 0.6 copy.404
  507.8 0.7 copy.405
  508.5 0.7 copy.406
  (155 shorter events, 2.3 us)
Async XLA Ops:
  0.7 4.6 copy-start.5
  7.3 1.1 copy-start
  7.3 1.1 copy-start.14
  7.4 1.1 copy-start.15
  7.8 2.0 copy-start.26
  7.8 2.3 copy-start.25
  7.9 3.8 copy-start.10
  7.9 3.9 copy-start.11
  8.5 3.4 copy-start.12
  9.7 89.8 %copy-start.19 = (f32[768]{0:T(1024)S(1)}, f32[768]{0:T(1024)}, u32[]{:S(2)}) copy-start(f32[768]{0:T(1024)} %param.30) | copy-start | bytes 9220
  9.7 89.9 %copy-start.20 = (f32[768]{0:T(1024)S(1)}, f32[768]{0:T(1024)}, u32[]{:S(2)}) copy-start(f32[768]{0:T(1024)} %param.27) | copy-start | bytes 9220
  218.0 19.4 %copy-start.2 = (f32[512,768]{1,0:T(8,128)S(1)}, f32[512,768]{1,0:T(8,128)}, u32[]{:S(2)}) copy-start(f32[512,768]{1,0:T(8,128)} %param.39) | copy-start | bytes 4718596
  238.7 0.7 copy-start.21
  238.7 1.4 copy-start.22
  238.8 2.0 copy-start.23
  238.8 2.6 copy-start.24
  239.1 2.9 copy-start.1
  388.1 12.3 %copy-start.17 = (f32[4,1,576]{2,1,0:T(1,128)S(1)}, f32[4,1,576]{2,1,0:T(1,128)}, u32[]{:S(2)}) copy-start(f32[4,1,576]{2,1,0:T(1,128)} %get-tuple-element.79) | copy-start | bytes 27652
  388.1 12.7 %copy-start.18 = (f32[8,768]{1,0:T(8,128)S(1)}, f32[8,768]{1,0:T(8,128)}, u32[]{:S(2)}) copy-start(f32[8,768]{1,0:T(8,128)} %get-tuple-element.80) | copy-start | bytes 73732
  388.1 12.8 %copy-start.16 = (f32[4,1,768]{2,1,0:T(1,128)S(1)}, f32[4,1,768]{2,1,0:T(1,128)}, u32[]{:S(2)}) copy-start(f32[4,1,768]{2,1,0:T(1,128)} %get-tuple-element.81) | copy-start | bytes 36868
  401.0 0.6 copy-start.13
  497.7 3.5 copy-start.9
  497.7 4.7 copy-start.4
  502.7 2.1 copy-start.3
  505.0 2.1 copy-start.8
  505.0 2.7 copy-start.7
  505.0 3.4 copy-start.6

commit v3 on v0

v3 whole, which is shorter than its diff:
```python
import functools
import math

import jax
import jax.numpy as jnp
from jax import lax
from jax.experimental import pallas as pl
from jax.experimental.pallas import tpu as pltpu
from jax.sharding import PartitionSpec as P

HEADS = 16

epsilon = 1e-05


NT = (((1,), (1,)), ((), ()))
NN = (((1,), (0,)), ((), ()))
f32 = jnp.float32
bf16 = jnp.bfloat16
BIG = 1e30
HD = 48
GROUP = 8
LANES = 128
BLOCK = 32
MSG = 160
FLAG = 2 * HD
MESH = pl.DeviceIdType.MESH
scale = HD ** (-0.5)
scale2 = scale * math.log2(math.e)
q_at = (0, 4096, 6144, 7168, 7680)
q_all = 7936
k_all = 9216


def reverse4(b):
    return (b & 1) * 8 + (b & 2) * 2 + (b & 4) // 2 + (b & 8) // 8


order = [reverse4(b) for b in range(16)]


def chunk_swap(head):
    return reverse4(head) >> 2


def block_swap(quad):
    return reverse4(4 * quad) & 3


def swap_blocks(rows, quad):
    return jnp.concatenate(
        [rows[BLOCK * (b ^ block_swap(quad)) :][:BLOCK] for b in range(16)], axis=0
    )


def swap_chunks(wide, head):
    return jnp.concatenate(
        [wide[:, LANES * (c ^ chunk_swap(head)) :][:, :LANES] for c in range(4)], axis=1
    )


def matmul(a, b, dims=NN):
    return lax.dot_general(a, b, dims, preferred_element_type=f32)


def column_sum(values):
    return jnp.sum(values, axis=0, keepdims=True)


def pick(ref, g):
    both = jnp.stack([ref[:, g], ref[:, g + 4]], axis=1)
    return both.reshape(768, ref.shape[3])


def put(ref, g, value):
    value = value.reshape(4, 2, 96, ref.shape[3])
    ref[:, g] = value[:, 0]
    ref[:, g + 4] = value[:, 1]


def vmem():
    return pl.BlockSpec(memory_space=pltpu.VMEM)


def anywhere():
    return pl.BlockSpec(memory_space=pl.ANY)


def sems(*dims):
    return pltpu.SemaphoreType.DMA(dims)


def params(identity=None):
    if identity is None:
        return pltpu.CompilerParams(vmem_limit_bytes=60 << 20)
    return pltpu.CompilerParams(
        vmem_limit_bytes=60 << 20, collective_id=identity, has_side_effects=True
    )


def shape(dims, dtype):
    return jax.ShapeDtypeStruct(dims, dtype)


def remote(src, dst, send_sem, recv_sem, target):
    return pltpu.make_async_remote_copy(
        src_ref=src, dst_ref=dst, send_sem=send_sem, recv_sem=recv_sem,
        device_id=target, device_id_type=MESH,
    )


class Spot:
    def __init__(self, grp):
        self.grp = grp
        self.linear = lax.axis_index("seq") * grp + lax.axis_index("grp")
        self.member = self.linear % GROUP
        self.base = self.linear - self.member
        self.layer = self.linear // GROUP % 4
        self.half = self.layer % 2

    def device(self, linear):
        return (linear // self.grp, linear % self.grp)

    def beside(self, j):
        return self.device(self.base + j)

    def over(self, layer):
        return self.device(self.linear + GROUP * (layer - self.layer))

    def pair(self):
        return self.device(self.linear + GROUP - 2 * GROUP * self.half)

    def greet(self):
        barrier = pltpu.get_barrier_semaphore()
        for j in range(GROUP):

            @pl.when(self.member != j)
            def _():
                pl.semaphore_signal(barrier, inc=1, device_id=self.beside(j), device_id_type=MESH)

        for o in range(1, 4):
            target = self.over((self.layer + o) % 4)
            pl.semaphore_signal(barrier, inc=1, device_id=target, device_id_type=MESH)
        return lambda: pl.semaphore_wait(barrier, GROUP + 2)


class Exchange:
    def __init__(self, spot, send, recv, send_sem, recv_sem):
        self.spot, self.send_ref, self.recv = spot, send, recv
        self.send_sem, self.recv_sem = send_sem, recv_sem

    def out(self, j):
        s = self.spot
        return remote(self.send_ref.at[j], self.recv.at[s.member], self.send_sem.at[j],
                      self.recv_sem.at[s.member], s.beside(j))

    def inner(self, j):
        return pltpu.make_async_copy(self.send_ref.at[j], self.recv.at[j], self.recv_sem.at[j])

    def choose(self, j, far, near):
        pl.when(self.spot.member != j)(far)
        pl.when(self.spot.member == j)(near)

    def send(self, j):
        self.choose(j, lambda: self.out(j).start(), lambda: self.inner(j).start())

    def wait(self, j):
        def far():
            remote(self.send_ref.at[j], self.recv.at[j], self.send_sem.at[j], self.recv_sem.at[j],
                   self.spot.beside(j)).wait_recv()

        self.choose(j, far, lambda: self.inner(j).wait())

    def drain(self):
        for j in range(GROUP):
            pl.when(self.spot.member != j)(lambda j=j: self.out(j).wait_send())


class Deep:
    def __init__(self, spot, eight, sixteen, send_sem, recv_sem):
        self.copies, self.waits = [], []
        s = spot
        for o in range(1, 4):
            other = (s.layer + o) % 4
            src, there, here = sixteen(o, other)
            self.copies.append(remote(src, there, send_sem.at[o], recv_sem.at[4 - o], s.over(other)))
            self.waits.append(remote(src, here, send_sem.at[o], recv_sem.at[o], s.over(other)))
        src, there, here = eight
        self.copies.append(remote(src, there, send_sem.at[0], recv_sem.at[0], s.pair()))
        self.waits.append(remote(src, here, send_sem.at[0], recv_sem.at[0], s.pair()))

    def start(self):
        for copy in self.copies:
            copy.start()

    def wait(self):
        for copy in self.waits:
            copy.wait_recv()

    def drain(self):
        for copy in self.copies:
            copy.wait_send()


def member_of(x, y, c):
    return x * 4 + y * 2 + c


def place():
    seq, col = lax.axis_index("seq"), lax.axis_index("grp")
    return seq // 2, seq % 2, col // 2, col % 2


def at_place(z, x, y, c):
    return (z * 2 + x, y * 2 + c)


def gather_sems(count):
    return [
        sems(count), sems(4, count), sems(4, count), sems(2, 4, count), sems(2, 4, count),
        sems(2, 4, count), sems(2, 4, count), sems(4, count), sems(4, count),
    ]


class Gather:
    def __init__(self, ins, outs, semaphores):
        self.ins, self.outs = ins, outs
        (self.loc, self.zs, self.zr, self.ps, self.pr,
         self.qs, self.qr, self.cs, self.cr) = semaphores
        self.place = z, x, y, c = place()
        self.me = member_of(x, y, c)
        self.arrays = range(len(ins))
        self.near = [(1 - x, y), (x, 1 - y)]
        self.started = []
        self.done = 0
        self.local = [
            pltpu.make_async_copy(ins[k], outs[k].at[z, self.me], self.loc.at[k])
            for k in self.arrays
        ]
        self.stages = [self.stage1, self.stage2, self.stage3, self.stage4, self.stage5, self.stage6]

    def go(self, copy):
        copy.start()
        self.started.append(copy)

    def start_layers(self):
        z, x, y, c = self.place
        for copy in self.local:
            copy.start()
        for o in (1, 2, 3):
            for k in self.arrays:
                self.go(remote(self.ins[k], self.outs[k].at[z, self.me], self.zs.at[o, k],
                               self.zr.at[4 - o, k], at_place((z + o) % 4, x, y, c)))

    def push(self, layer, slot, sources):
        z, x, y, c = self.place
        for p, (px, py) in enumerate(self.near):
            for k in self.arrays:
                self.go(remote(sources[k], self.outs[k].at[layer, self.me], self.ps.at[p, slot, k],
                               self.pr.at[p, slot, k], at_place(z, px, py, c)))

    def start_plane(self):
        self.push(self.place[0], 0, self.ins)

    def relay(self, slot):
        z, x, y, c = self.place
        layer = (z + slot) % 4
        for p, (px, py) in enumerate(self.near):
            m = member_of(px, py, c)
            for k in self.arrays:
                part = self.outs[k].at[layer, m]
                remote(part, part, self.ps.at[p, slot, k], self.pr.at[p, slot, k],
                       at_place(z, px, py, c)).wait_recv()
        for k in self.arrays:
            rows = self.ins[k].shape[0] // 2
            for p, (px, py) in enumerate(self.near):
                part = self.outs[k].at[layer, member_of(px, py, c), p * rows : (p + 1) * rows]
                self.go(remote(part, part, self.qs.at[p, slot, k], self.qr.at[p, slot, k],
                               at_place(z, *self.near[1 - p], c)))

    def layer_step(self, o):
        z, x, y, c = self.place
        layer = (z + o) % 4
        parts = [self.outs[k].at[layer, self.me] for k in self.arrays]
        for k in self.arrays:
            remote(parts[k], parts[k], self.zs.at[o, k], self.zr.at[o, k],
                   at_place(layer, x, y, c)).wait_recv()
        self.push(layer, o, parts)

    def stage1(self):
        for copy in self.local:
            copy.wait()
        self.layer_step(1)
        self.relay(0)

    def stage2(self):
        self.layer_step(2)
        self.relay(1)

    def stage3(self):
        self.layer_step(3)
        self.relay(2)

    def across(self, slot, px, py):
        z, x, y, c = self.place
        m = member_of(px, py, c)
        for k in self.arrays:
            part = self.outs[k].at[:, m]
            self.go(remote(part, part, self.cs.at[slot, k], self.cr.at[slot, k],
                           at_place(z, x, y, 1 - c)))

    def stage4(self):
        z, x, y, c = self.place
        self.across(0, x, y)
        self.relay(3)
        self.across(1, 1 - x, y)
        self.across(2, x, 1 - y)

    def stage5(self):
        z, x, y, c = self.place
        far = member_of(1 - x, 1 - y, c)
        for slot in range(4):
            layer = (z + slot) % 4
            for k in self.arrays:
                rows = self.ins[k].shape[0] // 2
                for p in range(2):
                    part = self.outs[k].at[layer, far, p * rows : (p + 1) * rows]
                    remote(part, part, self.qs.at[p, slot, k], self.qr.at[p, slot, k],
                           at_place(z, *self.near[1 - p], c)).wait_recv()
        self.across(3, 1 - x, 1 - y)

    def stage6(self):
        z, x, y, c = self.place
        for slot, (px, py) in enumerate([(x, y), (1 - x, y), (x, 1 - y), (1 - x, 1 - y)]):
            m = member_of(px, py, 1 - c)
            for k in self.arrays:
                part = self.outs[k].at[:, m]
                remote(part, part, self.cs.at[slot, k], self.cr.at[slot, k],
                       at_place(z, x, y, 1 - c)).wait_recv()

    def advance(self, upto):
        while self.done < upto:
            self.stages[self.done]()
            self.done += 1

    def finish(self):
        self.advance(6)

    def drain(self):
        for copy in self.started:
            copy.wait_send()


def reduce_scratch(dims):
    half = [(rows // 2, lanes) for rows, lanes in dims]
    count = len(dims)
    return (
        [pltpu.VMEM((4, 4) + d, bf16) for d in dims]
        + [pltpu.VMEM((4, 4) + d, bf16) for d in dims]
        + [pltpu.VMEM((4, 4) + d, bf16) for d in half]
        + [pltpu.VMEM((2, 4) + d, bf16) for d in half]
        + [pltpu.VMEM((4,) + d, bf16) for d in dims]
        + [sems(4, count), sems(4, count), sems(4, count)]
        + [sems(3, count) for _ in range(4)]
        + [sems(4, count), sems(4, count)]
    )


def add_to(target, source):
    def step(i, _):
        target[i] = (target[i].astype(f32) + source[i].astype(f32)).astype(bf16)
        return 0

    lax.fori_loop(0, 4, step, 0)


class Reduce:
    def __init__(self, ins, outs, scratch):
        count = len(ins)
        self.ins, self.outs, self.arrays = ins, outs, range(count)
        self.own, self.across, self.one, self.two, self.deep = [
            scratch[i * count : (i + 1) * count] for i in range(5)
        ]
        (self.loc, self.cs, self.cr, self.xs, self.xr, self.ys, self.yr, self.zs, self.zr) = scratch[
            5 * count :
        ]
        self.place = z, x, y, c = place()
        self.mine, self.px, self.py, self.far = (x, y), (1 - x, y), (x, 1 - y), (1 - x, 1 - y)
        self.other = at_place(z, x, y, 1 - c)
        self.to_x, self.to_y = at_place(z, *self.px, c), at_place(z, *self.py, c)
        self.started = []
        self.done = 0
        self.stages = [self.stage1, self.stage2, self.stage3, self.stage4, self.stage5, self.stage6]

    def slot(self, p):
        return p[0] * 2 + p[1]

    def go(self, copy):
        copy.start()
        self.started.append(copy)

    def theirs(self, n, p, k):
        c = self.place[3]
        return remote(self.ins[k].at[:, member_of(*p, 1 - c)], self.across[k].at[self.slot(p)],
                      self.cs.at[n, k], self.cr.at[n, k], self.other)

    def ours(self, n, p, k):
        c = self.place[3]
        return pltpu.make_async_copy(self.ins[k].at[:, member_of(*p, c)],
                                     self.own[k].at[self.slot(p)], self.loc.at[n, k])

    def start(self):
        for n, p in enumerate((self.far, self.px, self.py, self.mine)):
            for k in self.arrays:
                self.go(self.theirs(n, p, k))
                self.ours(n, p, k).start()

    def landed(self, n, p):
        for k in self.arrays:
            self.ours(n, p, k).wait()
            self.theirs(n, p, k).wait_recv()
            add_to(self.own[k].at[self.slot(p)], self.across[k].at[self.slot(p)])

    def part(self, k, p, along_x):
        rows = self.ins[k].shape[2] // 2
        at = 0 if along_x else rows
        return self.own[k].at[self.slot(p), :, at : at + rows]

    def hop(self, k, p, along_x, i, target):
        source = self.part(k, p, along_x)
        if along_x:
            return remote(source, target, self.xs.at[i, k], self.xr.at[i, k], self.to_x)
        return remote(source, target, self.ys.at[i, k], self.yr.at[i, k], self.to_y)

    def first(self, k, p, along_x):
        i = 0 if p is self.far else 1
        return self.hop(k, p, along_x, i, self.one[k].at[2 * i + (0 if along_x else 1)])

    def second(self, k, along_x):
        if along_x:
            return remote(self.part(k, self.py, True), self.two[k].at[0], self.ys.at[2, k],
                          self.yr.at[2, k], self.to_y)
        return remote(self.part(k, self.px, False), self.two[k].at[1], self.xs.at[2, k],
                      self.xr.at[2, k], self.to_x)

    def stage1(self):
        self.landed(0, self.far)
        for k in self.arrays:
            self.go(self.first(k, self.far, True))
            self.go(self.first(k, self.far, False))

    def stage2(self):
        self.landed(1, self.px)
        for k in self.arrays:
            self.go(self.first(k, self.px, True))
        self.landed(2, self.py)
        for k in self.arrays:
            self.go(self.first(k, self.py, False))

    def stage3(self):
        self.landed(3, self.mine)
        for k in self.arrays:
            for along_x, p in ((True, self.py), (False, self.px)):
                self.first(k, self.far, along_x).wait_recv()
                add_to(self.part(k, p, along_x), self.one[k].at[0 if along_x else 1])
                self.go(self.second(k, along_x))

    def stage4(self):
        for k in self.arrays:
            for along_x, p in ((True, self.px), (False, self.py)):
                self.first(k, p, along_x).wait_recv()
                add_to(self.part(k, self.mine, along_x), self.one[k].at[2 if along_x else 3])

    def last(self, k, o):
        z, x, y, c = self.place
        layer = (z + o) % 4
        return remote(self.own[k].at[self.slot(self.mine), layer], self.deep[k].at[4 - o],
                      self.zs.at[o, k], self.zr.at[4 - o, k], at_place(layer, x, y, c))

    def stage5(self):
        for k in self.arrays:
            for along_x in (True, False):
                self.second(k, along_x).wait_recv()
                add_to(self.part(k, self.mine, along_x), self.two[k].at[0 if along_x else 1])
            for o in (1, 2, 3):
                self.go(self.last(k, o))

    def stage6(self):
        z, x, y, c = self.place
        for k in self.arrays:
            value = self.own[k][self.slot(self.mine), z].astype(f32)
            for o in (1, 2, 3):
                here = self.deep[k].at[o]
                remote(here, here, self.zs.at[o, k], self.zr.at[o, k],
                       at_place((z + o) % 4, x, y, c)).wait_recv()
                value = value + self.deep[k][o].astype(f32)
            self.outs[k][...] = value

    def advance(self, upto):
        while self.done < upto:
            self.stages[self.done]()
            self.done += 1

    def drain(self):
        for copy in self.started:
            copy.wait_send()


class Total:
    def __init__(self, small, out, scratch):
        self.small, self.out = small, out
        self.at_c, self.at_p, self.at_z, self.ss, self.rs = scratch
        self.place = z, x, y, c = place()
        self.plane = ((1 - x, y), (x, 1 - y), (1 - x, 1 - y))
        self.started = []

    def swap(self, buffer, index, n, m, target):
        here = buffer.at[index]
        copy = remote(here, here, self.ss.at[n], self.rs.at[m], target)
        copy.start()
        self.started.append(copy)

    def arrive(self, buffer, index, n, target):
        here = buffer.at[index]
        remote(here, here, self.ss.at[n], self.rs.at[n], target).wait_recv()

    def start(self):
        z, x, y, c = self.place
        self.at_c[c] = self.small[...]
        self.swap(self.at_c, c, 0, 0, at_place(z, x, y, 1 - c))

    def middle(self):
        z, x, y, c = self.place
        self.arrive(self.at_c, 1 - c, 0, at_place(z, x, y, 1 - c))
        self.at_p[x * 2 + y] = self.at_c[0] + self.at_c[1]
        for n, p in enumerate(self.plane):
            self.swap(self.at_p, x * 2 + y, 1 + n, 1 + n, at_place(z, *p, c))

    def late(self):
        z, x, y, c = self.place
        for n, p in enumerate(self.plane):
            self.arrive(self.at_p, p[0] * 2 + p[1], 1 + n, at_place(z, *p, c))
        self.at_z[z] = (self.at_p[0] + self.at_p[1]) + (self.at_p[2] + self.at_p[3])
        for o in (1, 2, 3):
            self.swap(self.at_z, z, 3 + o, 7 - o, at_place((z + o) % 4, x, y, c))

    def finish(self):
        z, x, y, c = self.place
        for o in (1, 2, 3):
            self.arrive(self.at_z, (z + o) % 4, 3 + o, at_place((z + o) % 4, x, y, c))
        self.out[...] = (self.at_z[0] + self.at_z[1]) + (self.at_z[2] + self.at_z[3])
        for copy in self.started:
            copy.wait_send()


def block_barrier():
    z, x, y, c = place()
    barrier = pltpu.get_barrier_semaphore()
    near = [at_place((z + o) % 4, x, y, c) for o in (1, 2, 3)]
    near += [at_place(z, 1 - x, y, c), at_place(z, x, 1 - y, c), at_place(z, 1 - x, 1 - y, c)]
    near += [at_place(z, x, y, 1 - c)]
    for target in near:
        pl.semaphore_signal(barrier, inc=1, device_id=target, device_id_type=MESH)
    pl.semaphore_wait(barrier, len(near))


def total_scratch(dims):
    return [
        pltpu.VMEM((2,) + dims, f32), pltpu.VMEM((4,) + dims, f32), pltpu.VMEM((4,) + dims, f32),
        sems(7), sems(7),
    ]


def reduce_kernel(count, *refs):
    ins, small = refs[:count], refs[count]
    outs, total = refs[count + 1 : 2 * count + 1], refs[2 * count + 1]
    scratch = refs[2 * count + 2 :]
    block_barrier()
    sums = Reduce(ins, outs, scratch[:-5])
    rest = Total(small, total, scratch[-5:])
    rest.start()
    sums.start()
    sums.advance(1)
    rest.middle()
    sums.advance(3)
    rest.late()
    sums.advance(6)
    rest.finish()
    sums.drain()


def reduce_gradients(parts, small, identity):
    count = len(parts)
    dims = [part.shape[2:] for part in parts]
    return pl.pallas_call(
        functools.partial(reduce_kernel, count),
        name="reduce_gradients",
        in_specs=[anywhere()] * count + [vmem()],
        out_specs=[vmem()] * (count + 1),
        out_shape=[shape(d, f32) for d in dims] + [shape(small.shape, f32)],
        scratch_shapes=reduce_scratch(dims) + total_scratch(small.shape),
        compiler_params=params(identity),
    )(*parts, small)


def norm_parts(values):
    average = jnp.mean(values, axis=-1, keepdims=True)
    centred = values - average
    variance = jnp.mean(centred * centred, axis=-1, keepdims=True)
    inverse = lax.rsqrt(variance + epsilon)
    return centred * inverse, inverse


def norm_backward(hat, inverse, gain, grad):
    scaled = grad * gain
    first = jnp.mean(scaled, axis=-1, keepdims=True)
    second = jnp.mean(scaled * hat, axis=-1, keepdims=True)
    return (scaled - first - hat * second) * inverse


def compact(j, rows, packed, places):
    for place, size in places:
        packed[place + size * j : place + size * j + size] = rows[:size]


def widen(pieces):
    total = pieces[-1]
    for piece in reversed(pieces[:-1]):
        blank = jnp.zeros((piece.shape[0], piece.shape[1] - total.shape[1]), f32)
        total = piece + jnp.concatenate([total, blank], axis=1)
    return total


def join_quad(quad, read):
    wide = jnp.concatenate(
        [swap_chunks(read(4 * quad + i), 4 * quad + i) for i in range(4)], axis=0
    )
    return swap_blocks(wide.T, quad)


def join_quads(read):
    pairs = []
    for half in range(2):
        pairs.append(
            jnp.concatenate([join_quad(quad, read) for quad in (2 * half, 2 * half + 1)], axis=1)
        )
    return jnp.concatenate(pairs, axis=1)


def unit_forward(query, key, out):
    lane = lax.broadcasted_iota(jnp.int32, (256, LANES), 1)
    count = len(query)
    scores = [matmul(query[i](), key, NT) for i in range(count)]
    for i in range(count):
        top = jnp.max(scores[i], axis=1, keepdims=True) * scale2
        prob = jnp.exp2(scores[i] * scale2 - top).astype(bf16)
        value = jnp.where(lane == FLAG + 8, top, matmul(prob, key))
        out[i](value.T[HD : HD + 64])


def forward_kernel(grp, slides, gather, *refs):
    refs = list(refs)
    take = lambda n: [refs.pop(0) for _ in range(n)]
    tokens, coordinates, frequency, gain, shift, flags_ref, bias = take(7)
    shards = take(4) if gather else None
    (weight_in,) = (None,) if gather else take(1)
    base, msg, q_ref, kv_ref, kv8, kv16, stat, merged = take(8)
    gathered = take(4) if gather else None
    weight = gathered[0] if gather else weight_in
    send, osend, orecv, acc, qc, kvc, tok_sem, ss, rs, os_, or_, ds, dr = take(13)
    spot = Spot(grp)
    joined = spot.greet()
    loads = [
        pltpu.make_async_copy(
            tokens.at[:, order[b]], base.at[BLOCK * b : BLOCK * b + BLOCK], tok_sem.at[b]
        )
        for b in range(16)
    ]
    for copy in loads:
        copy.start()
    if gather:
        first = Gather(shards[:1], gathered[:1], take(9))
        rest = Gather(shards[1:], gathered[1:], take(9))
        joined()
        first.start_layers()
        first.start_plane()
        rest.start_layers()
    lane = lax.broadcasted_iota(jnp.int32, (512, 384), 1)
    angle = jnp.where(lane < 192, coordinates[:, 0:1], coordinates[:, 1:2]) * frequency[...]
    sine, cosine = jnp.sin(angle), jnp.cos(angle)
    table = jnp.concatenate(
        [
            jnp.concatenate([sine[:, :192], cosine[:, :192]], axis=1),
            jnp.concatenate([sine[:, 192:], cosine[:, 192:]], axis=1),
        ],
        axis=1,
    )
    for copy in loads:
        copy.wait()
    base[...] = base[...] + table
    hat, _ = norm_parts(base[...])
    normed = (hat * gain[...] + shift[...]).astype(bf16)
    if gather:
        first.finish()
    else:
        joined()
    plane = [Exchange(spot, send.at[i], msg.at[i], ss.at[i], rs.at[i]) for i in range(2)]
    for quad in range(4):
        part = matmul(normed, pick(weight, quad)) + bias[quad]
        wide = swap_blocks(part.astype(bf16), quad).T
        flags = flags_ref[...]
        flags = jnp.concatenate(
            [flags[:, BLOCK * (b ^ block_swap(quad)) :][:, :BLOCK] for b in range(16)], axis=1
        ).astype(bf16)
        for inner in (0, 2, 1, 3):
            head = 4 * quad + inner
            owner, i = head // 2, head % 2
            own = swap_chunks(wide[144 * inner : 144 * inner + 144], head)
            send[i, owner, :96] = own[48:]
            send[i, owner, 96:112] = swap_chunks(flags, head)
            send[i, owner, 112:] = own[:48]
            if i == 0:
                plane[0].send(owner)
    for owner in range(GROUP):
        plane[1].send(owner)
    row = lax.broadcasted_iota(jnp.int32, (16, 512), 0)
    deeps = []
    results = [Exchange(spot, osend.at[i], orecv.at[i], os_.at[i], or_.at[i]) for i in range(2)]
    if gather:
        rest.start_plane()
    for i in range(2):
        q, kv = q_ref.at[i], kv_ref.at[i]
        for j in range(GROUP):
            plane[i].wait(j)
            block = msg[i, j]
            key_part = jnp.concatenate([block[:112], jnp.zeros((16, 512), bf16)], axis=0).T
            flags = block[96:112].astype(f32)
            chosen = jnp.where(
                row == 0, 1.0, jnp.where((row <= slides) & (flags == 0.0), 1.0, 0.0)
            )
            query_part = jnp.concatenate(
                [block[112:], jnp.zeros((HD, 512), bf16), chosen.astype(bf16),
                 jnp.zeros((16, 512), bf16)],
                axis=0,
            ).T
            kv[512 * j : 512 * j + 512] = key_part
            q[512 * j : 512 * j + 512] = query_part
            compact(j, query_part, qc, ((0, 256), (2048, 128), (3072, 64), (3584, 32)))
            compact(j, key_part, kvc, ((0, 256), (2048, 128)))
            kv8[spot.half, i, 64 * j : 64 * j + 64] = key_part[:64]
            kv16[spot.layer, i, 32 * j : 32 * j + 32] = key_part[:32]
        own8, own16 = kv8.at[spot.half, i], kv16.at[spot.layer, i]
        deep = Deep(
            spot, (own8, own8, kv8.at[1 - spot.half, i]),
            lambda o, other: (own16, own16, kv16.at[other, i]), ds.at[i], dr.at[i],
        )
        deep.start()
        deeps.append(deep)
        if gather:
            rest.advance(1 + 2 * i)

        def unit(source, q_from, keys, k_from, out_from, count):
            def reader(n):
                return lambda: source[pl.ds(q_from + 256 * n, 256)]

            def writer(n):
                def save(value):
                    acc[:, pl.ds(out_from + 256 * n, 256)] = value

                return save

            unit_forward(
                [reader(n) for n in range(count)], keys[pl.ds(k_from, 1024)],
                [writer(n) for n in range(count)],
            )

        def early(u, _):
            at = pl.multiple_of(u * 1024, 1024)
            unit(q, at, kv, at, at, 4)
            return 0

        lax.fori_loop(0, 4, early, 0)
        if gather:
            rest.advance(2 + 2 * i)

        def late(u, _):
            at = pl.multiple_of(u * 1024, 1024)
            unit(qc, at, kvc, at, pl.multiple_of(at + 4096, 1024), 4)
            return 0

        lax.fori_loop(0, 3, late, 0)
        deep.wait()
        for n in range(2):
            kvc[3072 + 512 * n : 3584 + 512 * n] = kv8[n, i]
        for n in range(4):
            kvc[4096 + 256 * n : 4352 + 256 * n] = kv16[n, i]
        unit(qc, 3072, kvc, 3072, 7168, 2)
        unit(qc, 3584, kvc, 4096, 7680, 1)
        place = lax.broadcasted_iota(jnp.int32, (1, 512), 1)
        uses = jnp.where(place < 32, 5.0, jnp.where(place < 64, 4.0, jnp.where(
            place < 128, 3.0, jnp.where(place < 256, 2.0, 1.0))))
        for j in range(GROUP):
            key = msg[i, j, :HD].astype(f32)
            value = msg[i, j, HD : 2 * HD].astype(f32)
            query = msg[i, j, 112:].astype(f32)
            dropped = msg[i, j, FLAG : FLAG + 1].astype(f32) != 0.0
            own = jnp.where(dropped, column_sum(query * key) * scale2 + jnp.log2(uses), -BIG)
            pieces = [
                acc[:, q_at[r] + (512 >> r) * j : q_at[r] + (512 >> r) * (j + 1)] for r in range(5)
            ]
            top = own
            tops = [piece[HD + 8 : HD + 9] for piece in pieces]
            for item in tops:
                spread = item
                if spread.shape[1] < 512:
                    blank = jnp.full((1, 512 - spread.shape[1]), -BIG, f32)
                    spread = jnp.concatenate([spread, blank], axis=1)
                top = jnp.maximum(top, spread)
            scaled = [
                piece[: HD + 8] * jnp.exp2(item - top[:, : item.shape[1]])
                for piece, item in zip(pieces, tops)
            ]
            mix = widen(scaled)
            weight_own = jnp.exp2(own - top)
            total = mix[HD + 1 + slides : HD + 2 + slides] + weight_own
            result = (mix[:HD] + weight_own * value) / total
            stat[i, j, :HD] = result
            stat[i, j, HD : HD + 8] = jnp.broadcast_to(top + jnp.log2(total), (8, 512))
            osend[i, j] = result.astype(bf16)
            results[i].send(j)
    if gather:
        rest.advance(5)
    for i in range(2):
        for j in range(GROUP):
            results[i].wait(j)
    merged[...] = join_quads(lambda h: orecv[h % 2, h // 2])
    if gather:
        rest.finish()
        first.drain()
        rest.drain()
    for item in plane + deeps + results:
        item.drain()


def attention_forward(grp, slides, gather, inputs, weights):
    out_shape = [
        shape((512, 768), f32),
        shape((2, GROUP, MSG, 512), bf16),
        shape((2, 4096, LANES), bf16),
        shape((2, 4096, LANES), bf16),
        shape((2, 2, 512, LANES), bf16),
        shape((4, 2, 256, LANES), bf16),
        shape((2, GROUP, 56, 512), f32),
        shape((512, 768), bf16),
    ]
    out_specs = [vmem()] * 8
    in_specs = [anywhere()] + [vmem()] * 6
    extra = []
    if gather:
        in_specs += [anywhere()] * 4
        out_shape += [shape((4, GROUP) + w.shape, bf16) for w in weights]
        out_specs += [vmem()] + [anywhere()] * 3
        extra = gather_sems(1) + gather_sems(3)
    else:
        in_specs += [vmem()]
    return pl.pallas_call(
        functools.partial(forward_kernel, grp, slides, gather),
        name="attention_forward",
        in_specs=in_specs,
        out_specs=out_specs,
        out_shape=out_shape,
        scratch_shapes=[
            pltpu.VMEM((2, GROUP, MSG, 512), bf16),
            pltpu.VMEM((2, GROUP, HD, 512), bf16),
            pltpu.VMEM((2, GROUP, HD, 512), bf16),
            pltpu.VMEM((64, q_all), f32),
            pltpu.VMEM((q_all - 4096, LANES), bf16),
            pltpu.VMEM((k_all - 4096, LANES), bf16),
            sems(16),
            sems(2, GROUP), sems(2, GROUP), sems(2, GROUP), sems(2, GROUP), sems(2, 4), sems(2, 4),
        ] + extra,
        compiler_params=params(1),
    )(*inputs, *weights)


def dense_kernel(
    merged, base, cot, wo, wi, wt, out_bias, gain, shift, in_bias, last_bias,
    out, grad_middle, grad_merged, wo_grad, wi_grad, wt_grad, small, small_in,
    full, middle, hat, low, low_t, cot_low, cot_t, grad_low,
):
    for g in range(0, 4, 2):
        pair = [pick(wo, g + i) for i in range(2)]
        full[:, 192 * g : 192 * g + 384] = jnp.concatenate(pair, axis=1)
    middle[...] = base[...] + matmul(merged[...], full[...]) + out_bias[...]
    normal, inverse = norm_parts(middle[...])
    hat[...] = normal
    low[...] = (normal * gain[...] + shift[...]).astype(bf16)
    low_t[...] = low[...].T
    cot_low[...] = cot[...].astype(bf16)
    cot_t[...] = cot_low[...].T
    out[...] = middle[...] + last_bias[...]
    small[0:1] = column_sum(cot_low[...].astype(f32))
    grad_middle[...] = jnp.zeros((512, 768), f32)

    def chunk(g, _):
        weight = pick(wi, g)
        inner = matmul(low[...], weight) + in_bias[g]
        phi = 0.5 * (1.0 + lax.erf(inner * 0.7071067811865476))
        active = (inner * phi).astype(bf16)
        slope = phi + inner * jnp.exp(-0.5 * inner * inner) * 0.3989422804014327
        for x in range(2):
            part = wt[g, 4 * x : 4 * x + 4].reshape(768, 384)
            now = active[:, 384 * x : 384 * x + 384]
            out[...] += matmul(now, part, NT)
            wt_grad[g, 4 * x : 4 * x + 4] = (
                matmul(cot_t[...], now).astype(bf16).reshape(4, 192, 384)
            )
            back = matmul(cot_low[...], part)
            grad_low[:, 384 * x : 384 * x + 384] = (
                back * slope[:, 384 * x : 384 * x + 384]
            ).astype(bf16)
        small_in[g] = column_sum(grad_low[...].astype(f32))
        put(wi_grad, g, matmul(low_t[...], grad_low[...]).astype(bf16))
        grad_middle[...] += matmul(grad_low[...], weight, NT)
        return 0

    lax.fori_loop(0, 4, chunk, 0)
    grad = grad_middle[...]
    small[1:2] = column_sum(grad * hat[...])
    small[2:3] = column_sum(grad)
    grad = cot[...] + norm_backward(hat[...], inverse, gain[...], grad)
    grad_middle[...] = grad
    attended = grad.astype(bf16)
    small[3:4] = column_sum(attended.astype(f32))
    small[4:8] = jnp.zeros((4, 768), f32)
    grads = matmul(merged[...].T, attended).astype(bf16)
    for g in range(4):
        put(wo_grad, g, grads[:, 192 * g : 192 * g + 192])
    grad_merged[...] = matmul(attended, full[...], NT).astype(bf16)


def dense(merged, base, cot, wo, wi, wt, out_bias, gain, shift, in_bias, last_bias):
    rows = (512, 768)
    return pl.pallas_call(
        dense_kernel,
        name="dense",
        in_specs=[vmem()] * 11,
        out_specs=[vmem()] * 8,
        out_shape=[
            shape(rows, f32), shape(rows, f32), shape(rows, bf16),
            shape((4, GROUP, 96, 192), bf16), shape((4, GROUP, 96, 768), bf16),
            shape((4, GROUP, 192, 384), bf16), shape((8, 768), f32), shape((4, 1, 768), f32),
        ],
        scratch_shapes=[
            pltpu.VMEM((768, 768), bf16), pltpu.VMEM(rows, f32), pltpu.VMEM(rows, f32),
            pltpu.VMEM(rows, bf16), pltpu.VMEM((768, 512), bf16), pltpu.VMEM(rows, bf16),
            pltpu.VMEM((768, 512), bf16), pltpu.VMEM(rows, bf16),
        ],
        compiler_params=params(),
    )(merged, base, cot, wo, wi, wt, out_bias, gain, shift, in_bias, last_bias)


def final_kernel(
    base, grad_middle, d0, d1, d2, d3, weight, gain, shift, token_grad, grads_out, small,
):
    hat, inverse = norm_parts(base[...])
    low_t = (hat * gain[...] + shift[...]).astype(bf16).T
    grad = jnp.zeros((512, 768), f32)
    small[...] = jnp.zeros((8, 768), f32)
    for quad, part in enumerate((d0, d1, d2, d3)):
        now = part[...]
        put(grads_out, quad, matmul(low_t, now).astype(bf16))
        grad = grad + matmul(now, pick(weight, quad), NT)
    small[0:1] = column_sum(grad * hat)
    small[1:2] = column_sum(grad)
    token_grad[...] = grad_middle[...] + norm_backward(hat, inverse, gain[...], grad)


def final(base, grad_middle, quads, weight, gain, shift):
    rows = (512, 768)
    return pl.pallas_call(
        final_kernel,
        name="input_gradients",
        in_specs=[vmem()] * 9,
        out_specs=[vmem()] * 3,
        out_shape=[shape(rows, f32), shape((4, GROUP, 96, 576), bf16), shape((8, 768), f32)],
        compiler_params=params(),
    )(base, grad_middle, *quads, weight, gain, shift)


def backward_kernel(grp, reduce, *refs):
    refs = list(refs)
    take = lambda n: [refs.pop(0) for _ in range(n)]
    gm, q_ref, kv_ref, kv8, kv16, msg, stat = take(7)
    parts = take(3) if reduce else None
    outs, sums_ref = take(4), take(1)[0]
    reduced = take(3) if reduce else None
    (gsend, grecv, rsend, rrecv, got8, got16, send8, send16, qc, kvc, dor, kt, ld, dkv, dqt,
     gs, gr, ss, rs, ds, dr) = take(21)
    spot = Spot(grp)
    joined = spot.greet()
    shares = [Exchange(spot, gsend.at[i], grecv.at[i], gs.at[i], gr.at[i]) for i in range(2)]
    backs = [Exchange(spot, rsend.at[i], rrecv.at[i], ss.at[i], rs.at[i]) for i in range(2)]
    sums = Reduce(parts, reduced, refs) if reduce else None
    for quad in range(4):
        wide = swap_blocks(gm[:, 192 * quad : 192 * quad + 192], quad).T
        for inner in (0, 2, 1, 3):
            head = 4 * quad + inner
            i = head % 2
            gsend[i, head // 2] = swap_chunks(wide[HD * inner : HD * inner + HD], head)
            if quad == 0 and inner == 0:
                joined()
            if i == 0:
                shares[0].send(head // 2)
    for j in range(GROUP):
        shares[1].send(j)
    if reduce:
        sums.start()
    row = lax.broadcasted_iota(jnp.int32, (96, 1), 0)
    factor = jnp.where(row < HD, scale, 1.0)
    deeps = []
    for i in range(2):
        q, kv = q_ref.at[i], kv_ref.at[i]
        for n in range(2):
            kvc[3072 + 512 * n : 3584 + 512 * n] = kv8[n, i]
        for n in range(4):
            kvc[4096 + 256 * n : 4352 + 256 * n] = kv16[n, i]
        for n in range(2):
            kt[7 + n] = kvc[3072 + 1024 * n : 4096 + 1024 * n].T[:HD]
        rows = []
        for j in range(GROUP):
            compact(j, q[512 * j : 512 * j + 512], qc, ((0, 256), (2048, 128), (3072, 64), (3584, 32)))
            compact(j, kv[512 * j : 512 * j + 512], kvc, ((0, 256), (2048, 128)))
            key = msg[i, j, :HD]
            kt[j // 2, :, 512 * (j % 2) : 512 * (j % 2) + 512] = key
            kt[4 + j // 4, :, 256 * (j % 4) : 256 * (j % 4) + 256] = key[:, :256]
            kt[6, :, 128 * j : 128 * j + 128] = key[:, :128]
        for j in range(GROUP):
            shares[i].wait(j)
            grad = grecv[i, j]
            delta = column_sum(grad.astype(f32) * stat[i, j, :HD])
            both = jnp.concatenate(
                [stat[i, j, HD : HD + 1], delta, jnp.zeros((6, 512), f32)], axis=0
            )
            rows.append(both)
            ld[:, 512 * j : 512 * j + 512] = both
            ld[:, 4096 + 256 * j : 4352 + 256 * j] = both[:, :256]
            ld[:, 6144 + 128 * j : 6272 + 128 * j] = both[:, :128]
            tall = jnp.concatenate(
                [jnp.zeros((HD, 512), bf16), grad, jnp.zeros((32, 512), bf16)], axis=0
            ).T
            for r, at in enumerate(q_at):
                size = 512 >> r
                dor[at + size * j : at + size * j + size] = tall[:size]
        ld[:, 7168:7680] = jnp.concatenate([both[:, :64] for both in rows], axis=1)
        ld[:, 7680:7936] = jnp.concatenate([both[:, :32] for both in rows], axis=1)

        def unit(source, q_from, keys, k_from, at, seg, count):
            width = 256 * count
            query = source[pl.ds(q_from, width)]
            grad = dor[pl.ds(at, width)]
            total = ld[0:1, pl.ds(at, width)]
            delta = ld[1:2, pl.ds(at, width)]
            sides = jnp.concatenate([grad, query], axis=0)
            size = 256
            dq = jnp.zeros((HD, width), f32)
            for c in range(1024 // size):
                key = keys[pl.ds(k_from + size * c, size)]
                prob = jnp.exp2(matmul(key, query, NT) * scale2 - total)
                slope = (prob * (matmul(key, grad, NT) - delta)).astype(bf16)
                both = jnp.concatenate([prob.astype(bf16), slope], axis=1)
                dkv[pl.ds(seg * 1024 + size * c, size)] = matmul(both, sides)
                dq = dq + matmul(kt[seg, :, size * c : size * c + size], slope)
            dqt[:, pl.ds(at, width)] = dq

        unit(qc, 3072, kvc, 3072, 7168, 7, 2)
        unit(qc, 3584, kvc, 4096, 7680, 8, 1)
        for n in range(2):
            send8[n, i] = dkv[7168 + 512 * n : 7680 + 512 * n].astype(bf16)
        for n in range(4):
            send16[n, i] = dkv[8192 + 256 * n : 8448 + 256 * n].astype(bf16)
        deep = Deep(
            spot, (send8.at[1 - spot.half, i], got8.at[i], got8.at[i]),
            lambda o, other: (send16.at[other, i], got16.at[4 - o, i], got16.at[o, i]),
            ds.at[i], dr.at[i],
        )
        deep.start()
        deeps.append(deep)
        if reduce:
            sums.advance(1 + 2 * i)

        def early(u, _):
            at = pl.multiple_of(u * 1024, 1024)
            unit(q, at, kv, at, at, u, 4)
            return 0

        lax.fori_loop(0, 4, early, 0)
        if reduce:
            sums.advance(2 + 2 * i)

        def late(u, _):
            at = pl.multiple_of(u * 1024, 1024)
            unit(qc, at, kvc, at, pl.multiple_of(at + 4096, 1024), u + 4, 4)
            return 0

        lax.fori_loop(0, 3, late, 0)
        deep.wait()
        spot_lane = lax.broadcasted_iota(jnp.int32, (1, 512), 1)
        uses = jnp.where(spot_lane < 32, 5.0, jnp.where(spot_lane < 64, 4.0, jnp.where(
            spot_lane < 128, 3.0, jnp.where(spot_lane < 256, 2.0, 1.0))))
        for j in range(GROUP):
            tall = dkv[512 * j : 512 * j + 512]
            eight = send8[spot.half, i, 64 * j : 64 * j + 64].astype(f32) + got8[
                i, 64 * j : 64 * j + 64
            ].astype(f32)
            sixteen = send16[spot.layer, i, 32 * j : 32 * j + 32].astype(f32)
            for o in range(1, 4):
                sixteen = sixteen + got16[o, i, 32 * j : 32 * j + 32].astype(f32)
            second = dkv[4096 + 256 * j : 4352 + 256 * j]
            third = dkv[6144 + 128 * j : 6272 + 128 * j]
            fourth = third[:64] + eight
            fourth = jnp.concatenate([fourth[:32] + sixteen, fourth[32:]], axis=0)
            third = jnp.concatenate([fourth, third[64:]], axis=0)
            second = jnp.concatenate([second[:128] + third, second[128:]], axis=0)
            wide = jnp.concatenate([tall[:256] + second, tall[256:]], axis=0).T
            key = msg[i, j, :HD].astype(f32)
            value = msg[i, j, HD : 2 * HD].astype(f32)
            query = msg[i, j, 112:].astype(f32)
            grad = grecv[i, j].astype(f32)
            total = ld[0:1, 512 * j : 512 * j + 512]
            delta = ld[1:2, 512 * j : 512 * j + 512]
            dropped = msg[i, j, FLAG : FLAG + 1].astype(f32) != 0.0
            dots = column_sum(query * key) * scale2 - total
            prob = jnp.where(dropped, uses * jnp.exp2(jnp.where(dropped, dots, 0.0)), 0.0)
            slope = prob * (column_sum(grad * value) - delta)
            dq = widen([dqt[:, at + (512 >> r) * j : at + (512 >> r) * (j + 1)]
                        for r, at in enumerate(q_at)])
            rsend[i, j, :HD] = ((wide[:HD] + slope * query) * scale).astype(bf16)
            rsend[i, j, HD : 2 * HD] = (wide[HD : 2 * HD] + prob * grad).astype(bf16)
            rsend[i, j, 2 * HD :] = ((dq + slope * key) * scale).astype(bf16)
            backs[i].send(j)
    if reduce:
        sums.advance(5)
    for i in range(2):
        for j in range(GROUP):
            backs[i].wait(j)
    for quad, out in enumerate(outs):

        def read(head):
            block = rrecv[head % 2, head // 2]
            return jnp.concatenate([block[2 * HD :], block[: 2 * HD]], axis=0)

        result = join_quad(quad, read)
        out[...] = result
        sums_ref[quad] = column_sum(result.astype(f32))
    if reduce:
        sums.advance(6)
        sums.drain()
    for item in shares + backs + deeps:
        item.drain()


def attention_backward(grp, reduce, inputs, parts):
    out_shape = [shape((512, 576), bf16)] * 4 + [shape((4, 1, 576), f32)]
    extra = []
    if reduce:
        dims = [part.shape[2:] for part in parts]
        out_shape += [shape(d, f32) for d in dims]
        extra = reduce_scratch(dims)
    return pl.pallas_call(
        functools.partial(backward_kernel, grp, reduce),
        name="attention_backward",
        in_specs=[vmem()] * 7 + [anywhere()] * len(parts),
        out_specs=[vmem()] * len(out_shape),
        out_shape=out_shape,
        scratch_shapes=[
            pltpu.VMEM((2, GROUP, HD, 512), bf16),
            pltpu.VMEM((2, GROUP, HD, 512), bf16),
            pltpu.VMEM((2, GROUP, 3 * HD, 512), bf16),
            pltpu.VMEM((2, GROUP, 3 * HD, 512), bf16),
            pltpu.VMEM((2, 512, LANES), bf16),
            pltpu.VMEM((4, 2, 256, LANES), bf16),
            pltpu.VMEM((2, 2, 512, LANES), bf16),
            pltpu.VMEM((4, 2, 256, LANES), bf16),
            pltpu.VMEM((q_all - 4096, LANES), bf16),
            pltpu.VMEM((k_all - 4096, LANES), bf16),
            pltpu.VMEM((q_all, LANES), bf16),
            pltpu.VMEM((9, HD, 1024), bf16),
            pltpu.VMEM((8, q_all), f32),
            pltpu.VMEM((k_all, LANES), f32),
            pltpu.VMEM((HD, q_all), f32),
            sems(2, GROUP), sems(2, GROUP), sems(2, GROUP), sems(2, GROUP), sems(2, 4), sems(2, 4),
        ] + extra,
        compiler_params=params(2),
    )(*inputs, *parts)


def all_weights(parts, seq, grp):
    gathered = []
    for n, part in enumerate(parts):
        whole = lax.all_gather(lax.all_gather(part, "grp"), "seq")
        lead = whole.shape[0] // 8
        whole = whole.reshape((8, lead) + whole.shape[1:])
        if n == 3:
            whole = whole.transpose(0, 2, 3, 1, 4)
            whole = whole.reshape(4, GROUP, part.shape[0], lead * part.shape[1])
        else:
            whole = whole.transpose(0, 2, 1, 3, 4)
            whole = whole.reshape(4, GROUP, lead * part.shape[0], part.shape[1])
        gathered.append(whole)
    return gathered


def sum_gradients(parts, small, seq, grp):
    lead = seq // 8
    sums = []
    for n, part in enumerate(parts):
        height, lanes = part.shape[2:]
        whole = part.reshape(8, grp, height, lanes)
        if n == 3:
            whole = whole.reshape(8, grp, height, lead, lanes // lead).transpose(0, 3, 1, 2, 4)
        else:
            whole = whole.reshape(8, grp, lead, height // lead, lanes).transpose(0, 2, 1, 3, 4)
        whole = whole.reshape((seq, grp) + whole.shape[3:]).astype(f32)
        whole = lax.psum_scatter(whole, "seq", scatter_dimension=0)
        sums.append(lax.psum_scatter(whole, "grp", scatter_dimension=0))
    return sums + [lax.psum(small, ("seq", "grp"))]


def in_order(rows):
    split = rows.reshape((BLOCK, 16) + rows.shape[1:])
    return jnp.stack([split[:, b] for b in order]).reshape(rows.shape)


def back_order(rows):
    split = rows.reshape((16, BLOCK) + rows.shape[1:])
    return jnp.stack([split[b] for b in order], axis=1).reshape(rows.shape)


def body(
    tokens,
    coordinates,
    lengths,
    valid,
    first_gain,
    first_shift,
    query_weight,
    query_bias,
    key_weight,
    value_weight,
    value_bias,
    output_weight,
    output_bias,
    second_gain,
    second_shift,
    inner_weight,
    inner_bias,
    outer_weight,
    outer_bias,
    cotangent,
):
    rows, width = tokens.shape
    grp = lax.axis_size("grp")
    seq = lax.axis_size("seq")
    near = (seq, grp) == (8, 4)
    slides = lengths.shape[0]
    linear = lax.axis_index("seq") * grp + lax.axis_index("grp")
    shard = query_weight.shape[0]
    heads = [w.reshape(shard, 4, 1, HD) for w in (query_weight, key_weight, value_weight)]
    parts = [
        jnp.concatenate(heads, axis=2).reshape(shard, 576),
        output_weight,
        inner_weight,
        outer_weight.T,
    ]
    joint_bias = jnp.stack(
        [b.reshape(4, 4, HD) for b in (query_bias, jnp.zeros_like(query_bias), value_bias)], axis=2
    ).reshape(4, 1, 576)
    cotangent = in_order(cotangent)
    places = in_order(linear * rows + jnp.arange(rows, dtype=jnp.int32))
    keep = in_order(valid)
    slide = jnp.sum((places[:, None] >= jnp.cumsum(lengths)).astype(jnp.int32), axis=-1)
    apart = slide[None, :] != jnp.arange(slides, dtype=jnp.int32)[:, None]
    flags = jnp.concatenate(
        [
            jnp.where(keep == 1, 0.0, -BIG)[None, :],
            jnp.where(apart, -BIG, 0.0),
            jnp.ones((1, rows), f32),
            jnp.zeros((14 - slides, rows), f32),
        ],
        axis=0,
    )
    frequency = jnp.exp(jnp.arange(192, dtype=jnp.float32) * (-math.log(10000.0) / 192))
    row = lambda v: v.reshape(1, -1)
    inputs = [
        tokens.reshape(BLOCK, 16, width), in_order(coordinates).astype(f32),
        row(jnp.concatenate([frequency, frequency])), row(first_gain), row(first_shift), flags,
        joint_bias,
    ]
    if near:
        results = attention_forward(grp, slides, True, inputs, parts)
        joint_weight, wo, wi, wt = results[8:]
    else:
        joint_weight, wo, wi, wt = all_weights(parts, seq, grp)
        results = attention_forward(grp, slides, False, inputs, [joint_weight])
    base, msg, q_rows, kv_rows, kv8, kv16, stat, merged_low = results[:8]
    output, grad_middle, grad_merged, wo_grad, wi_grad, wt_grad, small, small_in = dense(
        merged_low, base, cotangent, wo, wi, wt, row(output_bias), row(second_gain),
        row(second_shift), inner_bias.reshape(4, 1, 768), row(outer_bias),
    )
    saved = [grad_merged, q_rows, kv_rows, kv8, kv16, msg, stat]
    late = [wo_grad, wi_grad, wt_grad]
    results = attention_backward(grp, near, saved, late if near else [])
    quads, sums = results[:4], results[4]
    token_grad, joint_grad, first_small = final(
        base, grad_middle, quads, joint_weight, row(first_gain), row(first_shift)
    )
    sums = sums.reshape(4, 4, 3, HD)
    vectors = [
        first_small[0], first_small[1], sums[:, :, 0].reshape(-1), sums[:, :, 2].reshape(-1),
        small[3], small[1], small[2], small_in.reshape(-1), small[0],
    ]
    sizes = [v.shape[0] for v in vectors]
    pack = jnp.concatenate(vectors).reshape(-1, LANES)
    if near:
        sum_output, sum_inner, sum_outer = results[5:]
        joint_sum, pack = reduce_gradients([joint_grad], pack, 3)
    else:
        joint_sum, sum_output, sum_inner, sum_outer, pack = sum_gradients(
            [joint_grad] + late, pack, seq, grp
        )
    joint_sum = joint_sum.reshape(shard, 4, 3, HD)
    sum_query, sum_key, sum_value = [joint_sum[:, :, i].reshape(shard, 192) for i in range(3)]
    sum_outer = sum_outer.T
    small = []
    pack = pack.reshape(-1)
    for size in sizes:
        small.append(pack[:size])
        pack = pack[size:]
    return (
        back_order(output),
        back_order(token_grad),
        small[0],
        small[1],
        sum_query,
        small[2],
        sum_key,
        sum_value,
        small[3],
        sum_output,
        small[4],
        small[5],
        small[6],
        sum_inner,
        small[7],
        sum_outer,
        small[8],
    )


def solution(mesh):
    placed = (
        P(("seq", "grp"), None),
        P(("seq", "grp"), None),
        P(),
        P(("seq", "grp")),
        P(),
        P(),
        P("seq", "grp"),
        P(),
        P("seq", "grp"),
        P("seq", "grp"),
        P(),
        P("seq", "grp"),
        P(),
        P(),
        P(),
        P("seq", "grp"),
        P(),
        P("seq", "grp"),
        P(),
        P(("seq", "grp"), None),
    )
    return jax.shard_map(
        body,
        mesh=mesh,
        in_specs=placed,
        out_specs=(
            P(("seq", "grp"), None),
            P(("seq", "grp"), None),
            P(),
            P(),
            P("seq", "grp"),
            P(),
            P("seq", "grp"),
            P("seq", "grp"),
            P(),
            P("seq", "grp"),
            P(),
            P(),
            P(),
            P("seq", "grp"),
            P(),
            P("seq", "grp"),
            P(),
        ),
        check_vma=False,
    )
```

time: 2370 us -> 362 us (0.15)
  waiting for transfers between devices: 691 us -> 0 us
  local copies, waits for them, and re-layouts: 646 us -> 26.1 us
  matrix products: 611 us -> 0 us
  Pallas kernels: 0 us -> 325 us
  other arithmetic: 245 us -> 1.89 us
  blocking collectives: 80.8 us -> 0 us
  starting transfers between devices: 58.9 us -> 0 us
    dot_general x128 -> x0, matrix products: 611 us -> none  [the longest x16 141 us: block_backward(): jnp.einsum('hij,hix->hjx', grad_scores, query_block, preferred_element_ty...]
    reduce_scatter x8 -> x0, waiting for transfers between devices: 377 us -> none  [the longest x1 80.7 us: body(): lax.psum_scatter(outer_weight_grad, 'grp', scatter_dimension=1, tiled=True)]
    pallas_call x0 -> x5, Pallas kernels: none -> 325 us  [the longest x1 127 us: attention_forward(): pl.pallas_call(functools.partial(forward_kernel, grp, slides, gather), na...]
    broadcast_in_dim x162 -> x1, local copies, waits for them, and re-layouts: 325 us -> 0.01 us  [body(): jnp.zeros((14 - slides, rows), f32)]
    unnamed x22 -> x0, waiting for transfers between devices: 205 us -> none
    another operation x42 -> x14, local copies, waits for them, and re-layouts: 120 us -> 4.71 us  [the longest x4 4.13 us: back_order(): return jnp.stack([split[b] for b in order], axis=1).reshape(rows.shape)]
    ppermute x75 -> x0, waiting for transfers between devices: 108 us -> none  [swapped(): return lax.ppermute(value, axis, pairs)]
    select_n x87 -> x2, other arithmetic: 86.2 us -> 0.01 us  [the longest x1 0.01 us: body(): jnp.where(apart, -BIG, 0.0)]
  transfers between devices with their start and end apart: 93 -> 0, of which waited for: 26 -> 0; matrix products, arithmetic and copies ran while one was open for 44% -> 0% of each run, Pallas kernels for 0% -> 0%
where the time goes in v3:
time: 362 us; the launch traced here: 355 us
  Pallas kernels  325 us (90%)
  local copies, waits for them, and re-layouts  26.1 us (7%)
    pallas_call x1, Pallas kernels, attention_forward(): pl.pallas_call(functools.partial(forward_kernel, grp, slides, gather), na...  127 us
    pallas_call x1, Pallas kernels, attention_backward(): pl.pallas_call(functools.partial(backward_kernel, grp, reduce), name='att...  115 us
    pallas_call x1, Pallas kernels, reduce_gradients(): pl.pallas_call(functools.partial(reduce_kernel, count), name='reduce_grad...  39.3 us
    pallas_call x1, Pallas kernels, dense(): pl.pallas_call(dense_kernel, name='dense', in_specs=[vmem()] * 11, out_sp...  31.6 us
    pallas_call x1, Pallas kernels, final(): pl.pallas_call(final_kernel, name='input_gradients', in_specs=[vmem()] *...  11.4 us

profile of v3, /device:TPU:0, one launch (start us, length us, event | category | flops | bytes accessed | tf_op | source)
XLA Modules:
  0.0 354.9 jit_solution(2258652203870228483)
XLA Ops:
  0.8 0.1 ge.15
  0.9 0.8 reduce-window.8
  1.7 0.1 convert_reduce_fusion
  1.8 0.8 reshape.245
  2.6 0.5 slice_reduce_fusion.16
  3.1 0.1 select_n.19
  3.2 0.1 pad.9.clone
  3.4 0.7 maximum_maximum_fusion.refs_5_
  4.0 0.8 reshape.241
  4.8 0.8 slice_reduce_fusion
  5.7 0.9 copy.176
  6.6 1.3 reshape.243.refs_3_.gain
  7.9 0.6 reshape.244.refs_4_.shift
  8.4 0.1 copy.177
  8.6 0.1 copy.178
  8.7 0.1 copy.179
  8.9 0.8 copy.182.refs_7_
  9.7 0.1 stack_reshape.11
  9.8 0.1 stack_reshape.9
  9.9 0.1 pad_maximum_fusion.1
  10.0 0.7 reshape.266.refs_6_
  10.7 0.1 pad_maximum_fusion.2
  10.8 0.6 reshape.242.refs_2_
  11.4 127.2 %attention_forward.1 = (f32[512,768]{1,0:T(8,128)}, bf16[2,8,160,512]{3,2,1,0:T(8,128)(2,1)}, bf16[2,4096,128]{2,1,0:T(8,128)(2,1)}, bf16[2,4096,128]{2,1,0:T(8,...) custom-call(f32[32,16,768]{2,1,0:T(8,128)} %bitcast.268, ...), custom_call_target="tpu_custom_call" | custom-call | tf_op jit(solution)/shard_map/attention_forward/pallas_call | solution.py:866
  138.6 1.4 fusion.1
  140.4 0.4 copy-done.18
  140.7 0.7 reshape.255.out_bias
  141.4 0.6 reshape.256.gain
  142.0 0.6 reshape.257.shift
  142.6 0.6 reshape.259.last_bias
  143.2 31.6 %dense.1 = (f32[512,768]{1,0:T(8,128)}, f32[512,768]{1,0:T(8,128)}, bf16[512,768]{1,0:T(8,128)(2,1)}, bf16[4,8,96,192]{3,2,1,0:T(8,128)(2,1)}, bf16[4,8,96,768]{...) custom-call(bf16[512,768]{1,0:T(8,128)(2,1)} %get-tuple-element.50.merged, ...), custom_call_target="tpu_custom_call" | custom-call | tf_op jit(solution)/shard_map/dense/pallas_call | solution.py:944
  174.8 115.4 %attention_backward.1 = (bf16[512,576]{1,0:T(8,128)(2,1)}, bf16[512,576]{1,0:T(8,128)(2,1)}, bf16[512,576]{1,0:T(8,128)(2,1)}, bf16[512,576]{1,0:T(8,128)(2,1)},...) custom-call(bf16[512,768]{1,0:T(8,128)(2,1)} %get-tuple-element.57.refs_0_, ...), custom_call_target="tpu_custom_call" | custom-call | tf_op jit(solution)/shard_map/attention_backward/pallas_call | solution.py:1170
  290.3 11.4 %input_gradients.1 = (f32[512,768]{1,0:T(8,128)}, bf16[4,8,96,576]{3,2,1,0:T(8,128)(2,1)}, f32[8,768]{1,0:T(8,128)}) custom-call(f32[512,768]{1,0:T(8,128)} %get-tuple-element.51.base, f32[512,768]{1,0:T(8,128)} %get-tuple-element.56.grad_middle, bf16[512,576]{1,0:T(8,128)(2,1)} %get-tuple-element.67.d0, bf16[512,576]{1,0:T(8,128)(2,1)} %get-tuple-element.68.d1, ...), custom_call_target="tpu_custom_call" | custom-call | tf_op jit(solution)/shard_map/input_gradients/pallas_call | solution.py:981
  301.7 0.8 slice_reduce_fusion.38
  302.7 0.1 reshape.262
  303.1 0.6 copy-done.11
  303.8 39.3 %reduce_gradients.1 = (f32[96,576]{1,0:T(8,128)}, f32[72,128]{1,0:T(8,128)}) custom-call(bf16[4,8,96,576]{3,2,1,0:T(8,128)(2,1)} %get-tuple-element.73.refs_0_, f32[72,128]{1,0:T(8,128)} %bitcast.283), custom_call_target="tpu_custom_call" | custom-call | tf_op jit(solution)/shard_map/reduce_gradients/pallas_call | solution.py:595
  343.0 1.2 copy.201
  344.3 0.7 copy.202
  345.0 0.7 copy.203
  345.7 0.7 copy.204
  346.5 0.6 slice_bitcast_fusion.1
  347.1 0.6 slice_bitcast_fusion
  348.0 2.1 copy.200
  350.4 2.1 copy.199
  352.4 0.6 copy.326
  353.1 0.7 copy.327
  353.8 0.7 copy.328
  (120 shorter events, 1.3 us)
Async XLA Ops:
  0.7 7.2 %copy-start.17 = (f32[768]{0:T(1024)S(1)}, f32[768]{0:T(1024)}, u32[]{:S(2)}) copy-start(f32[768]{0:T(1024)} %param.25) | copy-start | bytes 9220
  0.7 7.8 %copy-start.8 = (bf16[96,192]{1,0:T(8,128)(2,1)S(1)}, bf16[96,192]{1,0:T(8,128)(2,1)}, u32[]{:S(2)}) copy-start(bf16[96,192]{1,0:T(8,128)(2,1)} %param.26) | copy-start | bytes 110596
  0.7 7.9 %copy-start.9 = (bf16[96,192]{1,0:T(8,128)(2,1)S(1)}, bf16[96,192]{1,0:T(8,128)(2,1)}, u32[]{:S(2)}) copy-start(bf16[96,192]{1,0:T(8,128)(2,1)} %param.28) | copy-start | bytes 110596
  0.7 8.0 %copy-start.10 = (bf16[96,192]{1,0:T(8,128)(2,1)S(1)}, bf16[96,192]{1,0:T(8,128)(2,1)}, u32[]{:S(2)}) copy-start(bf16[96,192]{1,0:T(8,128)(2,1)} %param.29) | copy-start | bytes 110596
  0.7 9.0 %copy-start.15 = (f32[768]{0:T(1024)S(1)}, f32[768]{0:T(1024)}, u32[]{:S(2)}) copy-start(f32[768]{0:T(1024)} %param.30) | copy-start | bytes 9220
  0.7 9.0 %copy-start.16 = (f32[768]{0:T(1024)S(1)}, f32[768]{0:T(1024)}, u32[]{:S(2)}) copy-start(f32[768]{0:T(1024)} %param.27) | copy-start | bytes 9220
  8.8 129.8 %copy-start.1 = (f32[512,768]{1,0:T(8,128)S(1)}, f32[512,768]{1,0:T(8,128)}, u32[]{:S(2)}) copy-start(f32[512,768]{1,0:T(8,128)} %param.39) | copy-start | bytes 4718596
  140.0 0.7 copy-start.18
  140.0 1.4 copy-start.19
  140.0 2.0 copy-start.20
  140.1 2.6 copy-start.21
  140.3 2.9 copy-start
  290.3 12.4 %copy-start.13 = (f32[4,1,576]{2,1,0:T(1,128)S(1)}, f32[4,1,576]{2,1,0:T(1,128)}, u32[]{:S(2)}) copy-start(f32[4,1,576]{2,1,0:T(1,128)} %get-tuple-element.75) | copy-start | bytes 27652
  290.3 12.7 %copy-start.14 = (f32[8,768]{1,0:T(8,128)S(1)}, f32[8,768]{1,0:T(8,128)}, u32[]{:S(2)}) copy-start(f32[8,768]{1,0:T(8,128)} %get-tuple-element.76) | copy-start | bytes 73732
  290.3 12.8 %copy-start.12 = (f32[4,1,768]{2,1,0:T(1,128)S(1)}, f32[4,1,768]{2,1,0:T(1,128)}, u32[]{:S(2)}) copy-start(f32[4,1,768]{2,1,0:T(1,128)} %get-tuple-element.77) | copy-start | bytes 36868
  303.1 0.6 copy-start.11
  343.0 3.5 copy-start.7
  343.0 4.7 %copy-start.3 = (f32[512,768]{1,0:T(8,128)S(1)}, f32[512,768]{1,0:T(8,128)}, u32[]{:S(2)}) copy-start(f32[512,768]{1,0:T(8,128)} %get-tuple-element.72) | copy-start | bytes 4718596
  348.0 2.1 copy-start.2
  350.3 2.1 copy-start.6
  350.3 2.7 copy-start.5
  350.3 3.4 copy-start.4

commit v4 on v3

--- a/solution.py
+++ b/solution.py
@@ -7,8 +7,6 @@
 from jax.experimental import pallas as pl
 from jax.experimental.pallas import tpu as pltpu
 from jax.sharding import PartitionSpec as P
-
-HEADS = 16
 
 epsilon = 1e-05
 
@@ -351,11 +349,113 @@
             copy.wait_send()
 
 
+def gather_wide_sems():
+    return [sems(1), sems(2), sems(2), sems(2), sems(2), sems(4, 4), sems(4, 4), sems(4, 4), sems(4, 4)]
+
+
+class GatherWide:
+    def __init__(self, source, out, semaphores):
+        self.source, self.out = source, out
+        (self.loc, self.ps, self.pr, self.qs, self.qr, self.zs, self.zr, self.cs, self.cr) = semaphores
+        self.place = z, x, y, c = place()
+        self.near = [(1 - x, y), (x, 1 - y)]
+        self.spots = [(x, y), (1 - x, y), (x, 1 - y), (1 - x, 1 - y)]
+        self.started = []
+        self.done = 0
+        self.stages = [self.stage1, self.stage2, self.stage3, self.stage4, self.stage5]
+
+    def go(self, copy):
+        copy.start()
+        self.started.append(copy)
+
+    def block(self, layer, p, c):
+        return self.out.at[layer, member_of(*p, c)]
+
+    def start(self):
+        z, x, y, c = self.place
+        self.local = pltpu.make_async_copy(self.source, self.block(z, (x, y), c), self.loc.at[0])
+        self.local.start()
+        for n, p in enumerate(self.near):
+            self.go(remote(self.source, self.block(z, (x, y), c), self.ps.at[n], self.pr.at[n],
+                           at_place(z, *p, c)))
+
+    def up(self, slot):
+        z, x, y, c = self.place
+        part = self.block(z, self.spots[slot], c)
+        for o in (1, 2, 3):
+            self.go(remote(part, part, self.zs.at[o, slot], self.zr.at[4 - o, slot],
+                           at_place((z + o) % 4, x, y, c)))
+
+    def swap(self, o, slot):
+        z, x, y, c = self.place
+        part = self.block((z + o) % 4, self.spots[slot], c)
+        self.go(remote(part, part, self.cs.at[o, slot], self.cr.at[o, slot],
+                       at_place(z, x, y, 1 - c)))
+
+    def stage1(self):
+        z, x, y, c = self.place
+        self.local.wait()
+        self.up(0)
+        self.swap(0, 0)
+        rows = self.source.shape[0] // 2
+        for n, p in enumerate(self.near):
+            part = self.block(z, p, c)
+            remote(part, part, self.ps.at[n], self.pr.at[n], at_place(z, *p, c)).wait_recv()
+            part = self.out.at[z, member_of(*p, c), n * rows : (n + 1) * rows]
+            self.go(remote(part, part, self.qs.at[n], self.qr.at[n],
+                           at_place(z, *self.near[1 - n], c)))
+            self.up(1 + n)
+            self.swap(0, 1 + n)
+
+    def stage2(self):
+        z, x, y, c = self.place
+        rows = self.source.shape[0] // 2
+        for n in range(2):
+            part = self.out.at[z, member_of(*self.spots[3], c), n * rows : (n + 1) * rows]
+            remote(part, part, self.qs.at[n], self.qr.at[n],
+                   at_place(z, *self.near[1 - n], c)).wait_recv()
+        self.up(3)
+        self.swap(0, 3)
+
+    def arrive(self, slots):
+        z, x, y, c = self.place
+        for slot in slots:
+            for o in (1, 2, 3):
+                layer = (z + o) % 4
+                part = self.block(layer, self.spots[slot], c)
+                remote(part, part, self.zs.at[o, slot], self.zr.at[o, slot],
+                       at_place(layer, x, y, c)).wait_recv()
+                self.swap(o, slot)
+
+    def stage3(self):
+        self.arrive((0, 1))
+
+    def stage4(self):
+        self.arrive((2, 3))
+
+    def stage5(self):
+        z, x, y, c = self.place
+        for o in range(4):
+            for slot in range(4):
+                part = self.block((z + o) % 4, self.spots[slot], 1 - c)
+                remote(part, part, self.cs.at[o, slot], self.cr.at[o, slot],
+                       at_place(z, x, y, 1 - c)).wait_recv()
+
+    def advance(self, upto):
+        while self.done < upto:
+            self.stages[self.done]()
+            self.done += 1
+
+    def drain(self):
+        for copy in self.started:
+            copy.wait_send()
+
+
 def reduce_scratch(dims):
     half = [(rows // 2, lanes) for rows, lanes in dims]
     count = len(dims)
     return (
-        [pltpu.VMEM((4, 4) + d, bf16) for d in dims]
+        [pltpu.VMEM((4,) + d, bf16) for d in dims]
         + [pltpu.VMEM((4, 4) + d, bf16) for d in dims]
         + [pltpu.VMEM((4, 4) + d, bf16) for d in half]
         + [pltpu.VMEM((2, 4) + d, bf16) for d in half]
@@ -378,7 +478,7 @@
     def __init__(self, ins, outs, scratch):
         count = len(ins)
         self.ins, self.outs, self.arrays = ins, outs, range(count)
-        self.own, self.across, self.one, self.two, self.deep = [
+        self.stage, self.across, self.one, self.two, self.deep = [
             scratch[i * count : (i + 1) * count] for i in range(5)
         ]
         (self.loc, self.cs, self.cr, self.xs, self.xr, self.ys, self.yr, self.zs, self.zr) = scratch[
@@ -395,6 +495,11 @@
     def slot(self, p):
         return p[0] * 2 + p[1]
 
+    def held(self, k, p):
+        if self.stage[k] is None:
+            return self.ins[k].at[:, member_of(*p, self.place[3])]
+        return self.across[k].at[self.slot(p)]
+
     def go(self, copy):
         copy.start()
         self.started.append(copy)
@@ -407,24 +512,30 @@
     def ours(self, n, p, k):
         c = self.place[3]
         return pltpu.make_async_copy(self.ins[k].at[:, member_of(*p, c)],
-                                     self.own[k].at[self.slot(p)], self.loc.at[n, k])
+                                     self.stage[k], self.loc.at[n, k])
 
     def start(self):
         for n, p in enumerate((self.far, self.px, self.py, self.mine)):
             for k in self.arrays:
                 self.go(self.theirs(n, p, k))
-                self.ours(n, p, k).start()
+                if n == 0 and self.stage[k] is not None:
+                    self.ours(n, p, k).start()
 
     def landed(self, n, p):
         for k in self.arrays:
+            self.theirs(n, p, k).wait_recv()
+            if self.stage[k] is None:
+                add_to(self.held(k, p), self.across[k].at[self.slot(p)])
+                continue
             self.ours(n, p, k).wait()
-            self.theirs(n, p, k).wait_recv()
-            add_to(self.own[k].at[self.slot(p)], self.across[k].at[self.slot(p)])
+            add_to(self.held(k, p), self.stage[k])
+            if n < 3:
+                self.ours(n + 1, (self.far, self.px, self.py, self.mine)[n + 1], k).start()
 
     def part(self, k, p, along_x):
         rows = self.ins[k].shape[2] // 2
         at = 0 if along_x else rows
-        return self.own[k].at[self.slot(p), :, at : at + rows]
+        return self.held(k, p).at[:, at : at + rows]
 
     def hop(self, k, p, along_x, i, target):
         source = self.part(k, p, along_x)
@@ -474,7 +585,7 @@
     def last(self, k, o):
         z, x, y, c = self.place
         layer = (z + o) % 4
-        return remote(self.own[k].at[self.slot(self.mine), layer], self.deep[k].at[4 - o],
+        return remote(self.held(k, self.mine).at[layer], self.deep[k].at[4 - o],
                       self.zs.at[o, k], self.zr.at[4 - o, k], at_place(layer, x, y, c))
 
     def stage5(self):
@@ -488,7 +599,7 @@
     def stage6(self):
         z, x, y, c = self.place
         for k in self.arrays:
-            value = self.own[k][self.slot(self.mine), z].astype(f32)
+            value = self.held(k, self.mine)[z].astype(f32)
             for o in (1, 2, 3):
                 here = self.deep[k].at[o]
                 remote(here, here, self.zs.at[o, k], self.zr.at[o, k],
@@ -553,17 +664,6 @@
             copy.wait_send()
 
 
-def block_barrier():
-    z, x, y, c = place()
-    barrier = pltpu.get_barrier_semaphore()
-    near = [at_place((z + o) % 4, x, y, c) for o in (1, 2, 3)]
-    near += [at_place(z, 1 - x, y, c), at_place(z, x, 1 - y, c), at_place(z, 1 - x, 1 - y, c)]
-    near += [at_place(z, x, y, 1 - c)]
-    for target in near:
-        pl.semaphore_signal(barrier, inc=1, device_id=target, device_id_type=MESH)
-    pl.semaphore_wait(barrier, len(near))
-
-
 def total_scratch(dims):
     return [
         pltpu.VMEM((2,) + dims, f32), pltpu.VMEM((4,) + dims, f32), pltpu.VMEM((4,) + dims, f32),
@@ -571,36 +671,134 @@
     ]
 
 
-def reduce_kernel(count, *refs):
-    ins, small = refs[:count], refs[count]
-    outs, total = refs[count + 1 : 2 * count + 1], refs[2 * count + 1]
-    scratch = refs[2 * count + 2 :]
-    block_barrier()
-    sums = Reduce(ins, outs, scratch[:-5])
-    rest = Total(small, total, scratch[-5:])
-    rest.start()
-    sums.start()
-    sums.advance(1)
-    rest.middle()
-    sums.advance(3)
-    rest.late()
-    sums.advance(6)
-    rest.finish()
-    sums.drain()
-
-
-def reduce_gradients(parts, small, identity):
-    count = len(parts)
-    dims = [part.shape[2:] for part in parts]
-    return pl.pallas_call(
-        functools.partial(reduce_kernel, count),
-        name="reduce_gradients",
-        in_specs=[anywhere()] * count + [vmem()],
-        out_specs=[vmem()] * (count + 1),
-        out_shape=[shape(d, f32) for d in dims] + [shape(small.shape, f32)],
-        scratch_shapes=reduce_scratch(dims) + total_scratch(small.shape),
-        compiler_params=params(identity),
-    )(*parts, small)
+def reduce_wide_scratch(dims):
+    rows, lanes = dims
+    return [
+        pltpu.VMEM((4,) + dims, bf16), pltpu.VMEM((4, 4) + dims, bf16),
+        pltpu.VMEM((4, 4) + dims, bf16), pltpu.VMEM((4, rows // 2, lanes), bf16),
+        pltpu.VMEM((2, rows // 2, lanes), bf16),
+        sems(4), sems(4), sems(4), sems(4, 4), sems(4, 4), sems(4), sems(4), sems(2), sems(2),
+    ]
+
+
+class ReduceWide:
+    def __init__(self, source, out, scratch):
+        self.source, self.out = source, out
+        (self.stage, self.own, self.deep, self.one, self.two, self.loc, self.cs, self.cr, self.zs,
+         self.zr, self.ps, self.pr, self.qs, self.qr) = scratch
+        self.place = z, x, y, c = place()
+        self.spots = [(x, y), (1 - x, y), (x, 1 - y), (1 - x, 1 - y)]
+        self.other = at_place(z, x, y, 1 - c)
+        self.to_x, self.to_y = at_place(z, 1 - x, y, c), at_place(z, x, 1 - y, c)
+        self.rows = source.shape[2] // 2
+        self.started = []
+        self.done = 0
+        self.stages = [self.stage1, self.stage2, self.stage3, self.stage4, self.stage5, self.stage6]
+
+    def go(self, copy):
+        copy.start()
+        self.started.append(copy)
+
+    def theirs(self, n):
+        c = self.place[3]
+        return remote(self.source.at[:, member_of(*self.spots[n], 1 - c)], self.own.at[n],
+                      self.cs.at[n], self.cr.at[n], self.other)
+
+    def ours(self, n):
+        c = self.place[3]
+        return pltpu.make_async_copy(self.source.at[:, member_of(*self.spots[n], c)],
+                                     self.stage, self.loc.at[n])
+
+    def start(self):
+        for n in range(4):
+            self.go(self.theirs(n))
+        self.ours(0).start()
+
+    def landed(self, n):
+        z, x, y, c = self.place
+        self.ours(n).wait()
+        self.theirs(n).wait_recv()
+        add_to(self.own.at[n], self.stage)
+        if n < 3:
+            self.ours(n + 1).start()
+        for o in (1, 2, 3):
+            layer = (z + o) % 4
+            self.go(remote(self.own.at[n, layer], self.deep.at[n, 4 - o], self.zs.at[o, n],
+                           self.zr.at[4 - o, n], at_place(layer, x, y, c)))
+
+    def stage1(self):
+        self.landed(0)
+        self.landed(1)
+
+    def stage2(self):
+        self.landed(2)
+        self.landed(3)
+
+    def gathered(self, n):
+        z, x, y, c = self.place
+        total = self.own[n, z].astype(f32)
+        for o in (1, 2, 3):
+            here = self.deep.at[n, o]
+            remote(here, here, self.zs.at[o, n], self.zr.at[o, n],
+                   at_place((z + o) % 4, x, y, c)).wait_recv()
+            total = total + self.deep[n, o].astype(f32)
+        self.own[n, z] = total.astype(bf16)
+
+    def part(self, n, along_x):
+        at = 0 if along_x else self.rows
+        return self.own.at[n, self.place[0], at : at + self.rows]
+
+    def first(self, i):
+        n, along_x = ((3, True), (3, False), (1, True), (2, False))[i]
+        return remote(self.part(n, along_x), self.one.at[i], self.ps.at[i], self.pr.at[i],
+                      self.to_x if along_x else self.to_y)
+
+    def second(self, along_x):
+        if along_x:
+            return remote(self.part(2, True), self.two.at[0], self.qs.at[0], self.qr.at[0], self.to_y)
+        return remote(self.part(1, False), self.two.at[1], self.qs.at[1], self.qr.at[1], self.to_x)
+
+    def add(self, n, along_x, source):
+        at = 0 if along_x else self.rows
+        z = self.place[0]
+        rows = slice(at, at + self.rows)
+        self.own[n, z, rows] = (
+            self.own[n, z, rows].astype(f32) + source[...].astype(f32)
+        ).astype(bf16)
+
+    def stage3(self):
+        for n in (0, 1, 2, 3):
+            self.gathered(n)
+        for i in range(4):
+            self.go(self.first(i))
+
+    def stage4(self):
+        for i, (n, along_x) in enumerate(((2, True), (1, False))):
+            self.first(i).wait_recv()
+            self.add(n, along_x, self.one.at[i])
+            self.go(self.second(along_x))
+
+    def stage5(self):
+        for i, along_x in ((2, True), (3, False)):
+            self.first(i).wait_recv()
+            self.add(0, along_x, self.one.at[i])
+
+    def stage6(self):
+        z = self.place[0]
+        for i, along_x in ((0, True), (1, False)):
+            self.second(along_x).wait_recv()
+            at = 0 if along_x else self.rows
+            rows = slice(at, at + self.rows)
+            self.out[rows] = self.own[0, z, rows].astype(f32) + self.two[i].astype(f32)
+
+    def advance(self, upto):
+        while self.done < upto:
+            self.stages[self.done]()
+            self.done += 1
+
+    def drain(self):
+        for copy in self.started:
+            copy.wait_send()
 
 
 def norm_parts(values):
@@ -661,32 +859,64 @@
 def forward_kernel(grp, slides, gather, *refs):
     refs = list(refs)
     take = lambda n: [refs.pop(0) for _ in range(n)]
-    tokens, coordinates, frequency, gain, shift, flags_ref, bias = take(7)
-    shards = take(4) if gather else None
-    (weight_in,) = (None,) if gather else take(1)
-    base, msg, q_ref, kv_ref, kv8, kv16, stat, merged = take(8)
-    gathered = take(4) if gather else None
-    weight = gathered[0] if gather else weight_in
+    tokens, cot_in, local, ends, frequency, vectors, bias = take(7)
+    shards = take(4) if gather else take(0)
+    given = take(0) if gather else take(4)
+    base, msg, q_ref, kv_ref, kv8, kv16, stat = take(7)
+    out, grad_middle, grad_merged, small = take(4)
+    late_grads = take(3)
+    gathered = take(1) if gather else take(0)
     send, osend, orecv, acc, qc, kvc, tok_sem, ss, rs, os_, or_, ds, dr = take(13)
+    wo, wi, wt = take(3)
+    dense_scratch = take(9)
+    save_sem = take(1)[0]
+    weight = gathered[0] if gather else given[0]
+    cot = dense_scratch[0]
     spot = Spot(grp)
     joined = spot.greet()
-    loads = [
-        pltpu.make_async_copy(
-            tokens.at[:, order[b]], base.at[BLOCK * b : BLOCK * b + BLOCK], tok_sem.at[b]
-        )
-        for b in range(16)
-    ]
+    loads = []
+    for n, (source, target) in enumerate(((tokens, base), (cot_in, cot))):
+        for b in range(16):
+            at = BLOCK * b
+            loads.append(
+                pltpu.make_async_copy(source.at[:, order[b]], target.at[at : at + BLOCK], tok_sem.at[n, b])
+            )
     for copy in loads:
         copy.start()
     if gather:
         first = Gather(shards[:1], gathered[:1], take(9))
-        rest = Gather(shards[1:], gathered[1:], take(9))
+        rest = Gather([shards[1], shards[3]], [wo, wt], take(9))
+        wide_part = GatherWide(shards[2], wi, take(9))
         joined()
         first.start_layers()
         first.start_plane()
+        wide_part.start()
         rest.start_layers()
+    else:
+        loads_late = [
+            pltpu.make_async_copy(source, target, save_sem.at[n])
+            for n, (source, target) in enumerate(zip(given[1:], (wo, wi, wt)))
+        ]
+        for copy in loads_late:
+            copy.start()
+    place_lane = lax.broadcasted_iota(jnp.int32, (1, 512), 1)
+    b = place_lane // BLOCK
+    b = (b % 2) * 8 + (b // 2 % 2) * 4 + (b // 4 % 2) * 2 + b // 8
+    position = spot.linear * 512 + place_lane % BLOCK * 16 + b
+    begin = jnp.zeros((1, 512), jnp.int32)
+    lines = [jnp.where(local[0:1] == 1.0, 0.0, -BIG)]
+    before = 0
+    for n in range(slides):
+        after = before + ends[n]
+        inside = (position >= before) & (position < after)
+        lines.append(jnp.where(inside, 0.0, -BIG))
+        before = after
+    lines += [jnp.ones((1, 512), f32), jnp.zeros((14 - slides, 512), f32)]
+    flags_all = jnp.concatenate(lines, axis=0)
+    coordinates = local[...].T
+    gain, shift = vectors[0:1], vectors[1:2]
     lane = lax.broadcasted_iota(jnp.int32, (512, 384), 1)
-    angle = jnp.where(lane < 192, coordinates[:, 0:1], coordinates[:, 1:2]) * frequency[...]
+    angle = jnp.where(lane < 192, coordinates[:, 1:2], coordinates[:, 2:3]) * frequency[...]
     sine, cosine = jnp.sin(angle), jnp.cos(angle)
     table = jnp.concatenate(
         [
@@ -695,20 +925,23 @@
         ],
         axis=1,
     )
-    for copy in loads:
+    for copy in loads[:16]:
         copy.wait()
     base[...] = base[...] + table
     hat, _ = norm_parts(base[...])
-    normed = (hat * gain[...] + shift[...]).astype(bf16)
+    normed = (hat * gain + shift).astype(bf16)
     if gather:
+        first.advance(4)
+        wide_part.advance(1)
         first.finish()
+        wide_part.advance(2)
     else:
         joined()
     plane = [Exchange(spot, send.at[i], msg.at[i], ss.at[i], rs.at[i]) for i in range(2)]
     for quad in range(4):
         part = matmul(normed, pick(weight, quad)) + bias[quad]
         wide = swap_blocks(part.astype(bf16), quad).T
-        flags = flags_ref[...]
+        flags = flags_all
         flags = jnp.concatenate(
             [flags[:, BLOCK * (b ^ block_swap(quad)) :][:, :BLOCK] for b in range(16)], axis=1
         ).astype(bf16)
@@ -829,17 +1062,96 @@
             osend[i, j] = result.astype(bf16)
             results[i].send(j)
     if gather:
+        wide_part.advance(4)
         rest.advance(5)
     for i in range(2):
         for j in range(GROUP):
             results[i].wait(j)
-    merged[...] = join_quads(lambda h: orecv[h % 2, h // 2])
     if gather:
         rest.finish()
+        wide_part.advance(5)
+        rest.drain()
+        wide_part.drain()
         first.drain()
-        rest.drain()
+    else:
+        for copy in loads_late:
+            copy.wait()
+    for copy in loads[16:]:
+        copy.wait()
+    merged = dense_scratch[1]
+    merged[...] = join_quads(lambda h: orecv[h % 2, h // 2])
+    dense_part(
+        merged, base, cot, wo, wi, wt, vectors, out, grad_middle, grad_merged, small,
+        late_grads, save_sem, *dense_scratch[2:],
+    )
     for item in plane + deeps + results:
         item.drain()
+
+
+def dense_part(
+    merged, base, cot, wo, wi, wt, vectors, out, grad_middle, grad_merged, small,
+    late_grads, save_sem, middle, hat, low, low_t, cot_low, cot_t, grad_low,
+):
+    out_bias, gain, shift, last_bias = [vectors[n : n + 1] for n in range(2, 6)]
+    pairs = []
+    for g in range(0, 4, 2):
+        pair = [pick(wo, g + i) for i in range(2)]
+        pairs.append(jnp.concatenate(pair, axis=1))
+    full = jnp.concatenate(pairs, axis=1)
+    middle[...] = base[...] + matmul(merged[...], full) + out_bias
+    normal, inverse = norm_parts(middle[...])
+    hat[...] = normal
+    low[...] = (normal * gain + shift).astype(bf16)
+    low_t[...] = low[...].T
+    cot_low[...] = cot[...].astype(bf16)
+    cot_t[...] = cot_low[...].T
+    out[...] = middle[...] + last_bias
+    small[0:1] = column_sum(cot_low[...].astype(f32))
+    grad_middle[...] = jnp.zeros((512, 768), f32)
+
+    def chunk(g, _):
+        weight = pick(wi, g)
+        inner = matmul(low[...], weight) + vectors[pl.ds(6 + g, 1)]
+        phi = 0.5 * (1.0 + lax.erf(inner * 0.7071067811865476))
+        active = (inner * phi).astype(bf16)
+        slope = phi + inner * jnp.exp(-0.5 * inner * inner) * 0.3989422804014327
+        for x in range(2):
+            part = wt[g, 4 * x : 4 * x + 4].reshape(768, 384)
+            now = active[:, 384 * x : 384 * x + 384]
+            out[...] += matmul(now, part, NT)
+            back = matmul(cot_low[...], part)
+            wt[g, 4 * x : 4 * x + 4] = (
+                matmul(cot_t[...], now).astype(bf16).reshape(4, 192, 384)
+            )
+            grad_low[:, 384 * x : 384 * x + 384] = (
+                back * slope[:, 384 * x : 384 * x + 384]
+            ).astype(bf16)
+        small[pl.ds(4 + g, 1)] = column_sum(grad_low[...].astype(f32))
+        grad_middle[...] += matmul(grad_low[...], weight, NT)
+        put(wi, g, matmul(low_t[...], grad_low[...]).astype(bf16))
+        return 0
+
+    lax.fori_loop(0, 4, chunk, 0)
+    saves = [
+        pltpu.make_async_copy(source, target, save_sem.at[n])
+        for n, (source, target) in enumerate(zip((wo, wi, wt), late_grads))
+    ]
+    saves[1].start()
+    saves[2].start()
+    grad = grad_middle[...]
+    small[1:2] = column_sum(grad * hat[...])
+    small[2:3] = column_sum(grad)
+    grad = cot[...] + norm_backward(hat[...], inverse, gain, grad)
+    grad_middle[...] = grad
+    attended = grad.astype(bf16)
+    small[3:4] = column_sum(attended.astype(f32))
+    grad_merged[...] = matmul(attended, full, NT).astype(bf16)
+    grads = matmul(merged[...].T, attended).astype(bf16)
+    for g in range(4):
+        put(wo, g, grads[:, 192 * g : 192 * g + 192])
+    saves[0].start()
+    for copy in saves:
+        copy.wait()
 
 
 def attention_forward(grp, slides, gather, inputs, weights):
@@ -851,21 +1163,27 @@
         shape((2, 2, 512, LANES), bf16),
         shape((4, 2, 256, LANES), bf16),
         shape((2, GROUP, 56, 512), f32),
+        shape((512, 768), f32),
+        shape((512, 768), f32),
         shape((512, 768), bf16),
+        shape((8, 768), f32),
     ]
-    out_specs = [vmem()] * 8
-    in_specs = [anywhere()] + [vmem()] * 6
+    blocks = [(4, GROUP, 96, 192), (4, GROUP, 96, 768), (4, GROUP, 192, 384)]
+    out_specs = [vmem()] * len(out_shape) + [anywhere()] * 3
+    out_shape += [shape(dims, bf16) for dims in blocks]
+    in_specs = [anywhere()] * 2 + [vmem(), pl.BlockSpec(memory_space=pltpu.SMEM)] + [vmem()] * 3
     extra = []
     if gather:
         in_specs += [anywhere()] * 4
-        out_shape += [shape((4, GROUP) + w.shape, bf16) for w in weights]
-        out_specs += [vmem()] + [anywhere()] * 3
-        extra = gather_sems(1) + gather_sems(3)
+        out_shape += [shape((4, GROUP, 96, 576), bf16)]
+        out_specs += [vmem()]
+        extra = gather_sems(1) + gather_sems(2) + gather_wide_sems()
     else:
-        in_specs += [vmem()]
+        in_specs += [vmem()] + [anywhere()] * 3
+    rows = (512, 768)
     return pl.pallas_call(
         functools.partial(forward_kernel, grp, slides, gather),
-        name="attention_forward",
+        name="forward_and_feed",
         in_specs=in_specs,
         out_specs=out_specs,
         out_shape=out_shape,
@@ -876,132 +1194,151 @@
             pltpu.VMEM((64, q_all), f32),
             pltpu.VMEM((q_all - 4096, LANES), bf16),
             pltpu.VMEM((k_all - 4096, LANES), bf16),
-            sems(16),
+            sems(2, 16),
             sems(2, GROUP), sems(2, GROUP), sems(2, GROUP), sems(2, GROUP), sems(2, 4), sems(2, 4),
-        ] + extra,
+        ]
+        + [pltpu.VMEM(dims, bf16) for dims in blocks]
+        + [
+            pltpu.VMEM(rows, f32), pltpu.VMEM(rows, bf16), pltpu.VMEM(rows, f32),
+            pltpu.VMEM(rows, f32), pltpu.VMEM(rows, bf16), pltpu.VMEM((768, 512), bf16),
+            pltpu.VMEM(rows, bf16), pltpu.VMEM((768, 512), bf16), pltpu.VMEM(rows, bf16),
+            sems(3),
+        ]
+        + extra,
         compiler_params=params(1),
     )(*inputs, *weights)
-
-
-def dense_kernel(
-    merged, base, cot, wo, wi, wt, out_bias, gain, shift, in_bias, last_bias,
-    out, grad_middle, grad_merged, wo_grad, wi_grad, wt_grad, small, small_in,
-    full, middle, hat, low, low_t, cot_low, cot_t, grad_low,
-):
-    for g in range(0, 4, 2):
-        pair = [pick(wo, g + i) for i in range(2)]
-        full[:, 192 * g : 192 * g + 384] = jnp.concatenate(pair, axis=1)
-    middle[...] = base[...] + matmul(merged[...], full[...]) + out_bias[...]
-    normal, inverse = norm_parts(middle[...])
-    hat[...] = normal
-    low[...] = (normal * gain[...] + shift[...]).astype(bf16)
-    low_t[...] = low[...].T
-    cot_low[...] = cot[...].astype(bf16)
-    cot_t[...] = cot_low[...].T
-    out[...] = middle[...] + last_bias[...]
-    small[0:1] = column_sum(cot_low[...].astype(f32))
-    grad_middle[...] = jnp.zeros((512, 768), f32)
-
-    def chunk(g, _):
-        weight = pick(wi, g)
-        inner = matmul(low[...], weight) + in_bias[g]
-        phi = 0.5 * (1.0 + lax.erf(inner * 0.7071067811865476))
-        active = (inner * phi).astype(bf16)
-        slope = phi + inner * jnp.exp(-0.5 * inner * inner) * 0.3989422804014327
-        for x in range(2):
-            part = wt[g, 4 * x : 4 * x + 4].reshape(768, 384)
-            now = active[:, 384 * x : 384 * x + 384]
-            out[...] += matmul(now, part, NT)
-            wt_grad[g, 4 * x : 4 * x + 4] = (
-                matmul(cot_t[...], now).astype(bf16).reshape(4, 192, 384)
-            )
-            back = matmul(cot_low[...], part)
-            grad_low[:, 384 * x : 384 * x + 384] = (
-                back * slope[:, 384 * x : 384 * x + 384]
-            ).astype(bf16)
-        small_in[g] = column_sum(grad_low[...].astype(f32))
-        put(wi_grad, g, matmul(low_t[...], grad_low[...]).astype(bf16))
-        grad_middle[...] += matmul(grad_low[...], weight, NT)
-        return 0
-
-    lax.fori_loop(0, 4, chunk, 0)
-    grad = grad_middle[...]
-    small[1:2] = column_sum(grad * hat[...])
-    small[2:3] = column_sum(grad)
-    grad = cot[...] + norm_backward(hat[...], inverse, gain[...], grad)
-    grad_middle[...] = grad
-    attended = grad.astype(bf16)
-    small[3:4] = column_sum(attended.astype(f32))
-    small[4:8] = jnp.zeros((4, 768), f32)
-    grads = matmul(merged[...].T, attended).astype(bf16)
-    for g in range(4):
-        put(wo_grad, g, grads[:, 192 * g : 192 * g + 192])
-    grad_merged[...] = matmul(attended, full[...], NT).astype(bf16)
-
-
-def dense(merged, base, cot, wo, wi, wt, out_bias, gain, shift, in_bias, last_bias):
-    rows = (512, 768)
-    return pl.pallas_call(
-        dense_kernel,
-        name="dense",
-        in_specs=[vmem()] * 11,
-        out_specs=[vmem()] * 8,
-        out_shape=[
-            shape(rows, f32), shape(rows, f32), shape(rows, bf16),
-            shape((4, GROUP, 96, 192), bf16), shape((4, GROUP, 96, 768), bf16),
-            shape((4, GROUP, 192, 384), bf16), shape((8, 768), f32), shape((4, 1, 768), f32),
-        ],
-        scratch_shapes=[
-            pltpu.VMEM((768, 768), bf16), pltpu.VMEM(rows, f32), pltpu.VMEM(rows, f32),
-            pltpu.VMEM(rows, bf16), pltpu.VMEM((768, 512), bf16), pltpu.VMEM(rows, bf16),
-            pltpu.VMEM((768, 512), bf16), pltpu.VMEM(rows, bf16),
-        ],
-        compiler_params=params(),
-    )(merged, base, cot, wo, wi, wt, out_bias, gain, shift, in_bias, last_bias)
-
-
-def final_kernel(
-    base, grad_middle, d0, d1, d2, d3, weight, gain, shift, token_grad, grads_out, small,
-):
-    hat, inverse = norm_parts(base[...])
-    low_t = (hat * gain[...] + shift[...]).astype(bf16).T
-    grad = jnp.zeros((512, 768), f32)
-    small[...] = jnp.zeros((8, 768), f32)
-    for quad, part in enumerate((d0, d1, d2, d3)):
-        now = part[...]
-        put(grads_out, quad, matmul(low_t, now).astype(bf16))
-        grad = grad + matmul(now, pick(weight, quad), NT)
-    small[0:1] = column_sum(grad * hat)
-    small[1:2] = column_sum(grad)
-    token_grad[...] = grad_middle[...] + norm_backward(hat, inverse, gain[...], grad)
-
-
-def final(base, grad_middle, quads, weight, gain, shift):
-    rows = (512, 768)
-    return pl.pallas_call(
-        final_kernel,
-        name="input_gradients",
-        in_specs=[vmem()] * 9,
-        out_specs=[vmem()] * 3,
-        out_shape=[shape(rows, f32), shape((4, GROUP, 96, 576), bf16), shape((8, 768), f32)],
-        compiler_params=params(),
-    )(base, grad_middle, *quads, weight, gain, shift)
 
 
 def backward_kernel(grp, reduce, *refs):
     refs = list(refs)
     take = lambda n: [refs.pop(0) for _ in range(n)]
-    gm, q_ref, kv_ref, kv8, kv16, msg, stat = take(7)
-    parts = take(3) if reduce else None
-    outs, sums_ref = take(4), take(1)[0]
-    reduced = take(3) if reduce else None
-    (gsend, grecv, rsend, rrecv, got8, got16, send8, send16, qc, kvc, dor, kt, ld, dkv, dqt,
-     gs, gr, ss, rs, ds, dr) = take(21)
+    gm, vectors, small = take(3)
+    saved = take(6)
+    base_in, middle_in, weight_in = take(3)
+    parts = take(3) if reduce else take(0)
+    token_grad, joint_out, pack = take(3)
+    reduced = take(3) if reduce else take(0)
+    (gsend, grecv, rsend, rrecv, got8, got16, send8, send16, rows_ref,
+     gs, gr, ss, rs, ds, dr, load_sem) = take(16)
+    local = take(13)
+    (grads,) = take(1)
     spot = Spot(grp)
     joined = spot.greet()
     shares = [Exchange(spot, gsend.at[i], grecv.at[i], gs.at[i], gr.at[i]) for i in range(2)]
     backs = [Exchange(spot, rsend.at[i], rrecv.at[i], ss.at[i], rs.at[i]) for i in range(2)]
-    sums = Reduce(parts, reduced, refs) if reduce else None
+    deeps = []
+    if reduce:
+        two = [parts[0], parts[2]], [reduced[0], reduced[2]]
+        dims = [part.shape[2:] for part in two[0]]
+        sums = Reduce(*two, take(len(reduce_scratch(dims))))
+        wide_sum = ReduceWide(parts[1], reduced[1], take(14))
+        last_scratch = take(len(reduce_scratch([(96, 576)])) - 1)
+        total_sum = take(5)
+    else:
+        sums = wide_sum = None
+
+    attend_backward(
+        spot, joined, gm, saved, shares, backs, deeps, sums, wide_sum, gsend, grecv, rsend,
+        got8, got16, send8, send16, ds, dr, load_sem, *local,
+    )
+    rows_f32 = local[11]
+    late_loads = [pltpu.make_async_copy(weight_in, grads, load_sem.at[0])]
+    for n, source in enumerate((base_in, middle_in)):
+        for chunk in range(6):
+            at = 3072 * n + 512 * chunk
+            late_loads.append(
+                pltpu.make_async_copy(
+                    source.at[:, LANES * chunk : LANES * chunk + LANES],
+                    rows_f32.at[at : at + 512],
+                    load_sem.at[1 + 6 * n + chunk],
+                )
+            )
+    for copy in late_loads:
+        copy.start()
+
+    def loaded(n):
+        at = 3072 * n
+        return jnp.concatenate(
+            [rows_f32[at + 512 * chunk : at + 512 * chunk + 512] for chunk in range(6)], axis=1
+        )
+
+    if reduce:
+        sums.advance(5)
+        wide_sum.advance(5)
+    for copy in late_loads:
+        copy.wait()
+    gain, shift = vectors[0:1], vectors[1:2]
+    hat, inverse = norm_parts(loaded(0))
+    low_t = (hat * gain + shift).astype(bf16).T
+    for i in range(2):
+        for j in range(GROUP):
+            backs[i].wait(j)
+    lines = [[], []]
+    grad = jnp.zeros((512, 768), f32)
+    for quad in range(4):
+
+        def read(head):
+            block = rrecv[head % 2, head // 2]
+            return jnp.concatenate([block[2 * HD :], block[: 2 * HD]], axis=0)
+
+        now = join_quad(quad, read)
+        grad = grad + matmul(now, pick(grads, quad), NT)
+        put(grads, quad, matmul(low_t, now).astype(bf16))
+        total = column_sum(now.astype(f32))
+        for inner in range(4):
+            lines[0].append(total[:, 144 * inner : 144 * inner + HD])
+            lines[1].append(total[:, 144 * inner + 96 : 144 * inner + 144])
+    if reduce:
+        joint = Reduce([grads], [joint_out], [None] + list(last_scratch))
+        joint.start()
+    rows_ref[0:1] = column_sum(grad * hat)
+    rows_ref[1:2] = column_sum(grad)
+    rows_ref[2:3] = jnp.concatenate(lines[0], axis=1)
+    rows_ref[3:4] = jnp.concatenate(lines[1], axis=1)
+    rows_ref[4:5] = small[3:4]
+    rows_ref[5:6] = small[1:2]
+    rows_ref[6:7] = small[2:3]
+    rows_ref[7:8] = small[0:1]
+    rows_ref[8:12] = small[4:8]
+    rows_ref[12:16] = jnp.zeros((4, 768), f32)
+    token_grad[...] = loaded(1) + norm_backward(hat, inverse, gain, grad)
+    if reduce:
+        rest = Total(rows_ref, pack, total_sum)
+        rest.start()
+        joint.advance(1)
+        rest.middle()
+        joint.advance(3)
+        rest.late()
+        joint.advance(5)
+        sums.advance(6)
+        wide_sum.advance(6)
+        joint.advance(6)
+        rest.finish()
+        joint.drain()
+    else:
+        pack[...] = rows_ref[...]
+        save = pltpu.make_async_copy(grads, joint_out, load_sem.at[3])
+        save.start()
+        save.wait()
+    if reduce:
+        sums.drain()
+        wide_sum.drain()
+    for item in shares + backs + deeps:
+        item.drain()
+
+
+def attend_backward(
+    spot, joined, gm, saved, shares, backs, deeps, sums, wide_sum, gsend, grecv, rsend, got8, got16,
+    send8, send16, ds, dr, load_sem, q_ref, kv_ref, kv8, kv16, msg, stat,
+    qc, kvc, dor, kt, ld, dkv, dqt,
+):
+    reduce = sums is not None
+    loads = [
+        pltpu.make_async_copy(source, target, load_sem.at[n])
+        for n, (source, target) in enumerate(zip(saved, (q_ref, kv_ref, kv8, kv16, msg, stat)))
+    ]
+    for copy in loads:
+        copy.start()
     for quad in range(4):
         wide = swap_blocks(gm[:, 192 * quad : 192 * quad + 192], quad).T
         for inner in (0, 2, 1, 3):
@@ -1015,10 +1352,10 @@
     for j in range(GROUP):
         shares[1].send(j)
     if reduce:
+        wide_sum.start()
         sums.start()
-    row = lax.broadcasted_iota(jnp.int32, (96, 1), 0)
-    factor = jnp.where(row < HD, scale, 1.0)
-    deeps = []
+    for copy in loads:
+        copy.wait()
     for i in range(2):
         q, kv = q_ref.at[i], kv_ref.at[i]
         for n in range(2):
@@ -1087,6 +1424,7 @@
         deep.start()
         deeps.append(deep)
         if reduce:
+            wide_sum.advance(2 + i)
             sums.advance(1 + 2 * i)
 
         def early(u, _):
@@ -1097,6 +1435,7 @@
         lax.fori_loop(0, 4, early, 0)
         if reduce:
             sums.advance(2 + 2 * i)
+            wide_sum.advance(2 + 2 * i)
 
         def late(u, _):
             at = pl.multiple_of(u * 1024, 1024)
@@ -1139,39 +1478,29 @@
             rsend[i, j, HD : 2 * HD] = (wide[HD : 2 * HD] + prob * grad).astype(bf16)
             rsend[i, j, 2 * HD :] = ((dq + slope * key) * scale).astype(bf16)
             backs[i].send(j)
-    if reduce:
-        sums.advance(5)
-    for i in range(2):
-        for j in range(GROUP):
-            backs[i].wait(j)
-    for quad, out in enumerate(outs):
-
-        def read(head):
-            block = rrecv[head % 2, head // 2]
-            return jnp.concatenate([block[2 * HD :], block[: 2 * HD]], axis=0)
-
-        result = join_quad(quad, read)
-        out[...] = result
-        sums_ref[quad] = column_sum(result.astype(f32))
-    if reduce:
-        sums.advance(6)
-        sums.drain()
-    for item in shares + backs + deeps:
-        item.drain()
 
 
 def attention_backward(grp, reduce, inputs, parts):
-    out_shape = [shape((512, 576), bf16)] * 4 + [shape((4, 1, 576), f32)]
+    out_shape = [
+        shape((512, 768), f32),
+        shape((96, 576), f32) if reduce else shape((4, GROUP, 96, 576), bf16),
+        shape((16, 768), f32),
+    ]
+    out_specs = [vmem(), vmem() if reduce else anywhere(), vmem()]
     extra = []
     if reduce:
         dims = [part.shape[2:] for part in parts]
         out_shape += [shape(d, f32) for d in dims]
-        extra = reduce_scratch(dims)
+        out_specs += [vmem()] * 3
+        extra = (
+            reduce_scratch([dims[0], dims[2]]) + reduce_wide_scratch(dims[1])
+            + reduce_scratch([(96, 576)])[1:] + total_scratch((16, 768))
+        )
     return pl.pallas_call(
         functools.partial(backward_kernel, grp, reduce),
         name="attention_backward",
-        in_specs=[vmem()] * 7 + [anywhere()] * len(parts),
-        out_specs=[vmem()] * len(out_shape),
+        in_specs=[vmem()] * 3 + [anywhere()] * (9 + len(parts)),
+        out_specs=out_specs,
         out_shape=out_shape,
         scratch_shapes=[
             pltpu.VMEM((2, GROUP, HD, 512), bf16),
@@ -1182,17 +1511,65 @@
             pltpu.VMEM((4, 2, 256, LANES), bf16),
             pltpu.VMEM((2, 2, 512, LANES), bf16),
             pltpu.VMEM((4, 2, 256, LANES), bf16),
-            pltpu.VMEM((q_all - 4096, LANES), bf16),
-            pltpu.VMEM((k_all - 4096, LANES), bf16),
-            pltpu.VMEM((q_all, LANES), bf16),
-            pltpu.VMEM((9, HD, 1024), bf16),
-            pltpu.VMEM((8, q_all), f32),
-            pltpu.VMEM((k_all, LANES), f32),
+            pltpu.VMEM((16, 768), f32),
+            sems(2, GROUP), sems(2, GROUP), sems(2, GROUP), sems(2, GROUP), sems(2, 4), sems(2, 4),
+            sems(13),
+            pltpu.VMEM((2, 4096, LANES), bf16), pltpu.VMEM((2, 4096, LANES), bf16),
+            pltpu.VMEM((2, 2, 512, LANES), bf16), pltpu.VMEM((4, 2, 256, LANES), bf16),
+            pltpu.VMEM((2, GROUP, MSG, 512), bf16), pltpu.VMEM((2, GROUP, 56, 512), f32),
+            pltpu.VMEM((q_all - 4096, LANES), bf16), pltpu.VMEM((k_all - 4096, LANES), bf16),
+            pltpu.VMEM((q_all, LANES), bf16), pltpu.VMEM((9, HD, 1024), bf16),
+            pltpu.VMEM((8, q_all), f32), pltpu.VMEM((k_all, LANES), f32),
             pltpu.VMEM((HD, q_all), f32),
-            sems(2, GROUP), sems(2, GROUP), sems(2, GROUP), sems(2, GROUP), sems(2, 4), sems(2, 4),
+            pltpu.VMEM((4, GROUP, 96, 576), bf16),
         ] + extra,
         compiler_params=params(2),
     )(*inputs, *parts)
+
+
+def finish_kernel(out_in, token_in, joint, b_in, c_in, d_in, pack, *refs):
+    out, token, query, key, value, b_out, c_out, d_out = refs[:8]
+    vectors, done = refs[8:17], refs[17]
+    copies = []
+    for n, (source, target) in enumerate(((out_in, out), (token_in, token))):
+        for b in range(16):
+            at = BLOCK * b
+            copies.append(
+                pltpu.make_async_copy(source.at[at : at + BLOCK], target.at[:, order[b]], done.at[n, b])
+            )
+    for copy in copies:
+        copy.start()
+    for n, target in enumerate((query, key, value)):
+        target[...] = jnp.concatenate(
+            [joint[:, 144 * i + HD * n : 144 * i + HD * n + HD] for i in range(4)], axis=1
+        )
+    b_out[...] = b_in[...]
+    c_out[...] = c_in[...]
+    d_out[...] = d_in[...].T
+    for n in (0, 1, 2, 3, 4, 5, 6):
+        vectors[n][...] = pack[n]
+    vectors[7][...] = jnp.concatenate([pack[8 + n] for n in range(4)], axis=0)
+    vectors[8][...] = pack[7]
+    for copy in copies:
+        copy.wait()
+
+
+def finish(out, token_grad, joint, b_sum, c_sum, d_sum, pack):
+    shard, hidden = b_sum.shape[0], d_sum.shape[1]
+    rows = (BLOCK, 16, 768)
+    sizes = [768] * 7 + [3072, 768]
+    return pl.pallas_call(
+        finish_kernel,
+        name="finish",
+        in_specs=[anywhere()] * 2 + [vmem()] * 5,
+        out_specs=[anywhere()] * 2 + [vmem()] * 15,
+        out_shape=[shape(rows, f32)] * 2
+        + [shape((shard, 192), f32)] * 4
+        + [shape((shard, 768), f32), shape((hidden, 192), f32)]
+        + [shape((size,), f32) for size in sizes],
+        scratch_shapes=[sems(2, 16)],
+        compiler_params=params(),
+    )(out, token_grad, joint, b_sum, c_sum, d_sum, pack)
 
 
 def all_weights(parts, seq, grp):
@@ -1225,16 +1602,6 @@
         whole = lax.psum_scatter(whole, "seq", scatter_dimension=0)
         sums.append(lax.psum_scatter(whole, "grp", scatter_dimension=0))
     return sums + [lax.psum(small, ("seq", "grp"))]
-
-
-def in_order(rows):
-    split = rows.reshape((BLOCK, 16) + rows.shape[1:])
-    return jnp.stack([split[:, b] for b in order]).reshape(rows.shape)
-
-
-def back_order(rows):
-    split = rows.reshape((16, BLOCK) + rows.shape[1:])
-    return jnp.stack([split[b] for b in order], axis=1).reshape(rows.shape)
 
 
 def body(
@@ -1264,7 +1631,6 @@
     seq = lax.axis_size("seq")
     near = (seq, grp) == (8, 4)
     slides = lengths.shape[0]
-    linear = lax.axis_index("seq") * grp + lax.axis_index("grp")
     shard = query_weight.shape[0]
     heads = [w.reshape(shard, 4, 1, HD) for w in (query_weight, key_weight, value_weight)]
     parts = [
@@ -1276,70 +1642,41 @@
     joint_bias = jnp.stack(
         [b.reshape(4, 4, HD) for b in (query_bias, jnp.zeros_like(query_bias), value_bias)], axis=2
     ).reshape(4, 1, 576)
-    cotangent = in_order(cotangent)
-    places = in_order(linear * rows + jnp.arange(rows, dtype=jnp.int32))
-    keep = in_order(valid)
-    slide = jnp.sum((places[:, None] >= jnp.cumsum(lengths)).astype(jnp.int32), axis=-1)
-    apart = slide[None, :] != jnp.arange(slides, dtype=jnp.int32)[:, None]
-    flags = jnp.concatenate(
-        [
-            jnp.where(keep == 1, 0.0, -BIG)[None, :],
-            jnp.where(apart, -BIG, 0.0),
-            jnp.ones((1, rows), f32),
-            jnp.zeros((14 - slides, rows), f32),
-        ],
-        axis=0,
-    )
+    local = jnp.concatenate([valid[:, None], coordinates], axis=1).astype(f32)
+    local = local.reshape(BLOCK, 2, 2, 2, 2, 3).transpose(5, 4, 3, 2, 1, 0).reshape(3, rows)
+    local = jnp.concatenate([local, jnp.zeros((5, rows), f32)], axis=0)
     frequency = jnp.exp(jnp.arange(192, dtype=jnp.float32) * (-math.log(10000.0) / 192))
-    row = lambda v: v.reshape(1, -1)
+    vectors = [
+        first_gain, first_shift, output_bias, second_gain, second_shift, outer_bias, inner_bias,
+        jnp.zeros((6 * width,), f32),
+    ]
+    vectors = jnp.concatenate(vectors).reshape(16, width)
     inputs = [
-        tokens.reshape(BLOCK, 16, width), in_order(coordinates).astype(f32),
-        row(jnp.concatenate([frequency, frequency])), row(first_gain), row(first_shift), flags,
-        joint_bias,
+        tokens.reshape(BLOCK, 16, width), cotangent.reshape(BLOCK, 16, width), local, lengths,
+        jnp.concatenate([frequency, frequency]).reshape(1, 384), vectors, joint_bias,
     ]
+    weights = parts if near else all_weights(parts, seq, grp)
+    results = attention_forward(grp, slides, near, inputs, weights)
+    base, msg, q_rows, kv_rows, kv8, kv16, stat, out, grad_middle, grad_merged, small = results[:11]
+    late = results[11:14]
+    joint_weight = results[14] if near else weights[0]
+    saved = [
+        grad_merged, vectors, small, q_rows, kv_rows, kv8, kv16, msg, stat, base, grad_middle,
+        joint_weight,
+    ]
+    results = attention_backward(grp, near, saved, late if near else [])
+    token_grad, joint_sum, pack = results[:3]
     if near:
-        results = attention_forward(grp, slides, True, inputs, parts)
-        joint_weight, wo, wi, wt = results[8:]
+        sums = results[3:]
     else:
-        joint_weight, wo, wi, wt = all_weights(parts, seq, grp)
-        results = attention_forward(grp, slides, False, inputs, [joint_weight])
-    base, msg, q_rows, kv_rows, kv8, kv16, stat, merged_low = results[:8]
-    output, grad_middle, grad_merged, wo_grad, wi_grad, wt_grad, small, small_in = dense(
-        merged_low, base, cotangent, wo, wi, wt, row(output_bias), row(second_gain),
-        row(second_shift), inner_bias.reshape(4, 1, 768), row(outer_bias),
-    )
-    saved = [grad_merged, q_rows, kv_rows, kv8, kv16, msg, stat]
-    late = [wo_grad, wi_grad, wt_grad]
-    results = attention_backward(grp, near, saved, late if near else [])
-    quads, sums = results[:4], results[4]
-    token_grad, joint_grad, first_small = final(
-        base, grad_middle, quads, joint_weight, row(first_gain), row(first_shift)
-    )
-    sums = sums.reshape(4, 4, 3, HD)
-    vectors = [
-        first_small[0], first_small[1], sums[:, :, 0].reshape(-1), sums[:, :, 2].reshape(-1),
-        small[3], small[1], small[2], small_in.reshape(-1), small[0],
-    ]
-    sizes = [v.shape[0] for v in vectors]
-    pack = jnp.concatenate(vectors).reshape(-1, LANES)
-    if near:
-        sum_output, sum_inner, sum_outer = results[5:]
-        joint_sum, pack = reduce_gradients([joint_grad], pack, 3)
-    else:
-        joint_sum, sum_output, sum_inner, sum_outer, pack = sum_gradients(
-            [joint_grad] + late, pack, seq, grp
-        )
-    joint_sum = joint_sum.reshape(shard, 4, 3, HD)
-    sum_query, sum_key, sum_value = [joint_sum[:, :, i].reshape(shard, 192) for i in range(3)]
-    sum_outer = sum_outer.T
-    small = []
-    pack = pack.reshape(-1)
-    for size in sizes:
-        small.append(pack[:size])
-        pack = pack[size:]
+        joint_sum, *sums, pack = sum_gradients([joint_sum] + list(late), pack, seq, grp)
+    results = finish(out, token_grad, joint_sum, *sums, pack)
+    output, token_grad = [item.reshape(rows, width) for item in results[:2]]
+    sum_query, sum_key, sum_value, sum_output, sum_inner, sum_outer = results[2:8]
+    small = results[8:]
     return (
-        back_order(output),
-        back_order(token_grad),
+        output,
+        token_grad,
         small[0],
         small[1],
         sum_query,

time: 362 us -> 423 us (1.17)
  Pallas kernels: 325 us -> 398 us
  local copies, waits for them, and re-layouts: 26.1 us -> 16.1 us
    pallas_call x1, Pallas kernels: 115 us -> 150 us  [attention_backward(): pl.pallas_call(functools.partial(backward_kernel, grp, reduce), name='att...]
    pallas_call x1, Pallas kernels: 127 us -> 150 us  [attention_forward(): pl.pallas_call(functools.partial(forward_kernel, grp, slides, gather), na...]
    pallas_call x3 -> x1, Pallas kernels: 82.3 us -> 98.9 us  [finish(): pl.pallas_call(finish_kernel, name='finish', in_specs=[anywhere()] * 2 +...]
    reshape x10 -> x3, local copies, waits for them, and re-layouts: 6.51 us -> 1.3 us  [the longest x1 0.63 us: body(): vectors = jnp.concatenate(vectors).reshape(16, width)]
    slice x9 -> x0, local copies, waits for them, and re-layouts: 4.87 us -> none  [the longest x3 2.7 us: in_order(): return jnp.stack([split[:, b] for b in order]).reshape(rows.shape)]
    another operation x11 -> x0, local copies, waits for them, and re-layouts: 4.47 us -> none  [the longest x4 4.13 us: back_order(): return jnp.stack([split[b] for b in order], axis=1).reshape(rows.shape)]
    unnamed x106 -> x13, local copies, waits for them, and re-layouts: 6.13 us -> 9.46 us
where the time goes in v4:
time: 423 us; the launch traced here: 416 us
  Pallas kernels  398 us (94%)
  local copies, waits for them, and re-layouts  16.1 us (4%)
    pallas_call x1, Pallas kernels, attention_forward(): pl.pallas_call(functools.partial(forward_kernel, grp, slides, gather), na...  150 us
    pallas_call x1, Pallas kernels, attention_backward(): pl.pallas_call(functools.partial(backward_kernel, grp, reduce), name='att...  150 us
    pallas_call x1, Pallas kernels, finish(): pl.pallas_call(finish_kernel, name='finish', in_specs=[anywhere()] * 2 +...  98.9 us
    unnamed x13, local copies, waits for them, and re-layouts  9.46 us

profile of v4, /device:TPU:0, one launch (start us, length us, event | category | flops | bytes accessed | tf_op | source)
XLA Modules:
  0.0 416.0 jit_solution(176323571726079441)
XLA Ops:
  0.7 0.0 copy-start
  0.7 0.1 pad.5.clone
  0.7 0.1 pad_maximum_fusion.2
  0.8 0.6 reshape.77.refs_4_
  1.4 0.8 stack_reshape.9
  2.2 0.8 stack_reshape.11
  2.9 0.1 pad_maximum_fusion.1
  3.0 0.7 reshape.86.refs_6_
  3.7 0.9 copy.53
  4.6 0.9 copy.54
  5.5 0.9 copy.55
  6.5 0.8 copy.58.refs_7_
  7.3 0.7 constant_dynamic-update-slice_fusion.6
  8.0 0.7 constant_dynamic-update-slice_fusion.5
  8.7 0.7 constant_dynamic-update-slice_fusion.4
  9.4 0.7 constant_dynamic-update-slice_fusion.3
  10.1 0.7 constant_dynamic-update-slice_fusion.2
  10.8 0.7 constant_dynamic-update-slice_fusion.1
  11.5 0.7 constant_dynamic-update-slice_fusion
  12.2 0.6 reshape.78.refs_5_.refs_1_
  12.8 0.9 concatenate.20
  13.7 0.1 copy.50
  13.9 0.0 copy-done
  13.9 0.4 concatenate.21
  14.3 0.2 copy.51
  14.5 0.1 reshape.76
  14.6 0.6 concatenate.23.refs_2_
  15.2 150.0 %forward_and_feed.1 = (f32[512,768]{1,0:T(8,128)}, bf16[2,8,160,512]{3,2,1,0:T(8,128)(2,1)}, bf16[2,4096,128]{2,1,0:T(8,128)(2,1)}, bf16[2,4096,128]{2,1,0:T(8,1...) custom-call(f32[32,16,768]{2,1,0:T(8,128)} %bitcast.14, ...), custom_call_target="tpu_custom_call" | custom-call | tf_op jit(solution)/shard_map/forward_and_feed/pallas_call | solution.py:1184
  165.2 149.6 %attention_backward.1 = (f32[512,768]{1,0:T(8,128)}, f32[96,576]{1,0:T(8,128)}, f32[16,768]{1,0:T(8,128)}, f32[96,192]{1,0:T(8,128)}, f32[96,768]{1,0:T(8,128)}, /*index=5*/f32[192,384]{1,0:T(8,128)}) custom-call(bf16[512,768]{1,0:T(8,128)(2,1)} %get-tuple-element.56.refs_0_, f32[16,768]{1,0:T(8,128)} %reshape.78.refs_5_.refs_1_, ...), custom_call_target="tpu_custom_call" | custom-call | tf_op jit(solution)/shard_map/attention_backward/pallas_call | solution.py:1499
  314.8 98.9 %finish.1 = (f32[32,16,768]{2,1,0:T(8,128)}, f32[32,16,768]{2,1,0:T(8,128)}, f32[96,192]{1,0:T(8,128)}, f32[96,192]{1,0:T(8,128)}, f32[96,192]{1,0:T(8,128)}, /*...) custom-call(f32[512,768]{1,0:T(8,128)} %get-tuple-element.55.out_in,, ...), custom_call_target="tpu_custom_call" | custom-call | tf_op jit(solution)/shard_map/finish/pallas_call | solution.py:1561
  413.7 1.9 copy.59
  (7 shorter events, 0.1 us)
Async XLA Ops:
  0.7 13.2 %copy-start = (s32[512,2]{0,1:T(2,128)S(1)}, s32[512,2]{0,1:T(2,128)}, u32[]{:S(2)}) copy-start(s32[512,2]{0,1:T(2,128)} %param.21) | copy-start | bytes 12292
